TPU v7x, 32 devices: a whole 2x2x4 slice. The times are simulated.
32 devices in a mesh: region: 4 (over y, x), sub: 8 (over z, core).
Axes of the slice: x: 2, y: 2, z: 4, core: 2. Of those that a mesh axis runs over, the one named last changes fastest.
Arguments:
- scalars: float32 [4096, 128], P(('region', 'sub')), may hold values from -6 to 6
- vectors: float32 [3, 4096, 128], P(None, ('region', 'sub')), may hold values from -6 to 6
- positions: float32 [3, 4096], P(None, ('region', 'sub')), may hold values from 0 to 8
- pair_blocks: int32 [2, 48], replicated, may hold values from 0 to 31, as said below
- pair_mask: int32 [48, 547], replicated, may hold values from 0 to 1073741823
- wavevectors: float32 [3, 512], replicated, may hold values from -2 to 2
- message_in: float32 [2, 128, 128], replicated, may hold values from -0.5 to 0.5
- message_out: float32 [2, 128, 384], replicated, may hold values from -0.5 to 0.5
- filter_weight: float32 [2, 20, 384], replicated, may hold values from -0.3125 to 0.3125
- ewald_weight: float32 [2, 128, 128], replicated, may hold values from -0.5 to 0.5
- ewald_filter: float32 [2, 512, 128], replicated, may hold values from -6 to 6
- mixing_left: float32 [2, 128, 128], replicated, may hold values from -0.5 to 0.5
- mixing_right: float32 [2, 128, 128], replicated, may hold values from -0.5 to 0.5
- update_in: float32 [2, 256, 128], replicated, may hold values from -0.375 to 0.375
- update_out: float32 [2, 128, 384], replicated, may hold values from -0.5 to 0.5
Outputs:
- scalars_out: float32 [4096, 128], P(('region', 'sub'))
- vectors_out: float32 [3, 4096, 128], P(None, ('region', 'sub'))
Inputs may be any that keep to these rules, and one draw needn't show every extreme that they name: `pair_blocks`: pairs are listed region by region, 12 pairs for each of the 4 regions of 8 consecutive blocks. Both blocks of a pair lie in the same region, the first below the second; no pair is listed twice, and within a region the first blocks never fall along the list.
All inputs are finite; a program needn't handle non-finite values.
Results may differ from a plain program's by a relative error of at most 0.0003.
Values sent between devices are 32-bit elements; how exact they have to be, the bound alone decides.
No kernel may reach another device: no remote copies, remote signals or barrier semaphores. Data moves between devices by JAX's collectives and lax.ppermute only.
A program may use at most 128 MiB of HBM per device.

v0:
```python
import math

import jax
import jax.numpy as jnp
from jax import lax
from jax.sharding import PartitionSpec as P

NRBF = 20
BS = 128
KW = 512
LAYERS = 2


HIGHEST = lax.Precision.HIGHEST
CUTOFF = 8.0


def unpack_mask(packed):
    shifts = jnp.arange(30, dtype=jnp.int32)
    unpacked = jnp.right_shift(packed[:, None], shifts[None, :]) & 1
    return unpacked.reshape(-1)[: BS * BS].reshape(BS, BS).astype(jnp.float32)


def radial_basis(distance, tile_mask):
    spacing = CUTOFF / (NRBF - 1)
    centers = jnp.arange(NRBF, dtype=jnp.float32) * spacing
    scaled = (distance[None] - centers[:, None, None]) / spacing
    return jnp.exp(-0.5 * scaled * scaled) * tile_mask[None]


def geometry(pos_first, pos_second, packed):
    offset = pos_second[:, None, :] - pos_first[:, :, None]
    distance = jnp.sqrt(jnp.sum(offset * offset, axis=0) + 1.0)
    direction = offset / distance[None]
    return (radial_basis(distance, unpack_mask(packed)), direction)


def side_terms(radial, direction, source, filters):
    channels = source.shape[1] // 5
    rows = radial.shape[1]
    product = jnp.dot(radial.reshape(-1, radial.shape[2]), source, precision=HIGHEST)
    product = product.reshape(NRBF, rows, 5 * channels)
    steered = (direction[:, None] * radial[None]).reshape(-1, radial.shape[2])
    turned = jnp.dot(steered, source[:, 4 * channels :], precision=HIGHEST).reshape(
        3, NRBF, rows, channels
    )
    w_scalar = filters[:, :channels]
    w_vector = filters[:, channels : 2 * channels]
    w_radial = filters[:, 2 * channels :]
    delta_scalar = jnp.einsum("kic,kc->ic", product[..., :channels], w_scalar, precision=HIGHEST)
    parts = []
    for component in range(3):
        lower = (1 + component) * channels
        along = jnp.einsum(
            "kic,kc->ic", product[..., lower : lower + channels], w_vector, precision=HIGHEST
        )
        along = along + jnp.einsum("kic,kc->ic", turned[component], w_radial, precision=HIGHEST)
        parts.append(along)
    return (delta_scalar, jnp.stack(parts))


def pair_terms(radial, direction, source_first, source_second, filters):
    to_first = side_terms(radial, direction, source_second, filters)
    to_second = side_terms(
        radial.transpose(0, 2, 1), -direction.transpose(0, 2, 1), source_first, filters
    )
    return (to_first, to_second)


def message_sources(scalars_now, vectors_now, first_weight, second_weight):
    channels = scalars_now.shape[1]
    hidden = jax.nn.silu(jnp.dot(scalars_now, first_weight, precision=HIGHEST))
    filt_in = jnp.dot(hidden, second_weight, precision=HIGHEST)
    phi_vector = filt_in[:, channels : 2 * channels]
    return jnp.concatenate(
        [
            filt_in[:, :channels],
            phi_vector * vectors_now[0],
            phi_vector * vectors_now[1],
            phi_vector * vectors_now[2],
            filt_in[:, 2 * channels :],
        ],
        axis=1,
    )


def update_block(mid_scalars, mid_vectors, left_weight, right_weight, gate_in, gate_out):
    channels = mid_scalars.shape[1]
    flat = mid_vectors.reshape(-1, channels)
    left = jnp.dot(flat, left_weight, precision=HIGHEST).reshape(mid_vectors.shape)
    right = jnp.dot(flat, right_weight, precision=HIGHEST).reshape(mid_vectors.shape)
    vec_norm = jnp.sqrt(jnp.sum(right * right, axis=0) + 1.0)
    hidden = jax.nn.silu(
        jnp.dot(jnp.concatenate([mid_scalars, vec_norm], axis=1), gate_in, precision=HIGHEST)
    )
    gates = jnp.dot(hidden, gate_out, precision=HIGHEST)
    new_vectors = mid_vectors + gates[None, :, :channels] * left
    new_scalars = (
        mid_scalars
        + gates[:, channels : 2 * channels] * jnp.sum(left * right, axis=0)
        + gates[:, 2 * channels :]
    )
    return (new_scalars, new_vectors)


def add_rows(target, delta, row_at, axis_id):
    current = lax.dynamic_slice_in_dim(target, row_at, BS, axis_id)
    return lax.dynamic_update_slice_in_dim(target, current + delta, row_at, axis_id)


def body(
    scalars,
    vectors,
    positions,
    pair_blocks,
    pair_mask,
    wavevectors,
    message_in,
    message_out,
    filter_weight,
    ewald_weight,
    ewald_filter,
    mixing_left,
    mixing_right,
    update_in,
    update_out,
):
    n_region = lax.axis_size("region")
    n_sub = lax.axis_size("sub")
    region = lax.axis_index("region")
    sub_index = lax.axis_index("sub")
    natoms = BS * n_region * n_sub
    per_region = pair_blocks.shape[1] // n_region
    region_list = (
        lax.dynamic_slice_in_dim(pair_blocks, region * per_region, per_region, 1) - region * n_sub
    )
    region_masks = lax.dynamic_slice_in_dim(pair_mask, region * per_region, per_region, 0)
    first_pair = jnp.sum((region_list[0] < sub_index).astype(jnp.int32))
    pair_count = jnp.sum((region_list[0] == sub_index).astype(jnp.int32))
    phases = jnp.dot(wavevectors.T, positions, precision=HIGHEST)
    cosines = jnp.cos(phases)
    sines = jnp.sin(phases)
    scale = 1.0 / math.sqrt(natoms * KW)
    channels = scalars.shape[1]
    scalars_now, vectors_now = (scalars, vectors)
    for layer_id in range(LAYERS):
        local_sources = message_sources(
            scalars_now, vectors_now, message_in[layer_id], message_out[layer_id]
        )
        region_sources, region_positions = (
            lax.all_gather(local_sources, "sub", axis=0, tiled=True),
            lax.all_gather(positions, "sub", axis=1, tiled=True),
        )
        filters = filter_weight[layer_id]

        def visit(step_id, totals):
            sum_scalar, sum_vector = totals
            pair_id = first_pair + step_id
            first_row = region_list[0, pair_id] * BS
            second_row = region_list[1, pair_id] * BS
            pos_first = lax.dynamic_slice_in_dim(region_positions, first_row, BS, 1)
            pos_second = lax.dynamic_slice_in_dim(region_positions, second_row, BS, 1)
            radial, direction = geometry(pos_first, pos_second, region_masks[pair_id])
            source_first = lax.dynamic_slice_in_dim(region_sources, first_row, BS, 0)
            source_second = lax.dynamic_slice_in_dim(region_sources, second_row, BS, 0)
            to_first, to_second = pair_terms(
                radial, direction, source_first, source_second, filters
            )
            sum_scalar = add_rows(sum_scalar, to_first[0], first_row, 0)
            sum_scalar = add_rows(sum_scalar, to_second[0], second_row, 0)
            sum_vector = add_rows(sum_vector, to_first[1], first_row, 1)
            sum_vector = add_rows(sum_vector, to_second[1], second_row, 1)
            return (sum_scalar, sum_vector)

        start = (
            jnp.zeros((n_sub * BS, channels), jnp.float32),
            jnp.zeros((3, n_sub * BS, channels), jnp.float32),
        )
        sum_scalar, sum_vector = lax.fori_loop(0, pair_count, visit, start)
        delta_scalar, delta_vector = (
            lax.psum_scatter(sum_scalar, "sub", scatter_dimension=0, tiled=True),
            lax.psum_scatter(sum_vector, "sub", scatter_dimension=1, tiled=True),
        )
        charges = jnp.dot(scalars_now, ewald_weight[layer_id], precision=HIGHEST)
        local_re = jnp.dot(cosines, charges, precision=HIGHEST)
        local_im = jnp.dot(sines, charges, precision=HIGHEST)
        structure_re, structure_im = lax.psum((local_re, local_im), ("region", "sub"))
        ewald = jnp.dot(cosines.T, ewald_filter[layer_id] * structure_re, precision=HIGHEST)
        ewald = (
            ewald + jnp.dot(sines.T, ewald_filter[layer_id] * structure_im, precision=HIGHEST)
        ) * scale
        mid_scalars = scalars_now + delta_scalar + ewald
        mid_vectors = vectors_now + delta_vector
        scalars_now, vectors_now = update_block(
            mid_scalars,
            mid_vectors,
            mixing_left[layer_id],
            mixing_right[layer_id],
            update_in[layer_id],
            update_out[layer_id],
        )
    return (scalars_now, vectors_now)


def solution(mesh):
    placed = (
        P(("region", "sub"), None),
        P(None, ("region", "sub"), None),
        P(None, ("region", "sub")),
        P(),
        P(),
        P(),
        P(),
        P(),
        P(),
        P(),
        P(),
        P(),
        P(),
        P(),
        P(),
    )
    return jax.shard_map(
        body,
        mesh=mesh,
        in_specs=placed,
        out_specs=(P(("region", "sub"), None), P(None, ("region", "sub"), None)),
        check_vma=False,
    )
```

profile of v0, /device:TPU:0, one launch (start us, length us, event | category | flops | bytes accessed | tf_op | source)
XLA Modules:
  0.0 534.6 jit_solution(3791786770062615468)
XLA Ops:
  14.2 1.7 fusion.203
  18.8 14.6 %all_gather.10 = f32[3,1024]{1,0:T(4,128)S(1)} all-gather(f32[3,128]{1,0:T(4,128)S(1)} %copy-done.33), channel_id=1, replica_groups=mesh['region'=4,'sub'=8] {'sub'}, dimensions={1}, use_global_device_ids=true | all-gather | bytes 13824 | tf_op jit(solution)/shard_map/all_gather | solution.py:152
  34.2 17.5 %all-gather.3.cloned.1.call-done = f32[1024,640]{1,0:T(8,128)} async-done(((f32[128,640]{1,0:T(8,128)}), f32[1024,640]{1,0:T(8,128)}) %all-gather.3.cloned.1.call-update) | async-done | bytes 2621456 | tf_op jit(solution)/shard_map/all_gather | solution.py:151
  52.6 112.0 %while.28 = (s32[]{:T(128)}, f32[1024,128]{1,0:T(8,128)}, f32[3,1024,128]{2,1,0:T(8,128)S(1)}, s32[]{:T(128)}, s32[]{:T(128)}, /*index=5*/s32[2,12]{1,0:T(2,128)...) while((s32[]{:T(128)}, f32[1024,128]{1,0:T(8,128)}, ...), condition=%wide.region_4.5_spmd, body=%wide.region_2.4_spmd.sunk | while | flops 8071397376 | bytes 83159616 | solution.py:179
  57.6 2.4 broadcast_multiply_fusion.8
  59.9 5.5 %fusion.299 = f32[7680,128]{1,0:T(8,128)S(1)} fusion(f32[7680,128]{1,0:T(8,128)} %bitcast.491, f32[1024,640]{1,0:T(8,128)} %get-tuple-element.754, s32[]{:T(128)S(6)} %select_n.73, s32[]{:T(128)S(6)} %add.534), kind=kOutput, calls=%fused_computation.59.clone.1 | convolution fusion | flops 1509949440 | bytes 7929864 | tf_op jit(solution)/shard_map/while/body/dot_general | solution.py:44
  66.2 4.0 fusion.301
  70.5 6.7 %fusion.297 = f32[20,128,640]{2,1,0:T(8,128)S(1)} fusion(f32[1024,640]{1,0:T(8,128)} %get-tuple-element.754, s32[]{:T(128)S(6)} %select_n.72, f32[128,128]{1,0:T(8,128)S(1)} %copy.298, f32[128,128]{1,0:T(8,128)S(1)} %copy.299, f32[20]{0:T(128)S(1)} %iota_multiply_fusion.4), kind=kOutput, calls=%fused_computation.42.clone.1 | convolution fusion | flops 2518220800 | bytes 7012436 | tf_op jit(solution)/shard_map/while/body/dot_general | solution.py:41
  77.2 6.7 %fusion.296 = f32[20,128,640]{2,1,0:T(8,128)S(1)} fusion(f32[1024,640]{1,0:T(8,128)} %get-tuple-element.754, s32[]{:T(128)S(6)} %select_n.73, f32[128,128]{1,0:T(8,128)S(1)} %get-tuple-element.636, f32[20]{0:T(128)S(1)} %iota_multiply_fusion.4, f32[128,128]{1,0:T(8,128)S(1)} %get-tuple-element.639), kind=kOutput, calls=%fused_computation.44.clone.1 | convolution fusion | flops 2518220800 | bytes 7012436 | tf_op jit(solution)/shard_map/while/body/dot_general | solution.py:41
  84.0 2.6 fusion.303
  94.5 2.4 broadcast_multiply_fusion.8
  96.9 5.5 %fusion.299 = f32[7680,128]{1,0:T(8,128)S(1)} fusion(f32[7680,128]{1,0:T(8,128)} %bitcast.491, f32[1024,640]{1,0:T(8,128)} %get-tuple-element.754, s32[]{:T(128)S(6)} %select_n.73, s32[]{:T(128)S(6)} %add.534), kind=kOutput, calls=%fused_computation.59.clone.1 | convolution fusion | flops 1509949440 | bytes 7929864 | tf_op jit(solution)/shard_map/while/body/dot_general | solution.py:44
  103.2 4.1 fusion.301
  107.5 6.7 %fusion.297 = f32[20,128,640]{2,1,0:T(8,128)S(1)} fusion(f32[1024,640]{1,0:T(8,128)} %get-tuple-element.754, s32[]{:T(128)S(6)} %select_n.72, f32[128,128]{1,0:T(8,128)S(1)} %copy.298, f32[128,128]{1,0:T(8,128)S(1)} %copy.299, f32[20]{0:T(128)S(1)} %iota_multiply_fusion.4), kind=kOutput, calls=%fused_computation.42.clone.1 | convolution fusion | flops 2518220800 | bytes 7012436 | tf_op jit(solution)/shard_map/while/body/dot_general | solution.py:41
  114.2 6.7 %fusion.296 = f32[20,128,640]{2,1,0:T(8,128)S(1)} fusion(f32[1024,640]{1,0:T(8,128)} %get-tuple-element.754, s32[]{:T(128)S(6)} %select_n.73, f32[128,128]{1,0:T(8,128)S(1)} %get-tuple-element.636, f32[20]{0:T(128)S(1)} %iota_multiply_fusion.4, f32[128,128]{1,0:T(8,128)S(1)} %get-tuple-element.639), kind=kOutput, calls=%fused_computation.44.clone.1 | convolution fusion | flops 2518220800 | bytes 7012436 | tf_op jit(solution)/shard_map/while/body/dot_general | solution.py:41
  120.9 2.6 fusion.303
  131.5 2.4 broadcast_multiply_fusion.8
  133.9 5.5 %fusion.299 = f32[7680,128]{1,0:T(8,128)S(1)} fusion(f32[7680,128]{1,0:T(8,128)} %bitcast.491, f32[1024,640]{1,0:T(8,128)} %get-tuple-element.754, s32[]{:T(128)S(6)} %select_n.73, s32[]{:T(128)S(6)} %add.534), kind=kOutput, calls=%fused_computation.59.clone.1 | convolution fusion | flops 1509949440 | bytes 7929864 | tf_op jit(solution)/shard_map/while/body/dot_general | solution.py:44
  140.1 4.1 fusion.301
  144.4 6.7 %fusion.297 = f32[20,128,640]{2,1,0:T(8,128)S(1)} fusion(f32[1024,640]{1,0:T(8,128)} %get-tuple-element.754, s32[]{:T(128)S(6)} %select_n.72, f32[128,128]{1,0:T(8,128)S(1)} %copy.298, f32[128,128]{1,0:T(8,128)S(1)} %copy.299, f32[20]{0:T(128)S(1)} %iota_multiply_fusion.4), kind=kOutput, calls=%fused_computation.42.clone.1 | convolution fusion | flops 2518220800 | bytes 7012436 | tf_op jit(solution)/shard_map/while/body/dot_general | solution.py:41
  151.1 6.7 %fusion.296 = f32[20,128,640]{2,1,0:T(8,128)S(1)} fusion(f32[1024,640]{1,0:T(8,128)} %get-tuple-element.754, s32[]{:T(128)S(6)} %select_n.73, f32[128,128]{1,0:T(8,128)S(1)} %get-tuple-element.636, f32[20]{0:T(128)S(1)} %iota_multiply_fusion.4, f32[128,128]{1,0:T(8,128)S(1)} %get-tuple-element.639), kind=kOutput, calls=%fused_computation.44.clone.1 | convolution fusion | flops 2518220800 | bytes 7012436 | tf_op jit(solution)/shard_map/while/body/dot_general | solution.py:41
  157.9 2.6 fusion.303
  164.7 1.6 copy.84
  169.2 60.8 %reduce-scatter.5.cloned.1.call-done = f32[128,128]{1,0:T(8,128)} async-done(((f32[1024,128]{1,0:T(8,128)}), f32[128,128]{1,0:T(8,128)}) %reduce-scatter.5.cloned.1.call-update) | async-done | bytes 65552 | tf_op jit(solution)/shard_map/reduce_scatter | solution.py:181
  231.6 33.0 %reduce-scatter.7.cloned.1.call-done = f32[3,128,128]{1,2,0:T(8,128)} async-done(((f32[3,1024,128]{1,2,0:T(8,128)}), f32[3,128,128]{1,2,0:T(8,128)}) %reduce-scatter.7.cloned.1.call-update) | async-done | bytes 196624 | tf_op jit(solution)/shard_map/reduce_scatter | solution.py:182
  272.1 31.6 %all-gather.5.cloned.1.call-done = f32[1024,640]{0,1:T(8,128)} async-done(((f32[128,640]{0,1:T(8,128)}), f32[1024,640]{0,1:T(8,128)}) %all-gather.5.cloned.1.call-update) | async-done | bytes 2621456 | tf_op jit(solution)/shard_map/all_gather | solution.py:151
  303.7 3.2 copy.95
  307.9 113.9 %while.29 = (s32[]{:T(128)}, f32[1024,128]{1,0:T(8,128)}, f32[3,1024,128]{2,1,0:T(8,128)S(1)}, s32[]{:T(128)}, s32[]{:T(128)}, /*index=5*/s32[2,12]{1,0:T(2,128)...) while((s32[]{:T(128)}, f32[1024,128]{1,0:T(8,128)}, ...), condition=%wide.region_13.14_spmd, body=%wide.region_11.13_spmd.sunk | while | flops 8071397376 | bytes 82949512 | solution.py:179
  313.6 2.4 broadcast_multiply_fusion.10
  315.9 5.5 %fusion.323 = f32[7680,128]{1,0:T(8,128)S(1)} fusion(f32[7680,128]{1,0:T(8,128)} %bitcast.492, f32[1024,640]{1,0:T(8,128)} %get-tuple-element.802, s32[]{:T(128)S(6)} %select_n.76, s32[]{:T(128)S(6)} %add.551), kind=kOutput, calls=%fused_computation.151.clone.1 | convolution fusion | flops 1509949440 | bytes 7929864 | tf_op jit(solution)/shard_map/while/body/dot_general | solution.py:44
  322.2 4.0 fusion.325
  326.5 6.7 %fusion.321 = f32[20,128,640]{2,1,0:T(8,128)S(1)} fusion(f32[1024,640]{1,0:T(8,128)} %get-tuple-element.802, s32[]{:T(128)S(6)} %select_n.75, f32[128,128]{1,0:T(8,128)S(1)} %copy.300, f32[128,128]{1,0:T(8,128)S(1)} %copy.301, f32[20]{0:T(128)S(1)} %iota_multiply_fusion.5), kind=kOutput, calls=%fused_computation.134.clone.1 | convolution fusion | flops 2518220800 | bytes 7012436 | tf_op jit(solution)/shard_map/while/body/dot_general | solution.py:41
  333.2 6.7 %fusion.320 = f32[20,128,640]{2,1,0:T(8,128)S(1)} fusion(f32[1024,640]{1,0:T(8,128)} %get-tuple-element.802, s32[]{:T(128)S(6)} %select_n.76, f32[128,128]{1,0:T(8,128)S(1)} %get-tuple-element.681, f32[20]{0:T(128)S(1)} %iota_multiply_fusion.5, f32[128,128]{1,0:T(8,128)S(1)} %get-tuple-element.684), kind=kOutput, calls=%fused_computation.136.clone.1 | convolution fusion | flops 2518220800 | bytes 7012436 | tf_op jit(solution)/shard_map/while/body/dot_general | solution.py:41
  339.9 2.6 fusion.327
  351.2 2.4 broadcast_multiply_fusion.10
  353.5 5.5 %fusion.323 = f32[7680,128]{1,0:T(8,128)S(1)} fusion(f32[7680,128]{1,0:T(8,128)} %bitcast.492, f32[1024,640]{1,0:T(8,128)} %get-tuple-element.802, s32[]{:T(128)S(6)} %select_n.76, s32[]{:T(128)S(6)} %add.551), kind=kOutput, calls=%fused_computation.151.clone.1 | convolution fusion | flops 1509949440 | bytes 7929864 | tf_op jit(solution)/shard_map/while/body/dot_general | solution.py:44
  359.8 4.0 fusion.325
  364.1 6.7 %fusion.321 = f32[20,128,640]{2,1,0:T(8,128)S(1)} fusion(f32[1024,640]{1,0:T(8,128)} %get-tuple-element.802, s32[]{:T(128)S(6)} %select_n.75, f32[128,128]{1,0:T(8,128)S(1)} %copy.300, f32[128,128]{1,0:T(8,128)S(1)} %copy.301, f32[20]{0:T(128)S(1)} %iota_multiply_fusion.5), kind=kOutput, calls=%fused_computation.134.clone.1 | convolution fusion | flops 2518220800 | bytes 7012436 | tf_op jit(solution)/shard_map/while/body/dot_general | solution.py:41
  370.9 6.7 %fusion.320 = f32[20,128,640]{2,1,0:T(8,128)S(1)} fusion(f32[1024,640]{1,0:T(8,128)} %get-tuple-element.802, s32[]{:T(128)S(6)} %select_n.76, f32[128,128]{1,0:T(8,128)S(1)} %get-tuple-element.681, f32[20]{0:T(128)S(1)} %iota_multiply_fusion.5, f32[128,128]{1,0:T(8,128)S(1)} %get-tuple-element.684), kind=kOutput, calls=%fused_computation.136.clone.1 | convolution fusion | flops 2518220800 | bytes 7012436 | tf_op jit(solution)/shard_map/while/body/dot_general | solution.py:41
  377.6 2.6 fusion.327
  388.8 2.4 broadcast_multiply_fusion.10
  391.2 5.5 %fusion.323 = f32[7680,128]{1,0:T(8,128)S(1)} fusion(f32[7680,128]{1,0:T(8,128)} %bitcast.492, f32[1024,640]{1,0:T(8,128)} %get-tuple-element.802, s32[]{:T(128)S(6)} %select_n.76, s32[]{:T(128)S(6)} %add.551), kind=kOutput, calls=%fused_computation.151.clone.1 | convolution fusion | flops 1509949440 | bytes 7929864 | tf_op jit(solution)/shard_map/while/body/dot_general | solution.py:44
  397.5 4.0 fusion.325
  401.8 6.7 %fusion.321 = f32[20,128,640]{2,1,0:T(8,128)S(1)} fusion(f32[1024,640]{1,0:T(8,128)} %get-tuple-element.802, s32[]{:T(128)S(6)} %select_n.75, f32[128,128]{1,0:T(8,128)S(1)} %copy.300, f32[128,128]{1,0:T(8,128)S(1)} %copy.301, f32[20]{0:T(128)S(1)} %iota_multiply_fusion.5), kind=kOutput, calls=%fused_computation.134.clone.1 | convolution fusion | flops 2518220800 | bytes 7012436 | tf_op jit(solution)/shard_map/while/body/dot_general | solution.py:41
  408.5 6.7 %fusion.320 = f32[20,128,640]{2,1,0:T(8,128)S(1)} fusion(f32[1024,640]{1,0:T(8,128)} %get-tuple-element.802, s32[]{:T(128)S(6)} %select_n.76, f32[128,128]{1,0:T(8,128)S(1)} %get-tuple-element.681, f32[20]{0:T(128)S(1)} %iota_multiply_fusion.5, f32[128,128]{1,0:T(8,128)S(1)} %get-tuple-element.684), kind=kOutput, calls=%fused_computation.136.clone.1 | convolution fusion | flops 2518220800 | bytes 7012436 | tf_op jit(solution)/shard_map/while/body/dot_general | solution.py:41
  415.3 2.6 fusion.327
  426.2 61.5 %reduce-scatter.9.cloned.1.call-done = f32[128,128]{1,0:T(8,128)} async-done(((f32[1024,128]{1,0:T(8,128)}), f32[128,128]{1,0:T(8,128)}) %reduce-scatter.9.cloned.1.call-update) | async-done | bytes 65552 | tf_op jit(solution)/shard_map/reduce_scatter | solution.py:181
  489.4 33.1 %reduce-scatter.11.cloned.1.call-done = f32[3,128,128]{1,2,0:T(8,128)} async-done(((f32[3,1024,128]{1,2,0:T(8,128)}), f32[3,128,128]{1,2,0:T(8,128)}) %reduce-scatter.11.cloned.1.call-update) | async-done | bytes 196624 | tf_op jit(solution)/shard_map/reduce_scatter | solution.py:182
  (315 shorter events, 73.5 us)
Async XLA Ops:
  8.0 25.4 %copy-start = (s32[48,547]{1,0:T(8,128)S(1)}, s32[48,547]{1,0:T(8,128)}, u32[]{:S(2)}) copy-start(s32[48,547]{1,0:T(8,128)} %param.23) | copy-start | bytes 315076
  8.0 5.9 %copy-start.13 = (f32[128,128]{1,0:T(8,128)S(1)}, f32[128,128]{1,0:T(8,128)}, u32[]{:S(2)}) copy-start(f32[128,128]{1,0:T(8,128)} %param.19) | copy-start | bytes 196612
  8.0 5.9 %copy-start.22 = (f32[2,128,128]{2,1,0:T(8,128)S(1)}, f32[2,128,128]{2,1,0:T(8,128)}, u32[]{:S(2)}) copy-start(f32[2,128,128]{2,1,0:T(8,128)} %param.28) | copy-start | bytes 393220
  8.0 6.1 %copy-start.33 = (f32[3,128]{1,0:T(4,128)S(1)}, f32[3,128]{1,0:T(4,128)}, u32[]{:S(2)}) copy-start(f32[3,128]{1,0:T(4,128)} %param.21) | copy-start | bytes 4612
  8.0 6.1 %copy-start.32 = (f32[3,512]{1,0:T(4,128)S(1)}, f32[3,512]{1,0:T(4,128)}, u32[]{:S(2)}) copy-start(f32[3,512]{1,0:T(4,128)} %param.24) | copy-start | bytes 18436
  8.1 43.6 %all-gather.3.cloned.1.call-start = ((), (), s32[]{:S(2)}) async-start(), calls=%async_computation.4 | async-start | bytes 2949120 | tf_op jit(solution)/shard_map/all_gather | solution.py:151
  13.1 0.7 copy-start.15
  13.8 19.5 %copy-start.31 = (f32[2,20,384]{2,0,1:T(2,128)S(1)}, f32[2,20,384]{2,0,1:T(2,128)}, u32[]{:S(2)}) copy-start(f32[2,20,384]{2,0,1:T(2,128)} %param.27) | copy-start | bytes 184324
  13.8 153.6 %all-reduce.7.cloned.1.call-start = ((), (), s32[]{:S(2)}) async-start(), calls=%async_computation.11 | async-start | bytes 1048576 | tf_op jit(solution)/shard_map/psum | solution.py:187
  14.2 19.3 %copy-start.34 = (s32[2,48]{1,0:T(2,128)S(1)}, s32[2,48]{1,0:T(2,128)}, u32[]{:S(2)}) copy-start(s32[2,48]{1,0:T(2,128)} %param.22) | copy-start | bytes 1156
  15.8 0.7 copy-start.2
  15.8 1.8 copy-start.5
  18.7 211.3 %reduce-scatter.5.cloned.1.call-start = ((), (), s32[]{:S(2)}) async-start(), calls=%async_computation.5 | async-start | bytes 589824 | tf_op jit(solution)/shard_map/reduce_scatter | solution.py:181
  53.4 2.8 copy-start.28
  86.6 3.1 copy-start.29
  90.3 2.8 copy-start.28
  123.6 3.1 copy-start.29
  127.3 2.8 copy-start.28
  160.5 3.1 copy-start.29
  164.6 1.7 copy-start.30
  164.7 99.9 %reduce-scatter.7.cloned.1.call-start = ((), (), s32[]{:S(2)}) async-start(), calls=%async_computation.6 | async-start | bytes 1769472 | tf_op jit(solution)/shard_map/reduce_scatter | solution.py:182
  166.4 0.9 copy-start.12
  166.4 1.1 copy-start.3
  166.4 1.2 copy-start.8
  166.4 63.6 %copy-start.6 = (f32[512,128]{1,0:T(8,128)S(1)}, f32[512,128]{1,0:T(8,128)}, u32[]{:S(2)}) copy-start(f32[512,128]{1,0:T(8,128)} %copy-done.5) | copy-start | bytes 786436
  166.4 137.3 %all-gather.5.cloned.1.call-start = ((), (), s32[]{:S(2)}) async-start(), calls=%async_computation.7 | async-start | bytes 2949120 | tf_op jit(solution)/shard_map/all_gather | solution.py:151
  167.4 98.1 %copy-start.26 = (f32[2,128,128]{2,1,0:T(8,128)S(1)}, f32[2,128,128]{2,1,0:T(8,128)}, u32[]{:S(2)}) copy-start(f32[2,128,128]{2,1,0:T(8,128)} %param.30) | copy-start | bytes 393220
  169.2 96.9 %copy-start.24 = (f32[2,128,128]{2,1,0:T(8,128)S(1)}, f32[2,128,128]{2,1,0:T(8,128)}, u32[]{:S(2)}) copy-start(f32[2,128,128]{2,1,0:T(8,128)} %param.31) | copy-start | bytes 393220
  231.6 35.0 %copy-start.19 = (f32[2,256,128]{2,1,0:T(8,128)S(1)}, f32[2,256,128]{2,1,0:T(8,128)}, u32[]{:S(2)}) copy-start(f32[2,256,128]{2,1,0:T(8,128)} %param.32) | copy-start | bytes 786436
  231.6 35.3 %copy-start.17 = (f32[2,128,384]{2,1,0:T(8,128)S(1)}, f32[2,128,384]{2,1,0:T(8,128)}, u32[]{:S(2)}) copy-start(f32[2,128,384]{2,1,0:T(8,128)} %param.33) | copy-start | bytes 1179652
  265.5 1.7 copy-start.21
  265.9 1.6 copy-start.16
  267.3 2.4 copy-start.23
  268.2 0.7 copy-start.10
  268.9 0.7 copy-start.14
  269.6 154.0 %all-reduce.5.cloned.1.call-start = ((), (), s32[]{:S(2)}) async-start(), calls=%async_computation.10 | async-start | bytes 1048576 | tf_op jit(solution)/shard_map/psum | solution.py:187
  272.1 215.7 %reduce-scatter.9.cloned.1.call-start = ((), (), s32[]{:S(2)}) async-start(), calls=%async_computation.8 | async-start | bytes 589824 | tf_op jit(solution)/shard_map/reduce_scatter | solution.py:181
  421.8 100.7 %reduce-scatter.11.cloned.1.call-start = ((), (), s32[]{:S(2)}) async-start(), calls=%async_computation.9 | async-start | bytes 1769472 | tf_op jit(solution)/shard_map/reduce_scatter | solution.py:182
  423.5 0.9 copy-start.4
  423.5 1.1 copy-start.9
  423.5 64.3 %copy-start.7 = (f32[512,128]{1,0:T(8,128)S(1)}, f32[512,128]{1,0:T(8,128)}, u32[]{:S(2)}) copy-start(f32[512,128]{1,0:T(8,128)} %copy-done.5) | copy-start | bytes 786436
  423.5 99.0 %copy-start.11 = (f32[3,128,128]{1,2,0:T(8,128)S(1)}, f32[3,128,128]{1,2,0:T(8,128)}, u32[]{:S(2)}) copy-start(f32[3,128,128]{1,2,0:T(8,128)} %copy-done.10) | copy-start | bytes 589828
  423.5 99.9 %copy-start.25 = (f32[2,128,128]{2,1,0:T(8,128)S(1)}, f32[2,128,128]{2,1,0:T(8,128)}, u32[]{:S(2)}) copy-start(f32[2,128,128]{2,1,0:T(8,128)} %param.31) | copy-start | bytes 393220
  424.6 99.4 %copy-start.27 = (f32[2,128,128]{2,1,0:T(8,128)S(1)}, f32[2,128,128]{2,1,0:T(8,128)}, u32[]{:S(2)}) copy-start(f32[2,128,128]{2,1,0:T(8,128)} %param.30) | copy-start | bytes 393220
  487.8 36.7 %copy-start.20 = (f32[2,256,128]{2,1,0:T(8,128)S(1)}, f32[2,256,128]{2,1,0:T(8,128)}, u32[]{:S(2)}) copy-start(f32[2,256,128]{2,1,0:T(8,128)} %param.32) | copy-start | bytes 786436
  489.4 35.4 %copy-start.18 = (f32[2,128,384]{2,1,0:T(8,128)S(1)}, f32[2,128,384]{2,1,0:T(8,128)}, u32[]{:S(2)}) copy-start(f32[2,128,384]{2,1,0:T(8,128)} %param.33) | copy-start | bytes 1179652
  524.5 2.4 copy-start.1
Sparse Core Ops, SparseCore 0:
  14.0 37.6 all-gather.2
  164.8 65.1 reduce-scatter.4
  232.4 32.0 reduce-scatter.6
  269.7 33.9 all-gather.4
  421.9 65.7 reduce-scatter.8
  490.0 32.4 reduce-scatter.10
Sparse Core Ops, SparseCore 1:
  20.7 142.4 all-reduce.6
  276.4 137.9 all-reduce.4
where the time goes:
time: 541 us; the launch traced here: 535 us
  waiting for transfers between devices  238 us (44%)
  matrix products  157 us (29%)
  other arithmetic  63.9 us (12%)
  local copies, waits for them, and re-layouts  26.6 us (5%)
  loops' own time  18.2 us (3%)
  between operations  16.4 us (3%)
  blocking collectives  14.6 us (3%)
    reduce_scatter x2, waiting for transfers between devices, body(): lax.psum_scatter(sum_scalar, 'sub', scatter_dimension=0, tiled=True)  122 us
    dot_general x12, matrix products, side_terms(): jnp.dot(radial.reshape(-1, radial.shape[2]), source, precision=HIGHEST)  80.6 us
    reduce_scatter x2, waiting for transfers between devices, body(): lax.psum_scatter(sum_vector, 'sub', scatter_dimension=1, tiled=True)  66.1 us
    dot_general x12, matrix products, side_terms(): jnp.dot(steered, source[:, 4 * channels:], precision=HIGHEST)  57.3 us
    all_gather x2, waiting for transfers between devices, body(): lax.all_gather(local_sources, 'sub', axis=0, tiled=True)  49.1 us
    another operation x2, loops' own time, body(): sum_scalar, sum_vector = lax.fori_loop(0, pair_count, visit, start)  18.2 us
    dynamic_update_slice x24, other arithmetic, add_rows(): lax.dynamic_update_slice_in_dim(target, current + delta, row_at, axis_id)  18 us
    mul x12, other arithmetic, side_terms(): steered = (direction[:, None] * radial[None]).reshape(-1, radial.shape[2])  17 us
  transfers between devices with their start and end apart: 8, of which 6 were waited for; matrix products, arithmetic and copies ran while one was open for 43% of the time, Pallas kernels for 0%

commit v1 on v0

v1 whole, which is shorter than its diff:
```python
import functools
import math

import jax
import jax.numpy as jnp
import numpy as np
from jax import lax
from jax.experimental import pallas as pl
from jax.experimental.pallas import tpu as pltpu
from jax.sharding import PartitionSpec as P

NRBF = 20
BS = 128
KW = 512
LAYERS = 2
BITS = 30
CUTOFF = 8.0
SPACING = CUTOFF / (NRBF - 1)
CENTER = 0.5 * CUTOFF
VMEM = 58 * 1024 * 1024
F32 = jnp.float32
BF16 = jnp.bfloat16


def split(x):
    high = x.astype(BF16)
    return high, (x - high.astype(F32)).astype(BF16)


def wide_left(x):
    high, low = split(x)
    return jnp.concatenate([high, low, high], axis=1)


def wide_right(x):
    high, low = split(x)
    return jnp.concatenate([high, high, low], axis=0)


def stacked(x):
    high, low = split(x)
    return jnp.concatenate([high, high], axis=0), low


def dot(a, b):
    return jnp.dot(a, b, preferred_element_type=F32)


def dot3(a, b):
    return dot(wide_left(a), wide_right(b))


def silu(x):
    return x / (1.0 + jnp.exp(-x))


def turn_fits():
    nodes = 0.5 * np.cos(np.pi * (np.arange(400) + 0.5) / 400)
    cheb = np.polynomial.chebyshev
    fit_cos = cheb.Chebyshev.fit(nodes * nodes, np.cos(2 * np.pi * nodes), 7, domain=[0, 0.25])
    fit_sin = cheb.Chebyshev.fit(nodes * nodes, np.sinc(2 * nodes) * 2 * np.pi, 7, domain=[0, 0.25])
    to_poly = lambda fit: [float(c) for c in fit.convert(kind=np.polynomial.Polynomial).coef]
    return to_poly(fit_cos), to_poly(fit_sin)


COS_FIT, SIN_FIT = turn_fits()


def horner(coefs, x):
    total = jnp.full_like(x, coefs[-1])
    for c in coefs[-2::-1]:
        total = total * x + c
    return total


def cos_sin(turns):
    rest = turns - jnp.round(turns)
    square = rest * rest
    return horner(COS_FIT, square), horner(SIN_FIT, square) * rest


def columns_of(pos):
    return jnp.transpose(pos)


def cost(flops, moved, exps=0):
    return pl.CostEstimate(flops=int(flops), bytes_accessed=int(moved), transcendentals=int(exps))


def fixed(shape, *at):
    at = tuple(at) + (0,) * (len(shape) - len(at))
    return pl.BlockSpec(shape, lambda *_: at)


SMEM_SPEC = pl.BlockSpec(memory_space=pltpu.SMEM)


def meta_kernel(n_sub, per_region, slots, ids_ref, pairs_ref, meta_ref):
    region, sub = ids_ref[0], ids_ref[1]
    base = region * per_region
    for row in range(5):
        for slot in range(slots):
            meta_ref[row, slot] = 0

    def visit(p, found):
        first = pairs_ref[0, base + p] - region * n_sub
        second = pairs_ref[1, base + p] - region * n_sub
        hit = (first == sub) | (second == sub)

        @pl.when(hit & (found < slots))
        def _():
            other = jnp.where(first == sub, second, first)
            meta_ref[1, found] = base + p
            meta_ref[2, found] = other ^ sub
            meta_ref[3, found] = (first == sub).astype(jnp.int32)
            meta_ref[4, found] = other

        return found + hit.astype(jnp.int32)

    meta_ref[0, 0] = lax.fori_loop(0, per_region, visit, jnp.int32(0))


def find_pairs(ids, pair_blocks, n_sub, per_region, slots):
    return pl.pallas_call(
        functools.partial(meta_kernel, n_sub, per_region, slots),
        in_specs=[SMEM_SPEC, SMEM_SPEC],
        out_specs=SMEM_SPEC,
        out_shape=jax.ShapeDtypeStruct((5, slots), jnp.int32),
    )(ids, pair_blocks)


def at_pair(step, meta_ref):
    return (jnp.maximum(jnp.minimum(step, (meta_ref[0, 0] - 1) // 2), 0), 0, 0)


def near_dots(tables, rows, sources):
    number = len(sources)
    values = [tables[i, rows, :] for i in range(number)]
    highs = [v[:, :BS] for v in values]
    both = [b for b, _ in sources]
    low = [l for _, l in sources]
    return dot(jnp.concatenate(values, axis=1), jnp.concatenate(both, axis=0)) + dot(
        jnp.concatenate(highs, axis=1), jnp.concatenate(low, axis=0)
    )


def add_terms(totals, cols, tables, sources, weight):
    group = 4
    total = totals[:, cols]
    for k in range(0, NRBF, group):
        product = near_dots(tables, slice(k * BS, (k + group) * BS), sources)
        for g in range(group):
            total = total + product[g * BS : (g + 1) * BS] * weight[k + g : k + g + 1]
    totals[:, cols] = total


def one_or_two(step, count, act):
    for number in (1, 2):
        here = (2 * step + 1 == count) if number == 1 else (2 * step + 1 < count)
        pl.when(here)(functools.partial(act, number))


def radial_tables(meta_ref, listed, at, near, pos_ref, masks_ref, radial_ref, over_ref):
    pair = meta_ref[1, listed]
    slot = meta_ref[2, listed]
    is_first = meta_ref[3, listed]
    words = masks_ref[pl.ds(pair, 1), :]
    tiles = -(-words.shape[1] // BS)
    rest = tiles * BS - words.shape[1]
    if rest:
        words = jnp.concatenate([words, jnp.zeros((1, rest), jnp.int32)], axis=1)
    row = lax.broadcasted_iota(jnp.int32, (BS, BS), 0)
    row_tile = (row * 2185) >> 16
    spread = jnp.zeros((BS, BS), jnp.int32)
    for tile in range(tiles):
        spread = jnp.where(
            row_tile == tile,
            jnp.broadcast_to(words[:, tile * BS : (tile + 1) * BS], (BS, BS)),
            spread,
        )
    spot = (row - row_tile * BITS) * BS + lax.broadcasted_iota(jnp.int32, (BS, BS), 1)
    index = (spot * 34953) >> 20
    picked = jnp.take_along_axis(spread, index, axis=1)
    mask = (jnp.right_shift(picked, spot - index * BITS) & 1).astype(F32)
    mask = jnp.where(is_first == 1, mask, jnp.transpose(mask))
    source = jnp.zeros((8, BS), F32)
    for e in range(1, len(near)):
        source = jnp.where(slot == e, near[e][...], source)
    mine = columns_of(pos_ref[...])
    square = jnp.zeros((BS, BS), F32)
    for d in range(3):
        offset = source[d : d + 1, :] - mine[:, d : d + 1]
        square = square + offset * offset
    distance = jnp.sqrt(square + 1.0)
    inverse = 1.0 / distance
    root = math.sqrt(0.5 * math.log2(math.e))
    scaled = jnp.where(mask > 0.5, distance * (root / SPACING), 1.0e4)
    for k in range(NRBF):
        gap = scaled - k * root
        radial = jnp.exp2(-(gap * gap))
        rows = slice(k * BS, (k + 1) * BS)
        for ref, value in ((radial_ref, radial), (over_ref, radial * inverse)):
            high, low = split(value)
            ref[at, rows, 0:BS] = high
            ref[at, rows, BS : 2 * BS] = low


def early_kernel(n_sub, build, meta_ref, *refs):
    blocks, refs = refs[:n_sub], refs[n_sub:]
    places, refs = refs[:n_sub], refs[n_sub:]
    if build:
        in_ref, out_ref, filter_ref, masks_ref, partial_ref, phi_ref, radial_ref, over_ref, sources, totals = refs
    else:
        in_ref, out_ref, filter_ref, over_ref, partial_ref, phi_ref, sources, totals = refs
    step = pl.program_id(0)
    count = meta_ref[0, 0]

    @pl.when(step == 0)
    def _():
        totals[...] = jnp.zeros_like(totals)
        scalars = jnp.concatenate([blocks[e][...] for e in range(1, n_sub)], axis=0)
        hidden = silu(dot3(scalars, in_ref[0]))
        phi = dot3(hidden, out_ref[0])
        for e in range(1, n_sub):
            rows = phi[(e - 1) * BS : e * BS]
            phi_ref[e - 1] = rows[:, : 2 * BS]
            phi_r = rows[:, 2 * BS :]
            place = columns_of(places[e][...])
            parts = [phi_r] + [phi_r * (place[:, d : d + 1] - CENTER) for d in range(3)]
            for at, part in enumerate(parts):
                high, low = split(part)
                cols = slice(at * BS, (at + 1) * BS)
                sources[e - 1, 0:BS, cols] = high
                sources[e - 1, BS : 2 * BS, cols] = high
                sources[e - 1, 2 * BS :, cols] = low

    def act(number):
        if build:
            for i in range(number):
                radial_tables(meta_ref, 2 * step + i, i, places, places[0], masks_ref, radial_ref, over_ref)
        weight = filter_ref[0, :, 2 * BS :]
        weight = jnp.concatenate([weight, weight], axis=1)
        slot = [meta_ref[2, 2 * step + i] - 1 for i in range(number)]
        for tile in range(2):
            cols = slice(tile * 2 * BS, (tile + 1) * 2 * BS)
            near = [(sources[e, : 2 * BS, cols], sources[e, 2 * BS :, cols]) for e in slot]
            add_terms(totals, cols, over_ref, near, weight)

    one_or_two(step, count, act)

    @pl.when(step == pl.num_programs(0) - 1)
    def _():
        mine = columns_of(places[0][...])
        for d in range(3):
            partial_ref[d * BS : (d + 1) * BS, :] = (
                totals[:, (1 + d) * BS : (2 + d) * BS] - (mine[:, d : d + 1] - CENTER) * totals[:, :BS]
            )


def early_terms(meta, layer, blocks, spots, weights, masks=None, over=None):
    n_sub = len(blocks)
    slots = meta.shape[1]
    build = over is None
    table = pl.BlockSpec((2, NRBF * BS, 2 * BS), at_pair)
    shape = jax.ShapeDtypeStruct((slots, NRBF * BS, 2 * BS), BF16)
    out_specs = [fixed((3 * BS, BS)), fixed((n_sub - 1, BS, 2 * BS))]
    out_shape = [
        jax.ShapeDtypeStruct((3 * BS, BS), F32),
        jax.ShapeDtypeStruct((n_sub - 1, BS, 2 * BS), F32),
    ]
    return pl.pallas_call(
        functools.partial(early_kernel, n_sub, build),
        grid_spec=pltpu.PrefetchScalarGridSpec(
            num_scalar_prefetch=1,
            grid=(meta.shape[1] // 2,),
            in_specs=[fixed((BS, BS))] * n_sub
            + [fixed((8, BS), BS // 8)] * n_sub
            + [fixed((1,) + w.shape[1:], layer) for w in weights]
            + ([fixed(masks.shape)] if build else [table]),
            out_specs=out_specs + ([table, table] if build else []),
            scratch_shapes=[
                pltpu.VMEM((n_sub - 1, 3 * BS, 4 * BS), BF16),
                pltpu.VMEM((BS, 4 * BS), F32),
            ],
        ),
        out_shape=out_shape + ([shape, shape] if build else []),
        compiler_params=pltpu.CompilerParams(vmem_limit_bytes=VMEM),
        cost_estimate=cost(3 * 4 * NRBF * BS * BS * 4 * BS * 2 * 3, 10e6),
    )(meta, *blocks, *spots, *weights, masks if build else over)


def own_trig_kernel(waves_ref, place_ref, own_ref):
    waves = waves_ref[...] * (1.0 / (2.0 * math.pi))
    mine = columns_of(place_ref[...])
    turns = jnp.zeros((BS, waves.shape[1]), F32)
    for d in range(3):
        turns = turns + mine[:, d : d + 1] * waves[d : d + 1, :]
    own_ref[...] = jnp.concatenate(split(jnp.concatenate(cos_sin(turns), axis=1)), axis=1)


def own_trig_of(waves, spot):
    return pl.pallas_call(
        own_trig_kernel,
        grid=(1,),
        in_specs=[fixed(waves.shape), fixed((8, BS), BS // 8)],
        out_specs=fixed((BS, 4 * KW)),
        out_shape=jax.ShapeDtypeStruct((BS, 4 * KW), BF16),
        compiler_params=pltpu.CompilerParams(vmem_limit_bytes=VMEM),
        cost_estimate=cost(BS * KW * 40, 1e6),
    )(waves, spot)


def structure_kernel(n_sub, build, *refs):
    if build:
        ids_ref, waves_ref, refs = refs[0], refs[1], refs[2:]
        places, refs = refs[:n_sub], refs[n_sub:]
    blocks, refs = refs[:n_sub], refs[n_sub:]
    atoms = n_sub * BS
    if build:
        weight_ref, out_ref, trig_ref = refs
        waves = waves_ref[...] * (1.0 / (2.0 * math.pi))
        rows = waves.shape[1] // 2
        waves = jnp.where(ids_ref[1] % 2 == 0, waves[:, :rows], waves[:, rows:])
        half = jnp.transpose(jnp.concatenate([waves, jnp.zeros((5, rows), F32)], axis=0))
        for e in range(n_sub):
            place = places[e][...]
            turns = jnp.zeros((rows, BS), F32)
            for d in range(3):
                turns = turns + half[:, d : d + 1] * place[d : d + 1, :]
            for at, value in enumerate(cos_sin(turns)):
                block = slice(at * rows, (at + 1) * rows)
                for part, piece in enumerate(split(value)):
                    trig_ref[block, part * atoms + e * BS : part * atoms + (e + 1) * BS] = piece
    else:
        weight_ref, trig_ref, out_ref = refs
    both, low = stacked(jnp.concatenate([blocks[e][...] for e in range(n_sub)], axis=0))
    total = dot(trig_ref[...], both) + dot(trig_ref[:, :atoms], low)
    out_ref[...] = dot3(total, weight_ref[0])


def structure(layer, blocks, weight, ids=None, waves=None, spots=None, region_trig=None):
    n_sub = len(blocks)
    build = region_trig is None
    trig_shape = (KW, 2 * n_sub * BS)
    charges = [fixed((BS, BS))] * n_sub + [fixed((1,) + weight.shape[1:], layer)]
    out_shape = [jax.ShapeDtypeStruct((KW, BS), F32)]
    if build:
        in_specs = [SMEM_SPEC, fixed(waves.shape)] + [fixed((8, BS), BS // 8)] * n_sub + charges
        operands = (ids, waves, *spots, *blocks, weight)
        out_shape += [jax.ShapeDtypeStruct(trig_shape, BF16)]
    else:
        in_specs = charges + [fixed(trig_shape)]
        operands = (*blocks, weight, region_trig)
    return pl.pallas_call(
        functools.partial(structure_kernel, n_sub, build),
        grid=(1,),
        in_specs=in_specs,
        out_specs=[fixed(s.shape) for s in out_shape],
        out_shape=out_shape,
        compiler_params=pltpu.CompilerParams(vmem_limit_bytes=VMEM),
        cost_estimate=cost(KW * n_sub * BS * BS * 6, 4e6),
    )(*operands)


def late_kernel(
    scale, n_sub, meta_ref, ids_ref, scalars_ref, vectors_ref, phi_a_ref, phi_b_ref, radial_ref, partial_ref, *refs
):
    blocks, refs = refs[: n_sub - 1], refs[n_sub - 1 :]
    (
    mine_ref, other_ref, own_ref, factor_ref, filter_ref, left_ref, right_ref, gate_in_ref, gate_out_ref,
    new_scalars_ref, new_vectors_ref, totals,
    ) = refs
    step = pl.program_id(0)
    count = meta_ref[0, 0]

    @pl.when(step == 0)
    def _():
        totals[:, :BS] = jnp.zeros((BS, BS), F32)
        for d in range(3):
            totals[:, (1 + d) * BS : (2 + d) * BS] = partial_ref[d * BS : (d + 1) * BS, :]

    def act(number):
        w_s, w_v = filter_ref[0, :, :BS], filter_ref[0, :, BS : 2 * BS]
        parts = []
        for i, phi_ref in enumerate((phi_a_ref, phi_b_ref)[:number]):
            slot = meta_ref[2, 2 * step + i]
            near = blocks[0][...]
            for e in range(2, n_sub):
                near = jnp.where(slot == e, blocks[e - 1][...], near)
            phi_s, phi_v = phi_ref[0, :, :BS], phi_ref[0, :, BS:]
            parts.append([phi_s] + [phi_v * near[d * BS : (d + 1) * BS, :] for d in range(3)])
        for tile, names in enumerate(((w_s, w_v), (w_v, w_v))):
            cols = slice(tile * 2 * BS, (tile + 1) * 2 * BS)
            sources = [stacked(jnp.concatenate(p[2 * tile : 2 * tile + 2], axis=1)) for p in parts]
            add_terms(totals, cols, radial_ref, sources, jnp.concatenate(names, axis=1))

    one_or_two(step, count, act)

    @pl.when(step == pl.num_programs(0) - 1)
    def _():
        lower = ids_ref[1] % 2 == 0
        mine, other = mine_ref[...], other_ref[...]
        half = mine.shape[0] // 2
        first = jnp.where(lower, mine, other)
        second = jnp.where(lower, other, mine)
        factors = factor_ref[0] * scale
        both, low = stacked(
            jnp.concatenate(
                [
                    first[:half] * factors[:half],
                    second[:half] * factors[half:],
                    first[half:] * factors[:half],
                    second[half:] * factors[half:],
                ],
                axis=0,
            )
        )
        ewald = dot(own_ref[...], both) + dot(own_ref[:, : 2 * KW], low)
        mid_scalars = scalars_ref[...] + totals[:, :BS] + ewald
        mid_vectors = jnp.concatenate(
            [vectors_ref[d] + totals[:, (1 + d) * BS : (2 + d) * BS] for d in range(3)], axis=0
        )
        mixed = dot3(mid_vectors, jnp.concatenate([left_ref[0], right_ref[0]], axis=1))
        left, right = mixed[:, :BS], mixed[:, BS:]
        parts = [slice(d * BS, (d + 1) * BS) for d in range(3)]
        norm = jnp.sqrt(sum(right[p] * right[p] for p in parts) + 1.0)
        along = sum(left[p] * right[p] for p in parts)
        hidden = silu(dot3(jnp.concatenate([mid_scalars, norm], axis=1), gate_in_ref[0]))
        gates = dot3(hidden, gate_out_ref[0])
        g_v, g_sv, g_s = (gates[:, i * BS : (i + 1) * BS] for i in range(3))
        new_scalars_ref[...] = mid_scalars + g_sv * along + g_s
        for d, p in enumerate(parts):
            new_vectors_ref[d] = mid_vectors[p] + g_v * left[p]


def late_terms(meta, ids, layer, scale, scalars, vectors, phi, near, radial, partial, mine, other, own, weights):
    n_sub = len(near)

    def at_other(i, step, meta_ref):
        listed = jnp.minimum(2 * at_pair(step, meta_ref)[0] + i, meta_ref[0, 0] - 1)
        return (jnp.maximum(meta_ref[2, jnp.maximum(listed, 0)] - 1, 0), 0, 0)

    return pl.pallas_call(
        functools.partial(late_kernel, scale, n_sub),
        grid_spec=pltpu.PrefetchScalarGridSpec(
            num_scalar_prefetch=1,
            grid=(meta.shape[1] // 2,),
            in_specs=[
                SMEM_SPEC,
                fixed(scalars.shape),
                fixed(vectors.shape),
                pl.BlockSpec((1, BS, 2 * BS), functools.partial(at_other, 0)),
                pl.BlockSpec((1, BS, 2 * BS), functools.partial(at_other, 1)),
                pl.BlockSpec((2, NRBF * BS, 2 * BS), at_pair),
                fixed(partial.shape),
            ]
            + [fixed(b.shape) for b in near[1:]]
            + [
                fixed(mine.shape),
                fixed(other.shape),
                fixed(own.shape),
            ]
            + [fixed((1,) + w.shape[1:], layer) for w in weights],
            out_specs=[fixed(scalars.shape), fixed(vectors.shape)],
            scratch_shapes=[pltpu.VMEM((BS, 4 * BS), F32)],
        ),
        out_shape=[
            jax.ShapeDtypeStruct(scalars.shape, F32),
            jax.ShapeDtypeStruct(vectors.shape, F32),
        ],
        compiler_params=pltpu.CompilerParams(vmem_limit_bytes=VMEM),
        cost_estimate=cost(3 * 4 * NRBF * BS * BS * 4 * BS * 2 * 3, 10e6),
    )(meta, ids, scalars, vectors, phi, phi, radial, partial, *near[1:], mine, other, own, *weights)


def exchange(x, axis, mask):
    size = lax.axis_size(axis)
    return lax.ppermute(x, axis, [(i, i ^ mask) for i in range(size)])


def gather(x):
    n_sub = lax.axis_size("sub")
    parts = [None] * n_sub
    for e in range(0, n_sub, 2):
        parts[e] = x if e == 0 else exchange(x, "sub", e)
    for e in range(0, n_sub, 2):
        parts[e + 1] = exchange(parts[e], "sub", 1)
    return parts


def after(x, *others):
    return lax.optimization_barrier((x, *others))[0]


def body(
    scalars,
    vectors,
    positions,
    pair_blocks,
    pair_mask,
    wavevectors,
    message_in,
    message_out,
    filter_weight,
    ewald_weight,
    ewald_filter,
    mixing_left,
    mixing_right,
    update_in,
    update_out,
):
    n_region = lax.axis_size("region")
    n_sub = lax.axis_size("sub")
    natoms = BS * n_region * n_sub
    scale = 1.0 / math.sqrt(natoms * KW)
    per_region = pair_blocks.shape[1] // n_region
    slots = -(-min(n_sub - 1, per_region) // 2) * 2
    ids = jnp.stack([lax.axis_index("region"), lax.axis_index("sub")]).astype(jnp.int32)
    place = jnp.pad(positions, ((0, 8 - positions.shape[0]), (0, 0)))
    send = jnp.concatenate([scalars, place], axis=0)
    meta = find_pairs(ids, pair_blocks, n_sub, per_region, slots)
    own_trig = own_trig_of(wavevectors, send)
    radial = over = region_trig = spots = None
    for layer in range(LAYERS):
        blocks = gather(send)
        near = gather(vectors.reshape(3 * BS, -1))
        if layer == 0:
            spots = blocks
            first_ids = after(ids, meta, own_trig)
            partial, region_trig = structure(layer, blocks, ewald_weight, first_ids, wavevectors, spots)
        else:
            (partial,) = structure(layer, blocks, ewald_weight, region_trig=region_trig)
        others = [exchange(partial, "region", mask) for mask in range(1, n_region)]
        weights = (message_in, message_out, filter_weight)
        turn = after(meta, partial)
        if layer == 0:
            along, phi, radial, over = early_terms(turn, layer, blocks, spots, weights, masks=pair_mask)
        else:
            along, phi = early_terms(turn, layer, blocks, spots, weights, over=over)
        *others, along = lax.optimization_barrier((*others, along))
        mine = sum(others, partial)
        theirs = exchange(mine, "sub", 1)
        scalars, vectors = late_terms(
            meta, ids, layer, scale, scalars, vectors, phi, near, radial, along, mine, theirs, own_trig,
            (ewald_filter, filter_weight, mixing_left, mixing_right, update_in, update_out),
        )
        send = scalars
    return scalars, vectors


def solution(mesh):
    placed = (
        P(("region", "sub"), None),
        P(None, ("region", "sub"), None),
        P(None, ("region", "sub")),
    ) + (P(),) * 12
    return jax.shard_map(
        body,
        mesh=mesh,
        in_specs=placed,
        out_specs=(P(("region", "sub"), None), P(None, ("region", "sub"), None)),
        check_vma=False,
    )
```

time: 541 us -> 121 us (0.22); the launches traced: 535 us -> 121 us
  waiting for transfers between devices: 238 us -> 23.9 us
  matrix products: 157 us -> 0 us
  Pallas kernels: 0 us -> 63.4 us
  other arithmetic: 63.9 us -> 1.58 us
  starting transfers between devices: 0.33 us -> 25.8 us
  local copies, waits for them, and re-layouts: 26.6 us -> 4.84 us
  loops' own time: 18.2 us -> 0 us
  between operations: 16.4 us -> 1.35 us
  blocking collectives: 14.6 us -> 0 us
    reduce_scatter x4 -> x0, waiting for transfers between devices: 188 us -> none  [the longest x2 122 us: body(): lax.psum_scatter(sum_scalar, 'sub', scatter_dimension=0, tiled=True)]
    dot_general x47 -> x0, matrix products: 157 us -> none  [the longest x12 80.6 us: side_terms(): jnp.dot(radial.reshape(-1, radial.shape[2]), source, precision=HIGHEST)]
    pallas_call x0 -> x8, Pallas kernels: none -> 63.4 us  [the longest x2 26.6 us: early_terms(): pl.pallas_call(functools.partial(early_kernel, n_sub, build), grid_spec=p...]
    all_gather x2 -> x0, waiting for transfers between devices: 49.1 us -> none  [body(): lax.all_gather(local_sources, 'sub', axis=0, tiled=True)]
    ppermute x0 -> x36, starting transfers between devices: none -> 25.8 us  [exchange(): return lax.ppermute(x, axis, [(i, i ^ mask) for i in range(size)])]
    ppermute x0 -> x36, waiting for transfers between devices: none -> 23.9 us  [exchange(): return lax.ppermute(x, axis, [(i, i ^ mask) for i in range(size)])]
    mul x30 -> x0, other arithmetic: 21.1 us -> none  [the longest x12 17 us: side_terms(): steered = (direction[:, None] * radial[None]).reshape(-1, radial.shape[2])]
    another operation x2 -> x0, loops' own time: 18.2 us -> none  [body(): sum_scalar, sum_vector = lax.fori_loop(0, pair_count, visit, start)]
  transfers between devices with their start and end apart: 8 -> 36, of which waited for: 6 -> 8; matrix products, arithmetic and copies ran while one was open for 43% -> 2% of each run, Pallas kernels for 0% -> 32%
where the time goes in v1:
time: 121 us
  Pallas kernels  63.4 us (52%)
  starting transfers between devices  25.8 us (21%)
  waiting for transfers between devices  23.9 us (20%)
  local copies, waits for them, and re-layouts  4.84 us (4%)
  other arithmetic  1.58 us (1%)
  between operations  1.35 us (1%)
    pallas_call x2, Pallas kernels, early_terms(): pl.pallas_call(functools.partial(early_kernel, n_sub, build), grid_spec=p...  26.6 us
    ppermute x36, starting transfers between devices, exchange(): return lax.ppermute(x, axis, [(i, i ^ mask) for i in range(size)])  25.8 us
    pallas_call x2, Pallas kernels, late_terms(): pl.pallas_call(functools.partial(late_kernel, scale, n_sub), grid_spec=pl...  24.8 us
    ppermute x36, waiting for transfers between devices, exchange(): return lax.ppermute(x, axis, [(i, i ^ mask) for i in range(size)])  23.9 us
    pallas_call x2, Pallas kernels, structure(): pl.pallas_call(functools.partial(structure_kernel, n_sub, build), grid=(1...  8.53 us
    unnamed x75, local copies, waits for them, and re-layouts  4.84 us
  transfers between devices with their start and end apart: 36, of which 8 were waited for; matrix products, arithmetic and copies ran while one was open for 2% of the time, Pallas kernels for 32%

profile of v1, /device:TPU:0, one launch (start us, length us, event | category | flops | bytes accessed | tf_op | source)
XLA Modules:
  0.0 120.9 jit_solution(10260394896348818693)
XLA Ops:
  0.6 0.9 select_maximum_fusion.place_ref.refs_2_.refs_10_.refs_0_.refs_8_
  1.5 3.0 %collective-permute-start.1 = (f32[136,128]{1,0:T(8,128)S(1)}, f32[136,128]{1,0:T(8,128)S(1)}, u32[]{:S(2)}, u32[]{:S(2)}) collective-permute-start(f32[136,128]{1,0:T(8,128)S(1)} %select_maximum_fusion.place_ref.refs_2_.refs_10_.refs_0_.refs_8_), channel_id=1, source_target_pairs={{0,2},{1,3},{2,0},{3,1},{4,6},{5,7},{6,4},{7,5},{8,10},{9,11},{10,... | collective-permute-start | bytes 208904 | tf_op jit(solution)/shard_map/ppermute | solution.py:478
  4.5 2.6 %collective-permute-start.3 = (f32[136,128]{1,0:T(8,128)S(1)}, f32[136,128]{1,0:T(8,128)S(1)}, u32[]{:S(2)}, u32[]{:S(2)}) collective-permute-start(f32[136,128]{1,0:T(8,128)S(1)} %select_maximum_fusion.place_ref.refs_2_.refs_10_.refs_0_.refs_8_), channel_id=1, source_target_pairs={{0,4},{1,5},{2,6},{3,7},{4,0},{5,1},{6,2},{7,3},{8,12},{9,13},{10,... | collective-permute-start | bytes 208904 | tf_op jit(solution)/shard_map/ppermute | solution.py:478
  7.1 0.9 collective-permute-start.11
  8.0 0.2 collective-permute-start.2
  8.3 3.8 %collective-permute-done.3.refs_6_.refs_14_.refs_4_.refs_12_ = f32[136,128]{1,0:T(8,128)S(1)} collective-permute-done((f32[136,128]{1,0:T(8,128)S(1)}, f32[136,128]{1,0:T(8,128)S(1)}, u32[]{:S(2)}, u32[]{:S(2)}) %collective-permute-start.3) | collective-permute-done | bytes 69664 | tf_op jit(solution)/shard_map/ppermute | solution.py:478
  12.1 1.9 %collective-permute-done.5.refs_8_.refs_16_.refs_6_.refs_14_ = f32[136,128]{1,0:T(8,128)S(1)} collective-permute-done((f32[136,128]{1,0:T(8,128)S(1)}, f32[136,128]{1,0:T(8,128)S(1)}, u32[]{:S(2)}, u32[]{:S(2)}) %collective-permute-start.5) | collective-permute-done | bytes 69664 | tf_op jit(solution)/shard_map/ppermute | solution.py:478
  13.9 0.6 pad_add_fusion.ids_ref.refs_0_
  14.6 1.5 %shard_map.158.meta_ref = s32[5,8]{1,0:T(8,128)} custom-call(s32[2]{0:T(128)} %pad_add_fusion.ids_ref.refs_0_, s32[2,48]{1,0:T(2,128)} %pairs_ref.1), custom_call_target="tpu_custom_call" | custom-call | tf_op jit(solution)/shard_map/pallas_call | solution.py:124
  16.0 2.1 %shard_map.159.refs_9_ = bf16[128,2048]{1,0:T(8,128)(2,1)} custom-call(f32[3,512]{1,0:T(4,128)} %refs_1_.1, f32[136,128]{1,0:T(8,128)} %copy-done.1), custom_call_target="tpu_custom_call" | custom-call | flops 2621440 | bytes 1000000 | tf_op jit(solution)/shard_map/pallas_call | solution.py:302
  18.1 1.5 %copy.17.refs_18_.refs_11_ = f32[2,20,384]{2,1,0:T(8,128)} copy(f32[2,20,384]{2,0,1:T(2,128)} %param.23) | data formatting | bytes 122880 | tf_op args[8]
  19.6 1.2 collective-permute-start.13
  20.9 0.6 copy-done.34
  21.4 0.6 copy-done.36
  22.1 4.7 %shard_map.160 = (f32[512,128]{1,0:T(8,128)}, bf16[512,2048]{1,0:T(8,128)(2,1)}) custom-call(s32[2]{0:T(128)} %pad_add_fusion.ids_ref.refs_0_, f32[3,512]{1,0:T(4,128)} %refs_1_.1, f32[136,128]{1,0:T(8,128)} %copy-done.1, f32[136,128]{1,0:T(8,128)} %copy-done.33, f32[136,128]{1,0:T(8,128)} %copy-done.30, f32[136,128]{1,0:T(8,128)} %copy-done.34, ...), custom_call_target="tpu_custom_call" | custom-call | flops 402653184 | bytes 4000000 | tf_op jit(solution)/shard_map/pallas_call | solution.py:354
  26.7 1.6 %collective-permute-start.7 = (f32[512,128]{1,0:T(8,128)}, f32[512,128]{1,0:T(8,128)S(1)}, u32[]{:S(2)}, u32[]{:S(2)}) collective-permute-start(f32[512,128]{1,0:T(8,128)} %get-tuple-element.24), channel_id=1, source_target_pairs={{0,8},{8,0},{16,24},{24,16},{1,9},{9,1},{17,25},{25,17},{2,10},{10... | collective-permute-start | bytes 786440 | tf_op jit(solution)/shard_map/ppermute | solution.py:478
  28.3 1.5 %collective-permute-start.8 = (f32[512,128]{1,0:T(8,128)}, f32[512,128]{1,0:T(8,128)S(1)}, u32[]{:S(2)}, u32[]{:S(2)}) collective-permute-start(f32[512,128]{1,0:T(8,128)} %get-tuple-element.24), channel_id=1, source_target_pairs={{0,16},{8,24},{16,0},{24,8},{1,17},{9,25},{17,1},{25,9},{2,18},{10... | collective-permute-start | bytes 786440 | tf_op jit(solution)/shard_map/ppermute | solution.py:478
  29.8 0.5 collective-permute-start.9
  30.3 15.1 %shard_map.161 = (f32[384,128]{1,0:T(8,128)}, f32[7,128,256]{2,1,0:T(8,128)}, bf16[8,2560,256]{2,1,0:T(8,128)(2,1)}, bf16[8,2560,256]{2,1,0:T(8,128)(2,1)}) custom-call(s32[5,8]{1,0:T(8,128)} %shard_map.158.meta_ref, f32[136,128]{1,0:T(8,128)} %copy-done.1, f32[136,128]{1,0:T(8,128)} %copy-done.33, f32[136,128]{1,0:T(8,128)} %copy-done.30, ...), custom_call_target="tpu_custom_call" | custom-call | flops 12079595520 | bytes 10000000 | tf_op jit(solution)/shard_map/pallas_call | solution.py:271
  45.6 0.1 collective-permute-start.17
  45.7 0.5 collective-permute-start.10
  46.2 0.1 collective-permute-start.12
  46.3 0.4 collective-permute-start.14
  46.7 6.3 %collective-permute-done.15.refs_5_ = f32[384,128]{1,0:T(8,128)S(1)} collective-permute-done((f32[384,128]{1,0:T(8,128)S(1)}, f32[384,128]{1,0:T(8,128)S(1)}, u32[]{:S(2)}, u32[]{:S(2)}) %collective-permute-start.15) | collective-permute-done | bytes 196640 | tf_op jit(solution)/shard_map/ppermute | solution.py:478
  53.0 1.4 %collective-permute-done.16.refs_6_ = f32[384,128]{1,0:T(8,128)S(1)} collective-permute-done((f32[384,128]{1,0:T(8,128)S(1)}, f32[384,128]{1,0:T(8,128)S(1)}, u32[]{:S(2)}, u32[]{:S(2)}) %collective-permute-start.16) | collective-permute-done | bytes 196640 | tf_op jit(solution)/shard_map/ppermute | solution.py:478
  54.5 0.6 copy-done.29
  55.1 0.1 copy-done.13
  55.2 12.4 %shard_map.162 = (f32[128,128]{1,0:T(8,128)}, f32[3,128,128]{2,1,0:T(8,128)}) custom-call(s32[5,8]{1,0:T(8,128)} %shard_map.158.meta_ref, s32[2]{0:T(128)} %pad_add_fusion.ids_ref.refs_0_, f32[128,128]{1,0:T(8,128)} %scalars_ref.1, f32[3,128,128]{2,1,0:T(8,128)} %vectors_ref.1, f32[7,128,256]{2,1,0:T(8,128)} %get-tuple-element.26.phi_a_ref.phi_b_ref, ...), custom_call_target="tpu_custom_call" | custom-call | flops 12079595520 | bytes 10000000 | tf_op jit(solution)/shard_map/pallas_call | solution.py:443
  67.7 4.3 %collective-permute-start.23 = (f32[128,128]{1,0:T(8,128)}, f32[128,128]{1,0:T(8,128)S(1)}, u32[]{:S(2)}, u32[]{:S(2)}) collective-permute-start(f32[128,128]{1,0:T(8,128)} %get-tuple-element.33.refs_0_.scalars_ref), channel_id=1, source_target_pairs={{0,6},{1,7},{2,4},{3,5},{4,2},{5,3},{6,0},{7,1},{8,14},{9,15},{10,... | collective-permute-start | bytes 196616 | tf_op jit(solution)/shard_map/ppermute | solution.py:478
  72.0 1.4 %collective-permute-done.19.refs_2_ = f32[128,128]{1,0:T(8,128)S(1)} collective-permute-done((f32[128,128]{1,0:T(8,128)}, f32[128,128]{1,0:T(8,128)S(1)}, u32[]{:S(2)}, u32[]{:S(2)}) %collective-permute-start.19) | collective-permute-done | bytes 65568 | tf_op jit(solution)/shard_map/ppermute | solution.py:478
  73.4 0.5 collective-permute-start.22
  73.9 1.4 %collective-permute-done.23.refs_6_ = f32[128,128]{1,0:T(8,128)S(1)} collective-permute-done((f32[128,128]{1,0:T(8,128)}, f32[128,128]{1,0:T(8,128)S(1)}, u32[]{:S(2)}, u32[]{:S(2)}) %collective-permute-start.23) | collective-permute-done | bytes 65568 | tf_op jit(solution)/shard_map/ppermute | solution.py:478
  75.3 0.6 collective-permute-start.29
  75.9 3.0 %collective-permute-start.31 = (f32[384,128]{1,0:T(8,128)}, f32[384,128]{1,0:T(8,128)S(1)}, u32[]{:S(2)}, u32[]{:S(2)}) collective-permute-start(f32[384,128]{1,0:T(8,128)} %bitcast.9), channel_id=1, source_target_pairs={{0,4},{1,5},{2,6},{3,7},{4,0},{5,1},{6,2},{7,3},{8,12},{9,13},{10,... | collective-permute-start | bytes 589832 | tf_op jit(solution)/shard_map/ppermute | solution.py:478
  79.0 0.6 copy-done.9
  79.6 3.9 %shard_map.163 = f32[512,128]{1,0:T(8,128)} custom-call(f32[128,128]{1,0:T(8,128)} %get-tuple-element.33.refs_0_.scalars_ref, f32[128,128]{1,0:T(8,128)} %copy-done.8, f32[128,128]{1,0:T(8,128)} %copy-done.5, f32[128,128]{1,0:T(8,128)} %copy-done.9, f32[128,128]{1,0:T(8,128)} %copy-done.6, f32[128,128]{1,0:T(8,128)} %copy-done.10, f32[128,128]{1,0:T(8,128)} %copy-done.7, ...), custom_call_target="tpu_custom_call" | custom-call | flops 402653184 | bytes 4000000 | tf_op jit(solution)/shard_map/pallas_call | solution.py:354
  83.4 0.7 collective-permute-start.25
  84.1 0.8 collective-permute-start.26
  84.9 2.0 %collective-permute-start.27 = (f32[512,128]{1,0:T(8,128)}, f32[512,128]{1,0:T(8,128)S(1)}, u32[]{:S(2)}, u32[]{:S(2)}) collective-permute-start(f32[512,128]{1,0:T(8,128)} %shard_map.163), channel_id=1, source_target_pairs={{0,24},{8,16},{16,8},{24,0},{1,25},{9,17},{17,9},{25,1},{2,26},{10... | collective-permute-start | bytes 786440 | tf_op jit(solution)/shard_map/ppermute | solution.py:478
  86.9 11.5 %shard_map.164 = (f32[384,128]{1,0:T(8,128)}, f32[7,128,256]{2,1,0:T(8,128)}) custom-call(s32[5,8]{1,0:T(8,128)} %shard_map.158.meta_ref, f32[128,128]{1,0:T(8,128)} %get-tuple-element.33.refs_0_.scalars_ref, f32[128,128]{1,0:T(8,128)} %copy-done.8, f32[128,128]{1,0:T(8,128)} %copy-done.5, f32[128,128]{1,0:T(8,128)} %copy-done.9, f32[128,128]{1,0:T(8,128)} %copy-done.6, ...), custom_call_target="tpu_custom_call" | custom-call | flops 12079595520 | bytes 10000000 | tf_op jit(solution)/shard_map/pallas_call | solution.py:271
  98.7 0.5 collective-permute-start.28
  99.2 0.1 collective-permute-start.30
  99.3 0.4 collective-permute-start.32
  99.7 6.4 %collective-permute-done.33.refs_5_ = f32[384,128]{1,0:T(8,128)S(1)} collective-permute-done((f32[384,128]{1,0:T(8,128)S(1)}, f32[384,128]{1,0:T(8,128)S(1)}, u32[]{:S(2)}, u32[]{:S(2)}) %collective-permute-start.33) | collective-permute-done | bytes 196640 | tf_op jit(solution)/shard_map/ppermute | solution.py:478
  106.1 1.4 %collective-permute-done.34.refs_6_ = f32[384,128]{1,0:T(8,128)S(1)} collective-permute-done((f32[384,128]{1,0:T(8,128)S(1)}, f32[384,128]{1,0:T(8,128)S(1)}, u32[]{:S(2)}, u32[]{:S(2)}) %collective-permute-start.34) | collective-permute-done | bytes 196640 | tf_op jit(solution)/shard_map/ppermute | solution.py:478
  107.6 0.6 copy-done.27
  108.2 0.1 copy-done.12
  108.3 12.4 %shard_map.165 = (f32[128,128]{1,0:T(8,128)}, f32[3,128,128]{2,1,0:T(8,128)}) custom-call(s32[5,8]{1,0:T(8,128)} %shard_map.158.meta_ref, s32[2]{0:T(128)} %pad_add_fusion.ids_ref.refs_0_, f32[128,128]{1,0:T(8,128)} %get-tuple-element.33.refs_0_.scalars_ref, f32[3,128,128]{2,1,0:T(8,128)} %get-tuple-element.34.vectors_ref, ...), custom_call_target="tpu_custom_call" | custom-call | flops 12079595520 | bytes 10000000 | tf_op jit(solution)/shard_map/pallas_call | solution.py:443
  (111 shorter events, 0.7 us)
Async XLA Ops:
  1.5 14.5 %copy-start.1 = (f32[136,128]{1,0:T(8,128)}, f32[136,128]{1,0:T(8,128)S(1)}, u32[]{:S(2)}) copy-start(f32[136,128]{1,0:T(8,128)S(1)} %select_maximum_fusion.place_ref.refs_2_.refs_10_.refs_0_.refs_8_) | copy-start | bytes 208900
  1.5 6.5 %collective-permute-start.1 = (f32[136,128]{1,0:T(8,128)S(1)}, f32[136,128]{1,0:T(8,128)S(1)}, u32[]{:S(2)}, u32[]{:S(2)}) collective-permute-start(f32[136,128]{1,0:T(8,128)S(1)} %select_maximum_fusion.place_ref.refs_2_.refs_10_.refs_0_.refs_8_), channel_id=1, source_target_pairs={{0,2},{1,3},{2,0},{3,1},{4,6},{5,7},{6,4},{7,5},{8,10},{9,11},{10,... | collective-permute-start | bytes 208904 | tf_op jit(solution)/shard_map/ppermute | solution.py:478
  4.5 7.5 %collective-permute-start.3 = (f32[136,128]{1,0:T(8,128)S(1)}, f32[136,128]{1,0:T(8,128)S(1)}, u32[]{:S(2)}, u32[]{:S(2)}) collective-permute-start(f32[136,128]{1,0:T(8,128)S(1)} %select_maximum_fusion.place_ref.refs_2_.refs_10_.refs_0_.refs_8_), channel_id=1, source_target_pairs={{0,4},{1,5},{2,6},{3,7},{4,0},{5,1},{6,2},{7,3},{8,12},{9,13},{10,... | collective-permute-start | bytes 208904 | tf_op jit(solution)/shard_map/ppermute | solution.py:478
  7.1 6.8 %collective-permute-start.5 = (f32[136,128]{1,0:T(8,128)S(1)}, f32[136,128]{1,0:T(8,128)S(1)}, u32[]{:S(2)}, u32[]{:S(2)}) collective-permute-start(f32[136,128]{1,0:T(8,128)S(1)} %select_maximum_fusion.place_ref.refs_2_.refs_10_.refs_0_.refs_8_), channel_id=1, source_target_pairs={{0,6},{1,7},{2,4},{3,5},{4,2},{5,3},{6,0},{7,1},{8,14},{9,15},{10,... | collective-permute-start | bytes 208904 | tf_op jit(solution)/shard_map/ppermute | solution.py:478
  7.1 12.5 %collective-permute-start = (f32[136,128]{1,0:T(8,128)S(1)}, f32[136,128]{1,0:T(8,128)S(1)}, u32[]{:S(2)}, u32[]{:S(2)}) collective-permute-start(f32[136,128]{1,0:T(8,128)S(1)} %select_maximum_fusion.place_ref.refs_2_.refs_10_.refs_0_.refs_8_), channel_id=1, source_target_pairs={{0,1},{1,0},{2,3},{3,2},{4,5},{5,4},{6,7},{7,6},{8,9},{9,8},{10,11... | collective-permute-start | bytes 208904 | tf_op jit(solution)/shard_map/ppermute | solution.py:478
  7.1 39.0 %collective-permute-start.11 = (f32[384,128]{1,0:T(8,128)}, f32[384,128]{1,0:T(8,128)S(1)}, u32[]{:S(2)}, u32[]{:S(2)}) collective-permute-start(f32[384,128]{1,0:T(8,128)} %bitcast.4), channel_id=1, source_target_pairs={{0,2},{1,3},{2,0},{3,1},{4,6},{5,7},{6,4},{7,5},{8,10},{9,11},{10,... | collective-permute-start | bytes 589832 | tf_op jit(solution)/shard_map/ppermute | solution.py:478
  8.0 12.8 %copy-start.30 = (f32[136,128]{1,0:T(8,128)}, f32[136,128]{1,0:T(8,128)S(1)}, u32[]{:S(2)}) copy-start(f32[136,128]{1,0:T(8,128)S(1)} %collective-permute-done.1.refs_4_.refs_12_.refs_2_.refs_10_) | copy-start | bytes 208900
  8.0 12.8 %collective-permute-start.2 = (f32[136,128]{1,0:T(8,128)S(1)}, f32[136,128]{1,0:T(8,128)S(1)}, u32[]{:S(2)}, u32[]{:S(2)}) collective-permute-start(f32[136,128]{1,0:T(8,128)S(1)} %collective-permute-done.1.refs_4_.refs_12_.refs_2_.refs_10_), channel_id=1, source_target_pairs={{0,1},{1,0},{2,3},{3,2},{4,5},{5,4},{6,7},{7,6},{8,9},{9,8},{10,11... | collective-permute-start | bytes 208904 | tf_op jit(solution)/shard_map/ppermute | solution.py:478
  12.1 8.8 %copy-start.31 = (f32[136,128]{1,0:T(8,128)}, f32[136,128]{1,0:T(8,128)S(1)}, u32[]{:S(2)}) copy-start(f32[136,128]{1,0:T(8,128)S(1)} %collective-permute-done.3.refs_6_.refs_14_.refs_4_.refs_12_) | copy-start | bytes 208900
  12.1 8.7 %collective-permute-start.4 = (f32[136,128]{1,0:T(8,128)S(1)}, f32[136,128]{1,0:T(8,128)S(1)}, u32[]{:S(2)}, u32[]{:S(2)}) collective-permute-start(f32[136,128]{1,0:T(8,128)S(1)} %collective-permute-done.3.refs_6_.refs_14_.refs_4_.refs_12_), channel_id=1, source_target_pairs={{0,1},{1,0},{2,3},{3,2},{4,5},{5,4},{6,7},{7,6},{8,9},{9,8},{10,11... | collective-permute-start | bytes 208904 | tf_op jit(solution)/shard_map/ppermute | solution.py:478
  13.9 6.9 %collective-permute-start.6 = (f32[136,128]{1,0:T(8,128)S(1)}, f32[136,128]{1,0:T(8,128)S(1)}, u32[]{:S(2)}, u32[]{:S(2)}) collective-permute-start(f32[136,128]{1,0:T(8,128)S(1)} %collective-permute-done.5.refs_8_.refs_16_.refs_6_.refs_14_), channel_id=1, source_target_pairs={{0,1},{1,0},{2,3},{3,2},{4,5},{5,4},{6,7},{7,6},{8,9},{9,8},{10,11... | collective-permute-start | bytes 208904 | tf_op jit(solution)/shard_map/ppermute | solution.py:478
  19.6 26.7 %collective-permute-start.13 = (f32[384,128]{1,0:T(8,128)}, f32[384,128]{1,0:T(8,128)S(1)}, u32[]{:S(2)}, u32[]{:S(2)}) collective-permute-start(f32[384,128]{1,0:T(8,128)} %bitcast.5), channel_id=1, source_target_pairs={{0,4},{1,5},{2,6},{3,7},{4,0},{5,1},{6,2},{7,3},{8,12},{9,13},{10,... | collective-permute-start | bytes 589832 | tf_op jit(solution)/shard_map/ppermute | solution.py:478
  26.7 18.7 %copy-start.14 = (f32[3,128,128]{2,1,0:T(8,128)S(1)}, f32[3,128,128]{2,1,0:T(8,128)}, u32[]{:S(2)}) copy-start(f32[3,128,128]{2,1,0:T(8,128)} %vectors_ref.1) | copy-start | bytes 589828
  26.7 18.8 %copy-start.4 = (f32[512,128]{1,0:T(8,128)S(1)}, f32[512,128]{1,0:T(8,128)}, u32[]{:S(2)}) copy-start(f32[512,128]{1,0:T(8,128)} %get-tuple-element.24) | copy-start | bytes 786436
  26.7 18.7 %collective-permute-start.7 = (f32[512,128]{1,0:T(8,128)}, f32[512,128]{1,0:T(8,128)S(1)}, u32[]{:S(2)}, u32[]{:S(2)}) collective-permute-start(f32[512,128]{1,0:T(8,128)} %get-tuple-element.24), channel_id=1, source_target_pairs={{0,8},{8,0},{16,24},{24,16},{1,9},{9,1},{17,25},{25,17},{2,10},{10... | collective-permute-start | bytes 786440 | tf_op jit(solution)/shard_map/ppermute | solution.py:478
  28.3 17.2 %collective-permute-start.8 = (f32[512,128]{1,0:T(8,128)}, f32[512,128]{1,0:T(8,128)S(1)}, u32[]{:S(2)}, u32[]{:S(2)}) collective-permute-start(f32[512,128]{1,0:T(8,128)} %get-tuple-element.24), channel_id=1, source_target_pairs={{0,16},{8,24},{16,0},{24,8},{1,17},{9,25},{17,1},{25,9},{2,18},{10... | collective-permute-start | bytes 786440 | tf_op jit(solution)/shard_map/ppermute | solution.py:478
  29.8 15.7 %collective-permute-start.9 = (f32[512,128]{1,0:T(8,128)}, f32[512,128]{1,0:T(8,128)S(1)}, u32[]{:S(2)}, u32[]{:S(2)}) collective-permute-start(f32[512,128]{1,0:T(8,128)} %get-tuple-element.24), channel_id=1, source_target_pairs={{0,24},{8,16},{16,8},{24,0},{1,25},{9,17},{17,9},{25,1},{2,26},{10... | collective-permute-start | bytes 786440 | tf_op jit(solution)/shard_map/ppermute | solution.py:478
  45.4 7.5 %collective-permute-start.15 = (f32[384,128]{1,0:T(8,128)S(1)}, f32[384,128]{1,0:T(8,128)S(1)}, u32[]{:S(2)}, u32[]{:S(2)}) collective-permute-start(f32[384,128]{1,0:T(8,128)S(1)} %bitcast.6), channel_id=1, source_target_pairs={{0,6},{1,7},{2,4},{3,5},{4,2},{5,3},{6,0},{7,1},{8,14},{9,15},{10,... | collective-permute-start | bytes 589832 | tf_op jit(solution)/shard_map/ppermute | solution.py:478
  45.6 8.8 %copy-start.3 = (f32[512,128]{1,0:T(8,128)}, f32[512,128]{1,0:T(8,128)S(1)}, u32[]{:S(2)}) copy-start(f32[512,128]{1,0:T(8,128)S(1)} %add_add_fusion.1.refs_7_) | copy-start | bytes 786436
  45.6 8.8 %collective-permute-start.17 = (f32[512,128]{1,0:T(8,128)S(1)}, f32[512,128]{1,0:T(8,128)S(1)}, u32[]{:S(2)}, u32[]{:S(2)}) collective-permute-start(f32[512,128]{1,0:T(8,128)S(1)} %add_add_fusion.1.refs_7_), channel_id=1, source_target_pairs={{0,1},{1,0},{2,3},{3,2},{4,5},{5,4},{6,7},{7,6},{8,9},{9,8},{10,11... | collective-permute-start | bytes 786440 | tf_op jit(solution)/shard_map/ppermute | solution.py:478
  45.7 7.3 %collective-permute-start.10 = (f32[384,128]{1,0:T(8,128)S(1)}, f32[384,128]{1,0:T(8,128)S(1)}, u32[]{:S(2)}, u32[]{:S(2)}) collective-permute-start(f32[384,128]{1,0:T(8,128)S(1)} %bitcast.7), channel_id=1, source_target_pairs={{0,1},{1,0},{2,3},{3,2},{4,5},{5,4},{6,7},{7,6},{8,9},{9,8},{10,11... | collective-permute-start | bytes 589832 | tf_op jit(solution)/shard_map/ppermute | solution.py:478
  46.2 8.2 %copy-start.16 = (f32[384,128]{1,0:T(8,128)}, f32[384,128]{1,0:T(8,128)S(1)}, u32[]{:S(2)}) copy-start(f32[384,128]{1,0:T(8,128)S(1)} %collective-permute-done.11.refs_1_) | copy-start | bytes 589828
  46.2 6.8 %collective-permute-start.12 = (f32[384,128]{1,0:T(8,128)S(1)}, f32[384,128]{1,0:T(8,128)S(1)}, u32[]{:S(2)}, u32[]{:S(2)}) collective-permute-start(f32[384,128]{1,0:T(8,128)S(1)} %collective-permute-done.11.refs_1_), channel_id=1, source_target_pairs={{0,1},{1,0},{2,3},{3,2},{4,5},{5,4},{6,7},{7,6},{8,9},{9,8},{10,11... | collective-permute-start | bytes 589832 | tf_op jit(solution)/shard_map/ppermute | solution.py:478
  46.3 6.7 %collective-permute-start.14 = (f32[384,128]{1,0:T(8,128)S(1)}, f32[384,128]{1,0:T(8,128)S(1)}, u32[]{:S(2)}, u32[]{:S(2)}) collective-permute-start(f32[384,128]{1,0:T(8,128)S(1)} %collective-permute-done.13.refs_3_), channel_id=1, source_target_pairs={{0,1},{1,0},{2,3},{3,2},{4,5},{5,4},{6,7},{7,6},{8,9},{9,8},{10,11... | collective-permute-start | bytes 589832 | tf_op jit(solution)/shard_map/ppermute | solution.py:478
  53.0 1.4 %collective-permute-start.16 = (f32[384,128]{1,0:T(8,128)S(1)}, f32[384,128]{1,0:T(8,128)S(1)}, u32[]{:S(2)}, u32[]{:S(2)}) collective-permute-start(f32[384,128]{1,0:T(8,128)S(1)} %collective-permute-done.15.refs_5_), channel_id=1, source_target_pairs={{0,1},{1,0},{2,3},{3,2},{4,5},{5,4},{6,7},{7,6},{8,9},{9,8},{10,11... | collective-permute-start | bytes 589832 | tf_op jit(solution)/shard_map/ppermute | solution.py:478
  67.6 5.8 %collective-permute-start.19 = (f32[128,128]{1,0:T(8,128)}, f32[128,128]{1,0:T(8,128)S(1)}, u32[]{:S(2)}, u32[]{:S(2)}) collective-permute-start(f32[128,128]{1,0:T(8,128)} %get-tuple-element.33.refs_0_.scalars_ref), channel_id=1, source_target_pairs={{0,2},{1,3},{2,0},{3,1},{4,6},{5,7},{6,4},{7,5},{8,10},{9,11},{10,... | collective-permute-start | bytes 196616 | tf_op jit(solution)/shard_map/ppermute | solution.py:478
  67.7 5.8 %collective-permute-start.21 = (f32[128,128]{1,0:T(8,128)}, f32[128,128]{1,0:T(8,128)S(1)}, u32[]{:S(2)}, u32[]{:S(2)}) collective-permute-start(f32[128,128]{1,0:T(8,128)} %get-tuple-element.33.refs_0_.scalars_ref), channel_id=1, source_target_pairs={{0,4},{1,5},{2,6},{3,7},{4,0},{5,1},{6,2},{7,3},{8,12},{9,13},{10,... | collective-permute-start | bytes 196616 | tf_op jit(solution)/shard_map/ppermute | solution.py:478
  67.7 7.6 %collective-permute-start.23 = (f32[128,128]{1,0:T(8,128)}, f32[128,128]{1,0:T(8,128)S(1)}, u32[]{:S(2)}, u32[]{:S(2)}) collective-permute-start(f32[128,128]{1,0:T(8,128)} %get-tuple-element.33.refs_0_.scalars_ref), channel_id=1, source_target_pairs={{0,6},{1,7},{2,4},{3,5},{4,2},{5,3},{6,0},{7,1},{8,14},{9,15},{10,... | collective-permute-start | bytes 196616 | tf_op jit(solution)/shard_map/ppermute | solution.py:478
  72.0 3.8 %collective-permute-start.18 = (f32[128,128]{1,0:T(8,128)}, f32[128,128]{1,0:T(8,128)S(1)}, u32[]{:S(2)}, u32[]{:S(2)}) collective-permute-start(f32[128,128]{1,0:T(8,128)} %get-tuple-element.33.refs_0_.scalars_ref), channel_id=1, source_target_pairs={{0,1},{1,0},{2,3},{3,2},{4,5},{5,4},{6,7},{7,6},{8,9},{9,8},{10,11... | collective-permute-start | bytes 196616 | tf_op jit(solution)/shard_map/ppermute | solution.py:478
  73.4 5.5 %collective-permute-start.20 = (f32[128,128]{1,0:T(8,128)S(1)}, f32[128,128]{1,0:T(8,128)S(1)}, u32[]{:S(2)}, u32[]{:S(2)}) collective-permute-start(f32[128,128]{1,0:T(8,128)S(1)} %collective-permute-done.19.refs_2_), channel_id=1, source_target_pairs={{0,1},{1,0},{2,3},{3,2},{4,5},{5,4},{6,7},{7,6},{8,9},{9,8},{10,11... | collective-permute-start | bytes 196616 | tf_op jit(solution)/shard_map/ppermute | solution.py:478
  73.4 5.4 %collective-permute-start.22 = (f32[128,128]{1,0:T(8,128)S(1)}, f32[128,128]{1,0:T(8,128)S(1)}, u32[]{:S(2)}, u32[]{:S(2)}) collective-permute-start(f32[128,128]{1,0:T(8,128)S(1)} %collective-permute-done.21.refs_4_), channel_id=1, source_target_pairs={{0,1},{1,0},{2,3},{3,2},{4,5},{5,4},{6,7},{7,6},{8,9},{9,8},{10,11... | collective-permute-start | bytes 196616 | tf_op jit(solution)/shard_map/ppermute | solution.py:478
  75.3 3.6 %collective-permute-start.24 = (f32[128,128]{1,0:T(8,128)S(1)}, f32[128,128]{1,0:T(8,128)S(1)}, u32[]{:S(2)}, u32[]{:S(2)}) collective-permute-start(f32[128,128]{1,0:T(8,128)S(1)} %collective-permute-done.23.refs_6_), channel_id=1, source_target_pairs={{0,1},{1,0},{2,3},{3,2},{4,5},{5,4},{6,7},{7,6},{8,9},{9,8},{10,11... | collective-permute-start | bytes 196616 | tf_op jit(solution)/shard_map/ppermute | solution.py:478
  75.3 23.9 %collective-permute-start.29 = (f32[384,128]{1,0:T(8,128)}, f32[384,128]{1,0:T(8,128)S(1)}, u32[]{:S(2)}, u32[]{:S(2)}) collective-permute-start(f32[384,128]{1,0:T(8,128)} %bitcast.8), channel_id=1, source_target_pairs={{0,2},{1,3},{2,0},{3,1},{4,6},{5,7},{6,4},{7,5},{8,10},{9,11},{10,... | collective-permute-start | bytes 589832 | tf_op jit(solution)/shard_map/ppermute | solution.py:478
  75.9 23.4 %collective-permute-start.31 = (f32[384,128]{1,0:T(8,128)}, f32[384,128]{1,0:T(8,128)S(1)}, u32[]{:S(2)}, u32[]{:S(2)}) collective-permute-start(f32[384,128]{1,0:T(8,128)} %bitcast.9), channel_id=1, source_target_pairs={{0,4},{1,5},{2,6},{3,7},{4,0},{5,1},{6,2},{7,3},{8,12},{9,13},{10,... | collective-permute-start | bytes 589832 | tf_op jit(solution)/shard_map/ppermute | solution.py:478
  83.4 15.0 %collective-permute-start.25 = (f32[512,128]{1,0:T(8,128)}, f32[512,128]{1,0:T(8,128)S(1)}, u32[]{:S(2)}, u32[]{:S(2)}) collective-permute-start(f32[512,128]{1,0:T(8,128)} %shard_map.163), channel_id=1, source_target_pairs={{0,8},{8,0},{16,24},{24,16},{1,9},{9,1},{17,25},{25,17},{2,10},{10... | collective-permute-start | bytes 786440 | tf_op jit(solution)/shard_map/ppermute | solution.py:478
  84.1 14.4 %collective-permute-start.26 = (f32[512,128]{1,0:T(8,128)}, f32[512,128]{1,0:T(8,128)S(1)}, u32[]{:S(2)}, u32[]{:S(2)}) collective-permute-start(f32[512,128]{1,0:T(8,128)} %shard_map.163), channel_id=1, source_target_pairs={{0,16},{8,24},{16,0},{24,8},{1,17},{9,25},{17,1},{25,9},{2,18},{10... | collective-permute-start | bytes 786440 | tf_op jit(solution)/shard_map/ppermute | solution.py:478
  84.9 13.6 %collective-permute-start.27 = (f32[512,128]{1,0:T(8,128)}, f32[512,128]{1,0:T(8,128)S(1)}, u32[]{:S(2)}, u32[]{:S(2)}) collective-permute-start(f32[512,128]{1,0:T(8,128)} %shard_map.163), channel_id=1, source_target_pairs={{0,24},{8,16},{16,8},{24,0},{1,25},{9,17},{17,9},{25,1},{2,26},{10... | collective-permute-start | bytes 786440 | tf_op jit(solution)/shard_map/ppermute | solution.py:478
  86.9 11.5 %copy-start.15 = (f32[3,128,128]{2,1,0:T(8,128)S(1)}, f32[3,128,128]{2,1,0:T(8,128)}, u32[]{:S(2)}) copy-start(f32[3,128,128]{2,1,0:T(8,128)} %get-tuple-element.34.vectors_ref) | copy-start | bytes 589828
  86.9 11.6 %copy-start = (f32[512,128]{1,0:T(8,128)S(1)}, f32[512,128]{1,0:T(8,128)}, u32[]{:S(2)}) copy-start(f32[512,128]{1,0:T(8,128)} %shard_map.163) | copy-start | bytes 786436
  98.4 7.6 %collective-permute-start.33 = (f32[384,128]{1,0:T(8,128)S(1)}, f32[384,128]{1,0:T(8,128)S(1)}, u32[]{:S(2)}, u32[]{:S(2)}) collective-permute-start(f32[384,128]{1,0:T(8,128)S(1)} %bitcast.10), channel_id=1, source_target_pairs={{0,6},{1,7},{2,4},{3,5},{4,2},{5,3},{6,0},{7,1},{8,14},{9,15},{10,... | collective-permute-start | bytes 589832 | tf_op jit(solution)/shard_map/ppermute | solution.py:478
  98.6 8.9 %copy-start.2 = (f32[512,128]{1,0:T(8,128)}, f32[512,128]{1,0:T(8,128)S(1)}, u32[]{:S(2)}) copy-start(f32[512,128]{1,0:T(8,128)S(1)} %add_add_fusion.refs_7_) | copy-start | bytes 786436
  98.6 8.9 %collective-permute-start.35 = (f32[512,128]{1,0:T(8,128)S(1)}, f32[512,128]{1,0:T(8,128)S(1)}, u32[]{:S(2)}, u32[]{:S(2)}) collective-permute-start(f32[512,128]{1,0:T(8,128)S(1)} %add_add_fusion.refs_7_), channel_id=1, source_target_pairs={{0,1},{1,0},{2,3},{3,2},{4,5},{5,4},{6,7},{7,6},{8,9},{9,8},{10,11... | collective-permute-start | bytes 786440 | tf_op jit(solution)/shard_map/ppermute | solution.py:478
  98.7 7.4 %collective-permute-start.28 = (f32[384,128]{1,0:T(8,128)S(1)}, f32[384,128]{1,0:T(8,128)S(1)}, u32[]{:S(2)}, u32[]{:S(2)}) collective-permute-start(f32[384,128]{1,0:T(8,128)S(1)} %bitcast.11), channel_id=1, source_target_pairs={{0,1},{1,0},{2,3},{3,2},{4,5},{5,4},{6,7},{7,6},{8,9},{9,8},{10,11... | collective-permute-start | bytes 589832 | tf_op jit(solution)/shard_map/ppermute | solution.py:478
  99.2 8.3 %copy-start.17 = (f32[384,128]{1,0:T(8,128)}, f32[384,128]{1,0:T(8,128)S(1)}, u32[]{:S(2)}) copy-start(f32[384,128]{1,0:T(8,128)S(1)} %collective-permute-done.29.refs_1_) | copy-start | bytes 589828
  99.2 6.9 %collective-permute-start.30 = (f32[384,128]{1,0:T(8,128)S(1)}, f32[384,128]{1,0:T(8,128)S(1)}, u32[]{:S(2)}, u32[]{:S(2)}) collective-permute-start(f32[384,128]{1,0:T(8,128)S(1)} %collective-permute-done.29.refs_1_), channel_id=1, source_target_pairs={{0,1},{1,0},{2,3},{3,2},{4,5},{5,4},{6,7},{7,6},{8,9},{9,8},{10,11... | collective-permute-start | bytes 589832 | tf_op jit(solution)/shard_map/ppermute | solution.py:478
  99.3 8.3 %copy-start.18 = (f32[384,128]{1,0:T(8,128)}, f32[384,128]{1,0:T(8,128)S(1)}, u32[]{:S(2)}) copy-start(f32[384,128]{1,0:T(8,128)S(1)} %collective-permute-done.31.refs_3_) | copy-start | bytes 589828
  99.3 6.8 %collective-permute-start.32 = (f32[384,128]{1,0:T(8,128)S(1)}, f32[384,128]{1,0:T(8,128)S(1)}, u32[]{:S(2)}, u32[]{:S(2)}) collective-permute-start(f32[384,128]{1,0:T(8,128)S(1)} %collective-permute-done.31.refs_3_), channel_id=1, source_target_pairs={{0,1},{1,0},{2,3},{3,2},{4,5},{5,4},{6,7},{7,6},{8,9},{9,8},{10,11... | collective-permute-start | bytes 589832 | tf_op jit(solution)/shard_map/ppermute | solution.py:478
  106.1 1.4 %collective-permute-start.34 = (f32[384,128]{1,0:T(8,128)S(1)}, f32[384,128]{1,0:T(8,128)S(1)}, u32[]{:S(2)}, u32[]{:S(2)}) collective-permute-start(f32[384,128]{1,0:T(8,128)S(1)} %collective-permute-done.33.refs_5_), channel_id=1, source_target_pairs={{0,1},{1,0},{2,3},{3,2},{4,5},{5,4},{6,7},{7,6},{8,9},{9,8},{10,11... | collective-permute-start | bytes 589832 | tf_op jit(solution)/shard_map/ppermute | solution.py:478
  (25 other events, 52.6 us)

commit v2 on v1

v2 whole, which is shorter than its diff:
```python
import functools
import math

import jax
import jax.numpy as jnp
import numpy as np
from jax import lax
from jax.experimental import pallas as pl
from jax.experimental.pallas import tpu as pltpu
from jax.sharding import PartitionSpec as P

NRBF = 20
BS = 128
KW = 512
LAYERS = 2
BITS = 30
CUTOFF = 8.0
SPACING = CUTOFF / (NRBF - 1)
CENTER = 0.5 * CUTOFF
VMEM = 44 * 1024 * 1024
WINDOW = 1e10
F32 = jnp.float32
BF16 = jnp.bfloat16


def split(x):
    high = x.astype(BF16)
    return high, (x - high.astype(F32)).astype(BF16)


def wide_left(x):
    high, low = split(x)
    return jnp.concatenate([high, low, high], axis=1)


def wide_right(x):
    high, low = split(x)
    return jnp.concatenate([high, high, low], axis=0)


def stacked(x):
    high, low = split(x)
    return jnp.concatenate([high, high], axis=0), low


def dot(a, b):
    return jnp.dot(a, b, preferred_element_type=F32)


def dot3(a, b):
    return dot(wide_left(a), wide_right(b))


def silu(x):
    return x / (1.0 + jnp.exp(-x))


def turn_fits():
    nodes = 0.5 * np.cos(np.pi * (np.arange(400) + 0.5) / 400)
    cheb = np.polynomial.chebyshev
    fit_cos = cheb.Chebyshev.fit(nodes * nodes, np.cos(2 * np.pi * nodes), 7, domain=[0, 0.25])
    fit_sin = cheb.Chebyshev.fit(nodes * nodes, np.sinc(2 * nodes) * 2 * np.pi, 7, domain=[0, 0.25])
    to_poly = lambda fit: [float(c) for c in fit.convert(kind=np.polynomial.Polynomial).coef]
    return to_poly(fit_cos), to_poly(fit_sin)


COS_FIT, SIN_FIT = turn_fits()


def horner(coefs, x):
    total = jnp.full_like(x, coefs[-1])
    for c in coefs[-2::-1]:
        total = total * x + c
    return total


def cos_sin(turns):
    rest = turns - jnp.round(turns)
    square = rest * rest
    return horner(COS_FIT, square), horner(SIN_FIT, square) * rest


def columns_of(pos):
    return jnp.transpose(pos)


def cost(flops, moved, exps=0):
    return pl.CostEstimate(flops=int(flops), bytes_accessed=int(moved), transcendentals=int(exps))


SMEM_SPEC = pl.BlockSpec(memory_space=pltpu.SMEM)
VMEM_SPEC = pl.BlockSpec(memory_space=pltpu.VMEM)
HBM_SPEC = pl.BlockSpec(memory_space=pltpu.HBM)


def meta_kernel(n_sub, per_region, slots, ids_ref, pairs_ref, meta_ref):
    region, sub = ids_ref[0], ids_ref[1]
    base = region * per_region
    for row in range(5):
        for slot in range(slots):
            meta_ref[row, slot] = lax.rem(sub, 2) if row == 4 else 0

    def visit(p, found):
        first = pairs_ref[0, base + p] - region * n_sub
        second = pairs_ref[1, base + p] - region * n_sub
        hit = (first == sub) | (second == sub)

        @pl.when(hit & (found < slots))
        def _():
            other = jnp.where(first == sub, second, first)
            meta_ref[1, found] = base + p
            meta_ref[2, found] = other ^ sub
            meta_ref[3, found] = (first == sub).astype(jnp.int32)

        return found + hit.astype(jnp.int32)

    meta_ref[0, 0] = lax.fori_loop(0, per_region, visit, jnp.int32(0))


def find_pairs(ids, pair_blocks, n_sub, per_region, slots):
    return pl.pallas_call(
        functools.partial(meta_kernel, n_sub, per_region, slots),
        in_specs=[SMEM_SPEC, SMEM_SPEC],
        out_specs=SMEM_SPEC,
        out_shape=jax.ShapeDtypeStruct((5, slots), jnp.int32),
    )(ids, pair_blocks)


def near_dots(tables, rows, sources):
    number = len(sources)
    values = [tables[i, rows, :] for i in range(number)]
    highs = [v[:, :BS] for v in values]
    both = [b for b, _ in sources]
    low = [l for _, l in sources]
    return dot(jnp.concatenate(values, axis=1), jnp.concatenate(both, axis=0)) + dot(
        jnp.concatenate(highs, axis=1), jnp.concatenate(low, axis=0)
    )


def add_terms(totals, cols, tables, sources, weight):
    group = 4
    total = totals[:, cols]
    for k in range(0, NRBF, group):
        product = near_dots(tables, slice(k * BS, (k + group) * BS), sources)
        for g in range(group):
            total = total + product[g * BS : (g + 1) * BS] * weight[k + g : k + g + 1]
    totals[:, cols] = total


def one_or_two(step, count, act):
    for number in (1, 2):
        here = (2 * step + 1 == count) if number == 1 else (2 * step + 1 < count)
        pl.when(here)(functools.partial(act, number))


def table_copy(table, step, buffer, sems):
    slot = lax.rem(step, 2)
    return pltpu.make_async_copy(table.at[pl.ds(2 * step, 2)], buffer.at[slot], sems.at[slot])


def over_tables(count, table, buffer, sems, act):
    steps = (count + 1) // 2

    def one(step, carry):
        @pl.when(step + 1 < steps)
        def _():
            table_copy(table, step + 1, buffer, sems).start()

        table_copy(table, step, buffer, sems).wait()
        act(step, buffer.at[lax.rem(step, 2)])
        return carry

    lax.fori_loop(0, steps, one, 0)


def fill_tables(count, tables, act):
    steps = (count + 1) // 2

    def out(step, table, buffer, sems):
        slot = lax.rem(step, 2)
        return pltpu.make_async_copy(buffer.at[slot], table.at[pl.ds(2 * step, 2)], sems.at[slot])

    def one(step, carry):
        @pl.when(step >= 2)
        def _():
            for t in tables:
                out(step - 2, *t).wait()

        act(step, [buffer.at[lax.rem(step, 2)] for _, buffer, _ in tables])
        for t in tables:
            out(step, *t).start()
        return carry

    lax.fori_loop(0, steps, one, 0)
    for back in (2, 1):

        @pl.when(steps >= back)
        def _():
            for t in tables:
                out(steps - back, *t).wait()


def radial_tables(meta_ref, listed, at, near, pos_ref, masks_ref, radial_ref, over_ref):
    pair = meta_ref[1, listed]
    slot = meta_ref[2, listed]
    is_first = meta_ref[3, listed]
    words = masks_ref[pl.ds(pair, 1), :]
    tiles = -(-words.shape[1] // BS)
    rest = tiles * BS - words.shape[1]
    if rest:
        words = jnp.concatenate([words, jnp.zeros((1, rest), jnp.int32)], axis=1)
    row = lax.broadcasted_iota(jnp.int32, (BS, BS), 0)
    row_tile = (row * 2185) >> 16
    spread = jnp.zeros((BS, BS), jnp.int32)
    for tile in range(tiles):
        spread = jnp.where(
            row_tile == tile,
            jnp.broadcast_to(words[:, tile * BS : (tile + 1) * BS], (BS, BS)),
            spread,
        )
    spot = (row - row_tile * BITS) * BS + lax.broadcasted_iota(jnp.int32, (BS, BS), 1)
    index = (spot * 34953) >> 20
    picked = jnp.take_along_axis(spread, index, axis=1)
    mask = (jnp.right_shift(picked, spot - index * BITS) & 1).astype(F32)
    mask = jnp.where(is_first == 1, mask, jnp.transpose(mask))
    source = jnp.zeros((8, BS), F32)
    for e in range(1, len(near)):
        source = jnp.where(slot == e, near[e][...], source)
    mine = columns_of(pos_ref[...])
    square = jnp.zeros((BS, BS), F32)
    for d in range(3):
        offset = source[d : d + 1, :] - mine[:, d : d + 1]
        square = square + offset * offset
    distance = jnp.sqrt(square + 1.0)
    inverse = 1.0 / distance
    root = math.sqrt(0.5 * math.log2(math.e))
    scaled = jnp.where(mask > 0.5, distance * (root / SPACING), 1.0e4)
    for k in range(NRBF):
        gap = scaled - k * root
        radial = jnp.exp2(-(gap * gap))
        rows = slice(k * BS, (k + 1) * BS)
        for ref, value in ((radial_ref, radial), (over_ref, radial * inverse)):
            high, low = split(value)
            ref[at, rows, 0:BS] = high
            ref[at, rows, BS : 2 * BS] = low


def early_kernel(n_sub, build, layer, meta_ref, *refs):
    blocks, refs = [r.at[:BS, :] for r in refs[:n_sub]], refs[n_sub:]
    places, refs = [r.at[r.shape[0] - 8 :, :] for r in refs[:n_sub]], refs[n_sub:]
    if build:
        in_ref, out_ref, filter_ref, masks_ref, partial_ref, phi_ref, tables_hbm = refs[:7]
        sources, totals, over_buffer, over_sems, radial_buffer, radial_sems = refs[7:]
    else:
        in_ref, out_ref, filter_ref, tables_hbm, partial_ref, phi_ref, sources, totals, over_buffer, over_sems = refs
    radial_hbm, over_hbm = tables_hbm.at[0], tables_hbm.at[1]
    count = meta_ref[0, 0]
    if not build:

        @pl.when(count > 0)
        def _():
            table_copy(over_hbm, 0, over_buffer, over_sems).start()

    totals[...] = jnp.zeros_like(totals)
    scalars = jnp.concatenate([blocks[e][...] for e in range(1, n_sub)], axis=0)
    hidden = silu(dot3(scalars, in_ref[layer]))
    phi = dot3(hidden, out_ref[layer])
    for e in range(1, n_sub):
        rows = phi[(e - 1) * BS : e * BS]
        phi_ref[e - 1] = rows[:, : 2 * BS]
        phi_r = rows[:, 2 * BS :]
        place = columns_of(places[e][...])
        parts = [phi_r] + [phi_r * (place[:, d : d + 1] - CENTER) for d in range(3)]
        for at, part in enumerate(parts):
            high, low = split(part)
            cols = slice(at * BS, (at + 1) * BS)
            sources[e - 1, 0:BS, cols] = high
            sources[e - 1, BS : 2 * BS, cols] = high
            sources[e - 1, 2 * BS :, cols] = low

    weight = filter_ref[layer, :, 2 * BS :]
    weight = jnp.concatenate([weight, weight], axis=1)

    def terms(step, table, number):
        slot = [meta_ref[2, 2 * step + i] - 1 for i in range(number)]
        for tile in range(2):
            cols = slice(tile * 2 * BS, (tile + 1) * 2 * BS)
            near = [(sources[e, : 2 * BS, cols], sources[e, 2 * BS :, cols]) for e in slot]
            add_terms(totals, cols, table, near, weight)

    if build:

        def act(step, tables):
            radial, over = tables

            def both(number):
                for i in range(number):
                    radial_tables(meta_ref, 2 * step + i, i, places, places[0], masks_ref, radial, over)
                terms(step, over, number)

            one_or_two(step, count, both)

        fill_tables(
            count, ((radial_hbm, radial_buffer, radial_sems), (over_hbm, over_buffer, over_sems)), act
        )
    else:

        def act(step, table):
            one_or_two(step, count, functools.partial(terms, step, table))

        over_tables(count, over_hbm, over_buffer, over_sems, act)

    mine = columns_of(places[0][...])
    for d in range(3):
        partial_ref[d * BS : (d + 1) * BS, :] = (
            totals[:, (1 + d) * BS : (2 + d) * BS] - (mine[:, d : d + 1] - CENTER) * totals[:, :BS]
        )


def table_buffers(number):
    return [pltpu.VMEM((2, 2, NRBF * BS, 2 * BS), BF16), pltpu.SemaphoreType.DMA((2,))] * number


def early_terms(meta, layer, blocks, spots, weights, masks=None, tables=None):
    n_sub = len(blocks)
    slots = meta.shape[1]
    build = tables is None
    shape = jax.ShapeDtypeStruct((2, slots, NRBF * BS, 2 * BS), BF16)
    out_shape = [
        jax.ShapeDtypeStruct((3 * BS, BS), F32),
        jax.ShapeDtypeStruct((n_sub - 1, BS, 2 * BS), F32),
    ]
    return pl.pallas_call(
        functools.partial(early_kernel, n_sub, build, layer),
        in_specs=[SMEM_SPEC] + [VMEM_SPEC] * (2 * n_sub + 3) + [VMEM_SPEC if build else HBM_SPEC],
        out_specs=[VMEM_SPEC] * 2 + ([HBM_SPEC] if build else []),
        scratch_shapes=[
            pltpu.VMEM((n_sub - 1, 3 * BS, 4 * BS), BF16),
            pltpu.VMEM((BS, 4 * BS), F32),
        ]
        + table_buffers(2 if build else 1),
        out_shape=out_shape + ([shape] if build else []),
        compiler_params=pltpu.CompilerParams(vmem_limit_bytes=VMEM),
        cost_estimate=cost(3 * 4 * NRBF * BS * BS * 4 * BS * 2 * 3, 10e6),
    )(meta, *blocks, *spots, *weights, masks if build else tables)


def own_trig_kernel(waves_ref, place_ref, own_ref):
    waves = waves_ref[...] * (1.0 / (2.0 * math.pi))
    mine = columns_of(place_ref[BS:, :])
    turns = jnp.zeros((BS, waves.shape[1]), F32)
    for d in range(3):
        turns = turns + mine[:, d : d + 1] * waves[d : d + 1, :]
    own_ref[...] = jnp.concatenate(split(jnp.concatenate(cos_sin(turns), axis=1)), axis=1)


def own_trig_of(waves, spot):
    return pl.pallas_call(
        own_trig_kernel,
        in_specs=[VMEM_SPEC] * 2,
        out_specs=VMEM_SPEC,
        out_shape=jax.ShapeDtypeStruct((BS, 4 * KW), BF16),
        compiler_params=pltpu.CompilerParams(vmem_limit_bytes=VMEM),
        cost_estimate=cost(WINDOW, 1e6),
    )(waves, spot)


def structure_kernel(n_sub, build, layer, *refs):
    if build:
        meta_ref, waves_ref, refs = refs[0], refs[1], refs[2:]
        places = [r.at[r.shape[0] - 8 :, :] for r in refs[:n_sub]]
    blocks, refs = [r.at[:BS, :] for r in refs[:n_sub]], refs[n_sub:]
    atoms = n_sub * BS
    if build:
        weight_ref, out_ref, trig_ref = refs
        waves = waves_ref[...] * (1.0 / (2.0 * math.pi))
        rows = waves.shape[1] // 2
        waves = jnp.where(meta_ref[4, 0] == 0, waves[:, :rows], waves[:, rows:])
        half = jnp.transpose(jnp.concatenate([waves, jnp.zeros((5, rows), F32)], axis=0))
        for e in range(n_sub):
            place = places[e][...]
            turns = jnp.zeros((rows, BS), F32)
            for d in range(3):
                turns = turns + half[:, d : d + 1] * place[d : d + 1, :]
            for at, value in enumerate(cos_sin(turns)):
                block = slice(at * rows, (at + 1) * rows)
                for part, piece in enumerate(split(value)):
                    trig_ref[block, part * atoms + e * BS : part * atoms + (e + 1) * BS] = piece
    else:
        weight_ref, trig_ref, out_ref = refs
    both, low = stacked(jnp.concatenate([blocks[e][...] for e in range(n_sub)], axis=0))
    total = dot(trig_ref[...], both) + dot(trig_ref[:, :atoms], low)
    out_ref[...] = dot3(total, weight_ref[layer])


def structure(layer, blocks, weight, meta=None, waves=None, region_trig=None):
    n_sub = len(blocks)
    build = region_trig is None
    out_shape = [jax.ShapeDtypeStruct((KW, BS), F32)]
    if build:
        in_specs = [SMEM_SPEC] + [VMEM_SPEC] * (n_sub + 2)
        operands = (meta, waves, *blocks, weight)
        out_shape += [jax.ShapeDtypeStruct((KW, 2 * n_sub * BS), BF16)]
    else:
        in_specs = [VMEM_SPEC] * (n_sub + 2)
        operands = (*blocks, weight, region_trig)
    return pl.pallas_call(
        functools.partial(structure_kernel, n_sub, build, layer),
        in_specs=in_specs,
        out_specs=[VMEM_SPEC] * len(out_shape),
        out_shape=out_shape,
        compiler_params=pltpu.CompilerParams(vmem_limit_bytes=VMEM),
        cost_estimate=cost(KW * n_sub * BS * BS * 6, 4e6),
    )(*operands)


def late_kernel(scale, n_sub, layer, last, meta_ref, *refs):
    scalars_ref, vectors_ref, phi_ref, partial_ref, mine_ref, other_ref, own_ref = refs[:7]
    factor_ref, filter_ref, left_ref, right_ref, gate_in_ref, gate_out_ref = refs[7:13]
    near, refs = refs[13 : 12 + n_sub], refs[12 + n_sub :]
    radial_hbm, refs = refs[0].at[0], refs[1:]
    outs, (totals, buffer, sems) = refs[:-3], refs[-3:]
    count = meta_ref[0, 0]

    @pl.when(count > 0)
    def _():
        table_copy(radial_hbm, 0, buffer, sems).start()

    totals[:, :BS] = jnp.zeros((BS, BS), F32)
    for d in range(3):
        totals[:, (1 + d) * BS : (2 + d) * BS] = partial_ref[d * BS : (d + 1) * BS, :]
    w_s, w_v = filter_ref[layer, :, :BS], filter_ref[layer, :, BS : 2 * BS]

    def terms(step, table, number):
        parts = []
        for i in range(number):
            slot = meta_ref[2, 2 * step + i]
            vectors = near[0][...]
            for e in range(2, n_sub):
                vectors = jnp.where(slot == e, near[e - 1][...], vectors)
            phi = phi_ref[slot - 1]
            phi_s, phi_v = phi[:, :BS], phi[:, BS:]
            parts.append([phi_s] + [phi_v * vectors[d * BS : (d + 1) * BS, :] for d in range(3)])
        for tile, names in enumerate(((w_s, w_v), (w_v, w_v))):
            cols = slice(tile * 2 * BS, (tile + 1) * 2 * BS)
            sources = [stacked(jnp.concatenate(p[2 * tile : 2 * tile + 2], axis=1)) for p in parts]
            add_terms(totals, cols, table, sources, jnp.concatenate(names, axis=1))

    def act(step, table):
        one_or_two(step, count, functools.partial(terms, step, table))

    over_tables(count, radial_hbm, buffer, sems, act)

    lower = meta_ref[4, 0] == 0
    mine, other = mine_ref[...], other_ref[...]
    half = mine.shape[0] // 2
    first = jnp.where(lower, mine, other)
    second = jnp.where(lower, other, mine)
    factors = factor_ref[layer] * scale
    both, low = stacked(
        jnp.concatenate(
            [
                first[:half] * factors[:half],
                second[:half] * factors[half:],
                first[half:] * factors[:half],
                second[half:] * factors[half:],
            ],
            axis=0,
        )
    )
    ewald = dot(own_ref[...], both) + dot(own_ref[:, : 2 * KW], low)
    mid_scalars = scalars_ref[...] + totals[:, :BS] + ewald
    mid_vectors = jnp.concatenate(
        [vectors_ref[d * BS : (d + 1) * BS, :] + totals[:, (1 + d) * BS : (2 + d) * BS] for d in range(3)], axis=0
    )
    mixed = dot3(mid_vectors, jnp.concatenate([left_ref[layer], right_ref[layer]], axis=1))
    left, right = mixed[:, :BS], mixed[:, BS:]
    parts = [slice(d * BS, (d + 1) * BS) for d in range(3)]
    norm = jnp.sqrt(sum(right[p] * right[p] for p in parts) + 1.0)
    along = sum(left[p] * right[p] for p in parts)
    hidden = silu(dot3(jnp.concatenate([mid_scalars, norm], axis=1), gate_in_ref[layer]))
    gates = dot3(hidden, gate_out_ref[layer])
    g_v, g_sv, g_s = (gates[:, i * BS : (i + 1) * BS] for i in range(3))
    new_scalars = mid_scalars + g_sv * along + g_s
    new_vectors = [mid_vectors[p] + g_v * left[p] for p in parts]
    if last:
        outs[0][...] = new_scalars
        for d in range(3):
            outs[1][d] = new_vectors[d]
    else:
        outs[0][...] = new_scalars
        for d, p in enumerate(parts):
            outs[1][p, :] = new_vectors[d]


def late_terms(meta, layer, last, scale, scalars, vectors, phi, near, tables, partial, mine, other, own, weights):
    n_sub = len(near)
    shapes = [(BS, BS), (3, BS, BS)] if last else [(BS, BS), (3 * BS, BS)]
    return pl.pallas_call(
        functools.partial(late_kernel, scale, n_sub, layer, last),
        in_specs=[SMEM_SPEC] + [VMEM_SPEC] * (12 + n_sub) + [HBM_SPEC],
        out_specs=[VMEM_SPEC] * len(shapes),
        scratch_shapes=[pltpu.VMEM((BS, 4 * BS), F32)] + table_buffers(1),
        out_shape=[jax.ShapeDtypeStruct(shape, F32) for shape in shapes],
        compiler_params=pltpu.CompilerParams(vmem_limit_bytes=VMEM),
        cost_estimate=cost(3 * 4 * NRBF * BS * BS * 4 * BS * 2 * 3, 10e6),
    )(meta, scalars, vectors, phi, partial, mine, other, own, *weights, *near[1:], tables)


def exchange(x, axis, mask):
    size = lax.axis_size(axis)
    return lax.ppermute(x, axis, [(i, i ^ mask) for i in range(size)])


def gather(x, first=()):
    n_sub = lax.axis_size("sub")
    parts = [None] * n_sub
    for e in range(0, n_sub, 2):
        parts[e] = x if e == 0 else exchange(x, "sub", e)
    if first:
        parts[::2] = lax.optimization_barrier((*parts[::2], *first))[: len(parts[::2])]
    for e in range(0, n_sub, 2):
        parts[e + 1] = exchange(parts[e], "sub", 1)
    return parts


def after(x, *others):
    return lax.optimization_barrier((x, *others))[0]


def body(
    scalars,
    vectors,
    positions,
    pair_blocks,
    pair_mask,
    wavevectors,
    message_in,
    message_out,
    filter_weight,
    ewald_weight,
    ewald_filter,
    mixing_left,
    mixing_right,
    update_in,
    update_out,
):
    n_region = lax.axis_size("region")
    n_sub = lax.axis_size("sub")
    natoms = BS * n_region * n_sub
    scale = 1.0 / math.sqrt(natoms * KW)
    per_region = pair_blocks.shape[1] // n_region
    slots = -(-min(n_sub - 1, per_region) // 2) * 2
    ids = jnp.stack([lax.axis_index("region"), lax.axis_index("sub")]).astype(jnp.int32)
    place = jnp.pad(positions, ((0, 8 - positions.shape[0]), (0, 0)))
    lean = jnp.concatenate([scalars, place], axis=0)
    vectors = vectors.reshape(3 * BS, -1)
    meta = find_pairs(ids, pair_blocks, n_sub, per_region, slots)
    own_trig = own_trig_of(wavevectors, lean)
    tables = region_trig = spots = None
    for layer in range(LAYERS):
        last = layer == LAYERS - 1
        blocks = gather(lean, (meta, own_trig) if layer == 0 else ())
        near = gather(after(vectors, *blocks[2::2]))
        near[0] = vectors
        if layer == 0:
            spots = blocks
            partial, region_trig = structure(layer, blocks, ewald_weight, meta, wavevectors)
        else:
            (partial,) = structure(layer, blocks, ewald_weight, region_trig=region_trig)
        others = [exchange(partial, "region", mask) for mask in range(1, n_region)]
        weights = (message_in, message_out, filter_weight)
        turn = after(meta, partial, *near[2:3])
        if layer == 0:
            along, phi, tables = early_terms(turn, layer, blocks, spots, weights, masks=pair_mask)
        else:
            along, phi = early_terms(turn, layer, blocks, spots, weights, tables=tables)
        *others, along = lax.optimization_barrier((*others, along))
        mine = sum(others, partial)
        theirs = exchange(mine, "sub", 1)
        results = late_terms(
            meta, layer, last, scale, scalars, vectors, phi, near, tables, along, mine, theirs, own_trig,
            (ewald_filter, filter_weight, mixing_left, mixing_right, update_in, update_out),
        )
        if last:
            scalars, vectors = results
        else:
            scalars, vectors = results
            lean = scalars
    return scalars, vectors


def solution(mesh):
    placed = (
        P(("region", "sub"), None),
        P(None, ("region", "sub"), None),
        P(None, ("region", "sub")),
    ) + (P(),) * 12
    return jax.shard_map(
        body,
        mesh=mesh,
        in_specs=placed,
        out_specs=(P(("region", "sub"), None), P(None, ("region", "sub"), None)),
        check_vma=False,
    )
```

time: 121 us -> 96.5 us (0.80)
  Pallas kernels: 63.4 us -> 49.2 us
  waiting for transfers between devices: 23.9 us -> 12.5 us
  starting transfers between devices: 25.8 us -> 30.8 us
  local copies, waits for them, and re-layouts: 4.84 us -> 1.45 us
    pallas_call x7, Pallas kernels: 62 us -> 47.8 us  [the longest x2 22.5 us: early_terms(): pl.pallas_call(functools.partial(early_kernel, n_sub, build, layer), in_s...]
    ppermute x36, waiting for transfers between devices: 23.9 us -> 12.5 us  [exchange(): return lax.ppermute(x, axis, [(i, i ^ mask) for i in range(size)])]
    ppermute x36, starting transfers between devices: 25.8 us -> 30.8 us  [exchange(): return lax.ppermute(x, axis, [(i, i ^ mask) for i in range(size)])]
    unnamed x75 -> x31, local copies, waits for them, and re-layouts: 4.84 us -> 1.45 us
  transfers between devices with their start and end apart: 36 -> 36, of which waited for: 8 -> 15; matrix products, arithmetic and copies ran while one was open for 2% -> 1% of each run, Pallas kernels for 32% -> 30%
where the time goes in v2:
time: 96.5 us; the launch traced here: 96.9 us
  Pallas kernels  49.2 us (51%)
  starting transfers between devices  30.8 us (32%)
  waiting for transfers between devices  12.5 us (13%)
  other arithmetic  1.75 us (2%)
  local copies, waits for them, and re-layouts  1.45 us (2%)
  between operations  1.14 us (1%)
    ppermute x36, starting transfers between devices, exchange(): return lax.ppermute(x, axis, [(i, i ^ mask) for i in range(size)])  30.8 us
    pallas_call x2, Pallas kernels, early_terms(): pl.pallas_call(functools.partial(early_kernel, n_sub, build, layer), in_s...  22.5 us
    pallas_call x2, Pallas kernels, late_terms(): pl.pallas_call(functools.partial(late_kernel, scale, n_sub, layer, last),...  20 us
    ppermute x36, waiting for transfers between devices, exchange(): return lax.ppermute(x, axis, [(i, i ^ mask) for i in range(size)])  12.5 us
    pallas_call x2, Pallas kernels, structure(): pl.pallas_call(functools.partial(structure_kernel, n_sub, build, layer),...  4.69 us
  transfers between devices with their start and end apart: 36, of which 15 were waited for; matrix products, arithmetic and copies ran while one was open for 1% of the time, Pallas kernels for 30%

profile of v2, /device:TPU:0, one launch (start us, length us, event | category | flops | bytes accessed | tf_op | source)
XLA Modules:
  0.0 96.9 jit_solution(5264247616401238912)
XLA Ops:
  0.7 0.9 select_maximum_fusion.place_ref.refs_2_.refs_0_.refs_8_
  1.6 3.0 %collective-permute-start = (f32[136,128]{1,0:T(8,128)S(1)}, f32[136,128]{1,0:T(8,128)S(1)}, u32[]{:S(2)}, u32[]{:S(2)}) collective-permute-start(f32[136,128]{1,0:T(8,128)S(1)} %select_maximum_fusion.place_ref.refs_2_.refs_0_.refs_8_), channel_id=1, source_target_pairs={{0,2},{1,3},{2,0},{3,1},{4,6},{5,7},{6,4},{7,5},{8,10},{9,11},{10,... | collective-permute-start | bytes 208904 | tf_op jit(solution)/shard_map/ppermute | solution.py:512
  4.6 2.6 %collective-permute-start.1 = (f32[136,128]{1,0:T(8,128)S(1)}, f32[136,128]{1,0:T(8,128)S(1)}, u32[]{:S(2)}, u32[]{:S(2)}) collective-permute-start(f32[136,128]{1,0:T(8,128)S(1)} %select_maximum_fusion.place_ref.refs_2_.refs_0_.refs_8_), channel_id=1, source_target_pairs={{0,4},{1,5},{2,6},{3,7},{4,0},{5,1},{6,2},{7,3},{8,12},{9,13},{10,... | collective-permute-start | bytes 208904 | tf_op jit(solution)/shard_map/ppermute | solution.py:512
  7.2 0.7 copy-done.12
  7.9 0.5 shard_map.159.refs_6_
  8.5 0.7 pad_add_fusion.ids_ref
  9.1 1.5 %shard_map.158.refs_0_.meta_ref = s32[5,8]{1,0:T(8,128)} custom-call(s32[2]{0:T(128)} %pad_add_fusion.ids_ref, s32[2,48]{1,0:T(2,128)} %pairs_ref.1), custom_call_target="tpu_custom_call" | custom-call | tf_op jit(solution)/shard_map/pallas_call | solution.py:121
  10.6 1.6 %collective-permute-done.1.refs_6_.refs_4_.refs_12_ = f32[136,128]{1,0:T(8,128)S(1)} collective-permute-done((f32[136,128]{1,0:T(8,128)S(1)}, f32[136,128]{1,0:T(8,128)S(1)}, u32[]{:S(2)}, u32[]{:S(2)}) %collective-permute-start.1) | collective-permute-done | bytes 69664 | tf_op jit(solution)/shard_map/ppermute | solution.py:512
  12.2 1.3 %collective-permute-done.2.refs_8_.refs_6_.refs_14_ = f32[136,128]{1,0:T(8,128)S(1)} collective-permute-done((f32[136,128]{1,0:T(8,128)S(1)}, f32[136,128]{1,0:T(8,128)S(1)}, u32[]{:S(2)}, u32[]{:S(2)}) %collective-permute-start.2) | collective-permute-done | bytes 69664 | tf_op jit(solution)/shard_map/ppermute | solution.py:512
  13.5 0.8 collective-permute-start.7
  14.2 0.5 collective-permute-start.5
  14.7 0.5 collective-permute-start.3
  15.3 0.2 collective-permute-done.4.refs_5_.refs_3_.refs_11_
  15.5 1.7 %collective-permute-start.14 = (f32[384,128]{1,0:T(8,128)S(1)}, f32[384,128]{1,0:T(8,128)S(1)}, u32[]{:S(2)}, u32[]{:S(2)}) collective-permute-start(f32[384,128]{1,0:T(8,128)S(1)} %bitcast.4), channel_id=1, source_target_pairs={{0,4},{1,5},{2,6},{3,7},{4,0},{5,1},{6,2},{7,3},{8,12},{9,13},{10,... | collective-permute-start | bytes 589832 | tf_op jit(solution)/shard_map/ppermute | solution.py:512
  17.2 1.9 %collective-permute-start.16 = (f32[384,128]{1,0:T(8,128)S(1)}, f32[384,128]{1,0:T(8,128)S(1)}, u32[]{:S(2)}, u32[]{:S(2)}) collective-permute-start(f32[384,128]{1,0:T(8,128)S(1)} %bitcast.5), channel_id=1, source_target_pairs={{0,6},{1,7},{2,4},{3,5},{4,2},{5,3},{6,0},{7,1},{8,14},{9,15},{10,... | collective-permute-start | bytes 589832 | tf_op jit(solution)/shard_map/ppermute | solution.py:512
  19.1 0.7 copy-done.2
  19.8 3.4 %shard_map.160 = (f32[512,128]{1,0:T(8,128)S(1)}, bf16[512,2048]{1,0:T(8,128)(2,1)S(1)}) custom-call(s32[5,8]{1,0:T(8,128)S(1)} %copy-done.2, f32[3,512]{1,0:T(4,128)S(1)} %copy-done.13, f32[136,128]{1,0:T(8,128)S(1)} %select_maximum_fusion.place_ref.refs_2_.refs_0_.refs_8_, f32[136,128]{1,0:T(8,128)S(1)} %collective-permute-done.3.refs_3_.refs_1_.refs_9_, ...), custom_call_target="tpu_custom_call" | custom-call | flops 402653184 | bytes 4000000 | tf_op jit(solution)/shard_map/pallas_call | solution.py:407
  23.3 2.5 %collective-permute-start.10 = (f32[512,128]{1,0:T(8,128)S(1)}, f32[512,128]{1,0:T(8,128)S(1)}, u32[]{:S(2)}, u32[]{:S(2)}) collective-permute-start(f32[512,128]{1,0:T(8,128)S(1)} %get-tuple-element.31), channel_id=1, source_target_pairs={{0,24},{8,16},{16,8},{24,0},{1,25},{9,17},{17,9},{25,1},{2,26},{10... | collective-permute-start | bytes 786440 | tf_op jit(solution)/shard_map/ppermute | solution.py:512
  25.8 0.5 collective-permute-start.8
  26.4 0.5 collective-permute-start.9
  26.9 12.8 %shard_map.161 = (f32[384,128]{1,0:T(8,128)S(1)}, f32[7,128,256]{2,1,0:T(8,128)S(1)}, bf16[2,8,2560,256]{3,2,1,0:T(8,128)(2,1)}) custom-call(s32[5,8]{1,0:T(8,128)S(1)} %copy-done.2, f32[136,128]{1,0:T(8,128)S(1)} %select_maximum_fusion.place_ref.refs_2_.refs_0_.refs_8_, f32[136,128]{1,0:T(8,128)S(1)} %collective-permute-done.3.refs_3_.refs_1_.refs_9_, ...), custom_call_target="tpu_custom_call" | custom-call | flops 12079595520 | bytes 10000000 | tf_op jit(solution)/shard_map/pallas_call | solution.py:333
  39.9 0.5 collective-permute-start.12
  40.5 0.4 collective-permute-start.15
  41.0 0.7 collective-permute-done.12.refs_13_
  41.7 0.3 collective-permute-done.13.refs_15_
  42.0 0.3 collective-permute-done.15.refs_17_
  42.3 0.3 collective-permute-done.17.refs_19_
  42.6 9.7 %shard_map.162 = (f32[128,128]{1,0:T(8,128)S(1)}, f32[384,128]{1,0:T(8,128)S(1)}) custom-call(s32[5,8]{1,0:T(8,128)S(1)} %copy-done.2, f32[128,128]{1,0:T(8,128)S(1)} %copy-done.1, f32[384,128]{1,0:T(8,128)S(1)} %bitcast.7, f32[7,128,256]{2,1,0:T(8,128)S(1)} %get-tuple-element.34.refs_2_, f32[384,128]{1,0:T(8,128)S(1)} %get-tuple-element.36.refs_3_, ...), custom_call_target="tpu_custom_call" | custom-call | flops 12079595520 | bytes 10000000 | tf_op jit(solution)/shard_map/pallas_call | solution.py:499
  52.5 4.3 %collective-permute-start.23 = (f32[128,128]{1,0:T(8,128)S(1)}, f32[128,128]{1,0:T(8,128)S(1)}, u32[]{:S(2)}, u32[]{:S(2)}) collective-permute-start(f32[128,128]{1,0:T(8,128)S(1)} %get-tuple-element.41.refs_0_), channel_id=1, source_target_pairs={{0,6},{1,7},{2,4},{3,5},{4,2},{5,3},{6,0},{7,1},{8,14},{9,15},{10,... | collective-permute-start | bytes 196616 | tf_op jit(solution)/shard_map/ppermute | solution.py:512
  56.8 0.9 collective-permute-done.21.refs_4_
  57.6 3.5 %collective-permute-done.23.refs_6_ = f32[128,128]{1,0:T(8,128)S(1)} collective-permute-done((f32[128,128]{1,0:T(8,128)S(1)}, f32[128,128]{1,0:T(8,128)S(1)}, u32[]{:S(2)}, u32[]{:S(2)}) %collective-permute-start.23) | collective-permute-done | bytes 65568 | tf_op jit(solution)/shard_map/ppermute | solution.py:512
  61.1 0.5 collective-permute-start.20
  61.6 0.5 collective-permute-start.24
  62.1 0.2 collective-permute-done.18.refs_1_
  62.4 2.8 %collective-permute-start.32 = (f32[384,128]{1,0:T(8,128)S(1)}, f32[384,128]{1,0:T(8,128)S(1)}, u32[]{:S(2)}, u32[]{:S(2)}) collective-permute-start(f32[384,128]{1,0:T(8,128)S(1)} %get-tuple-element.44.refs_1_), channel_id=1, source_target_pairs={{0,4},{1,5},{2,6},{3,7},{4,0},{5,1},{6,2},{7,3},{8,12},{9,13},{10,... | collective-permute-start | bytes 589832 | tf_op jit(solution)/shard_map/ppermute | solution.py:512
  65.1 1.6 %collective-permute-start.34 = (f32[384,128]{1,0:T(8,128)S(1)}, f32[384,128]{1,0:T(8,128)S(1)}, u32[]{:S(2)}, u32[]{:S(2)}) collective-permute-start(f32[384,128]{1,0:T(8,128)S(1)} %get-tuple-element.44.refs_1_), channel_id=1, source_target_pairs={{0,6},{1,7},{2,4},{3,5},{4,2},{5,3},{6,0},{7,1},{8,14},{9,15},{10,... | collective-permute-start | bytes 589832 | tf_op jit(solution)/shard_map/ppermute | solution.py:512
  66.8 1.3 %shard_map.163 = f32[512,128]{1,0:T(8,128)S(1)} custom-call(f32[128,128]{1,0:T(8,128)S(1)} %get-tuple-element.41.refs_0_, f32[128,128]{1,0:T(8,128)S(1)} %collective-permute-done.18.refs_1_, f32[128,128]{1,0:T(8,128)S(1)} %collective-permute-done.19.refs_2_, f32[128,128]{1,0:T(8,128)S(1)} %collective-permute-done.20.refs_3_, ...), custom_call_target="tpu_custom_call" | custom-call | flops 402653184 | bytes 4000000 | tf_op jit(solution)/shard_map/pallas_call | solution.py:407
  68.1 2.6 %collective-permute-start.27 = (f32[512,128]{1,0:T(8,128)S(1)}, f32[512,128]{1,0:T(8,128)S(1)}, u32[]{:S(2)}, u32[]{:S(2)}) collective-permute-start(f32[512,128]{1,0:T(8,128)S(1)} %shard_map.163), channel_id=1, source_target_pairs={{0,16},{8,24},{16,0},{24,8},{1,17},{9,25},{17,1},{25,9},{2,18},{10... | collective-permute-start | bytes 786440 | tf_op jit(solution)/shard_map/ppermute | solution.py:512
  70.7 1.4 %collective-permute-start.28 = (f32[512,128]{1,0:T(8,128)S(1)}, f32[512,128]{1,0:T(8,128)S(1)}, u32[]{:S(2)}, u32[]{:S(2)}) collective-permute-start(f32[512,128]{1,0:T(8,128)S(1)} %shard_map.163), channel_id=1, source_target_pairs={{0,24},{8,16},{16,8},{24,0},{1,25},{9,17},{17,9},{25,1},{2,26},{10... | collective-permute-start | bytes 786440 | tf_op jit(solution)/shard_map/ppermute | solution.py:512
  72.1 9.7 %shard_map.164 = (f32[384,128]{1,0:T(8,128)S(1)}, f32[7,128,256]{2,1,0:T(8,128)S(1)}) custom-call(s32[5,8]{1,0:T(8,128)S(1)} %copy-done.2, f32[128,128]{1,0:T(8,128)S(1)} %get-tuple-element.41.refs_0_, f32[128,128]{1,0:T(8,128)S(1)} %collective-permute-done.18.refs_1_, f32[128,128]{1,0:T(8,128)S(1)} %collective-permute-done.19.refs_2_, ...), custom_call_target="tpu_custom_call" | custom-call | flops 12079595520 | bytes 10000000 | tf_op jit(solution)/shard_map/pallas_call | solution.py:333
  81.8 1.7 %collective-permute-done.28 = f32[512,128]{1,0:T(8,128)S(1)} collective-permute-done((f32[512,128]{1,0:T(8,128)S(1)}, f32[512,128]{1,0:T(8,128)S(1)}, u32[]{:S(2)}, u32[]{:S(2)}) %collective-permute-start.28) | collective-permute-done | bytes 262176 | tf_op jit(solution)/shard_map/ppermute | solution.py:512
  83.7 0.5 collective-permute-start.30
  84.3 0.4 collective-permute-start.33
  84.8 0.7 collective-permute-done.30.refs_13_
  85.5 0.3 collective-permute-done.31.refs_15_
  85.8 0.3 collective-permute-done.33.refs_17_
  86.0 0.3 collective-permute-done.35.refs_19_
  86.3 10.3 %shard_map.165 = (f32[128,128]{1,0:T(8,128)}, f32[3,128,128]{2,1,0:T(8,128)}) custom-call(s32[5,8]{1,0:T(8,128)S(1)} %copy-done.2, f32[128,128]{1,0:T(8,128)S(1)} %get-tuple-element.41.refs_0_, f32[384,128]{1,0:T(8,128)S(1)} %get-tuple-element.44.refs_1_, f32[7,128,256]{2,1,0:T(8,128)S(1)} %get-tuple-element.46.refs_2_, ...), custom_call_target="tpu_custom_call" | custom-call | flops 12079595520 | bytes 10000000 | tf_op jit(solution)/shard_map/pallas_call | solution.py:499
  (67 shorter events, 1.0 us)
Async XLA Ops:
  0.6 12.8 %copy-start.7 = (f32[3,128,128]{2,1,0:T(8,128)S(1)}, f32[3,128,128]{2,1,0:T(8,128)}, u32[]{:S(2)}) copy-start(f32[3,128,128]{2,1,0:T(8,128)} %param.16) | copy-start | bytes 589828
  0.6 18.5 %copy-start = (f32[2,128,128]{2,1,0:T(8,128)S(1)}, f32[2,128,128]{2,1,0:T(8,128)}, u32[]{:S(2)}) copy-start(f32[2,128,128]{2,1,0:T(8,128)} %refs_8_.3) | copy-start | bytes 393220
  0.7 26.2 %copy-start.11 = (s32[48,547]{1,0:T(8,128)S(1)}, s32[48,547]{1,0:T(8,128)}, u32[]{:S(2)}) copy-start(s32[48,547]{1,0:T(8,128)} %refs_19_.1) | copy-start | bytes 315076
  0.7 26.2 %copy-start.8 = (f32[2,128,128]{2,1,0:T(8,128)S(1)}, f32[2,128,128]{2,1,0:T(8,128)}, u32[]{:S(2)}) copy-start(f32[2,128,128]{2,1,0:T(8,128)} %refs_16_.3) | copy-start | bytes 393220
  0.7 26.2 %copy-start.4 = (f32[2,128,384]{2,1,0:T(8,128)S(1)}, f32[2,128,384]{2,1,0:T(8,128)}, u32[]{:S(2)}) copy-start(f32[2,128,384]{2,1,0:T(8,128)} %refs_17_.3) | copy-start | bytes 1179652
  1.6 9.0 %collective-permute-start = (f32[136,128]{1,0:T(8,128)S(1)}, f32[136,128]{1,0:T(8,128)S(1)}, u32[]{:S(2)}, u32[]{:S(2)}) collective-permute-start(f32[136,128]{1,0:T(8,128)S(1)} %select_maximum_fusion.place_ref.refs_2_.refs_0_.refs_8_), channel_id=1, source_target_pairs={{0,2},{1,3},{2,0},{3,1},{4,6},{5,7},{6,4},{7,5},{8,10},{9,11},{10,... | collective-permute-start | bytes 208904 | tf_op jit(solution)/shard_map/ppermute | solution.py:512
  4.6 7.5 %collective-permute-start.1 = (f32[136,128]{1,0:T(8,128)S(1)}, f32[136,128]{1,0:T(8,128)S(1)}, u32[]{:S(2)}, u32[]{:S(2)}) collective-permute-start(f32[136,128]{1,0:T(8,128)S(1)} %select_maximum_fusion.place_ref.refs_2_.refs_0_.refs_8_), channel_id=1, source_target_pairs={{0,4},{1,5},{2,6},{3,7},{4,0},{5,1},{6,2},{7,3},{8,12},{9,13},{10,... | collective-permute-start | bytes 208904 | tf_op jit(solution)/shard_map/ppermute | solution.py:512
  7.2 6.2 %collective-permute-start.2 = (f32[136,128]{1,0:T(8,128)S(1)}, f32[136,128]{1,0:T(8,128)S(1)}, u32[]{:S(2)}, u32[]{:S(2)}) collective-permute-start(f32[136,128]{1,0:T(8,128)S(1)} %select_maximum_fusion.place_ref.refs_2_.refs_0_.refs_8_), channel_id=1, source_target_pairs={{0,6},{1,7},{2,4},{3,5},{4,2},{5,3},{6,0},{7,1},{8,14},{9,15},{10,... | collective-permute-start | bytes 208904 | tf_op jit(solution)/shard_map/ppermute | solution.py:512
  7.9 11.2 %copy-start.13 = (f32[3,512]{1,0:T(4,128)S(1)}, f32[3,512]{1,0:T(4,128)}, u32[]{:S(2)}) copy-start(f32[3,512]{1,0:T(4,128)} %refs_1_.1) | copy-start | bytes 18436
  13.5 12.9 %collective-permute-start.7 = (f32[384,128]{1,0:T(8,128)S(1)}, f32[384,128]{1,0:T(8,128)S(1)}, u32[]{:S(2)}, u32[]{:S(2)}) collective-permute-start(f32[384,128]{1,0:T(8,128)S(1)} %bitcast.3), channel_id=1, source_target_pairs={{0,2},{1,3},{2,0},{3,1},{4,6},{5,7},{6,4},{7,5},{8,10},{9,11},{10,... | collective-permute-start | bytes 589832 | tf_op jit(solution)/shard_map/ppermute | solution.py:512
  14.2 1.3 %collective-permute-start.4 = (f32[136,128]{1,0:T(8,128)S(1)}, f32[136,128]{1,0:T(8,128)S(1)}, u32[]{:S(2)}, u32[]{:S(2)}) collective-permute-start(f32[136,128]{1,0:T(8,128)S(1)} %collective-permute-done.refs_4_.refs_2_.refs_10_), channel_id=1, source_target_pairs={{0,1},{1,0},{2,3},{3,2},{4,5},{5,4},{6,7},{7,6},{8,9},{9,8},{10,11... | collective-permute-start | bytes 208904 | tf_op jit(solution)/shard_map/ppermute | solution.py:512
  14.2 3.0 %collective-permute-start.5 = (f32[136,128]{1,0:T(8,128)S(1)}, f32[136,128]{1,0:T(8,128)S(1)}, u32[]{:S(2)}, u32[]{:S(2)}) collective-permute-start(f32[136,128]{1,0:T(8,128)S(1)} %collective-permute-done.1.refs_6_.refs_4_.refs_12_), channel_id=1, source_target_pairs={{0,1},{1,0},{2,3},{3,2},{4,5},{5,4},{6,7},{7,6},{8,9},{9,8},{10,11... | collective-permute-start | bytes 208904 | tf_op jit(solution)/shard_map/ppermute | solution.py:512
  14.7 4.4 %collective-permute-start.6 = (f32[136,128]{1,0:T(8,128)S(1)}, f32[136,128]{1,0:T(8,128)S(1)}, u32[]{:S(2)}, u32[]{:S(2)}) collective-permute-start(f32[136,128]{1,0:T(8,128)S(1)} %collective-permute-done.2.refs_8_.refs_6_.refs_14_), channel_id=1, source_target_pairs={{0,1},{1,0},{2,3},{3,2},{4,5},{5,4},{6,7},{7,6},{8,9},{9,8},{10,11... | collective-permute-start | bytes 208904 | tf_op jit(solution)/shard_map/ppermute | solution.py:512
  14.7 4.4 %collective-permute-start.3 = (f32[136,128]{1,0:T(8,128)S(1)}, f32[136,128]{1,0:T(8,128)S(1)}, u32[]{:S(2)}, u32[]{:S(2)}) collective-permute-start(f32[136,128]{1,0:T(8,128)S(1)} %select_maximum_fusion.place_ref.refs_2_.refs_0_.refs_8_), channel_id=1, source_target_pairs={{0,1},{1,0},{2,3},{3,2},{4,5},{5,4},{6,7},{7,6},{8,9},{9,8},{10,11... | collective-permute-start | bytes 208904 | tf_op jit(solution)/shard_map/ppermute | solution.py:512
  15.5 25.0 %collective-permute-start.14 = (f32[384,128]{1,0:T(8,128)S(1)}, f32[384,128]{1,0:T(8,128)S(1)}, u32[]{:S(2)}, u32[]{:S(2)}) collective-permute-start(f32[384,128]{1,0:T(8,128)S(1)} %bitcast.4), channel_id=1, source_target_pairs={{0,4},{1,5},{2,6},{3,7},{4,0},{5,1},{6,2},{7,3},{8,12},{9,13},{10,... | collective-permute-start | bytes 589832 | tf_op jit(solution)/shard_map/ppermute | solution.py:512
  17.2 23.7 %collective-permute-start.16 = (f32[384,128]{1,0:T(8,128)S(1)}, f32[384,128]{1,0:T(8,128)S(1)}, u32[]{:S(2)}, u32[]{:S(2)}) collective-permute-start(f32[384,128]{1,0:T(8,128)S(1)} %bitcast.5), channel_id=1, source_target_pairs={{0,6},{1,7},{2,4},{3,5},{4,2},{5,3},{6,0},{7,1},{8,14},{9,15},{10,... | collective-permute-start | bytes 589832 | tf_op jit(solution)/shard_map/ppermute | solution.py:512
  23.2 19.3 %copy-start.1 = (f32[128,128]{1,0:T(8,128)S(1)}, f32[128,128]{1,0:T(8,128)}, u32[]{:S(2)}) copy-start(f32[128,128]{1,0:T(8,128)} %refs_0_.1) | copy-start | bytes 196612
  23.2 19.3 %copy-start.3 = (f32[2,512,128]{2,1,0:T(8,128)S(1)}, f32[2,512,128]{2,1,0:T(8,128)}, u32[]{:S(2)}) copy-start(f32[2,512,128]{2,1,0:T(8,128)} %refs_7_.3) | copy-start | bytes 1572868
  23.3 19.3 %copy-start.5 = (f32[2,128,384]{2,1,0:T(8,128)S(1)}, f32[2,128,384]{2,1,0:T(8,128)}, u32[]{:S(2)}) copy-start(f32[2,128,384]{2,1,0:T(8,128)} %refs_12_.3) | copy-start | bytes 1179652
  23.3 19.3 %copy-start.6 = (f32[2,256,128]{2,1,0:T(8,128)S(1)}, f32[2,256,128]{2,1,0:T(8,128)}, u32[]{:S(2)}) copy-start(f32[2,256,128]{2,1,0:T(8,128)} %refs_11_.3) | copy-start | bytes 786436
  23.3 19.3 %copy-start.9 = (f32[2,128,128]{2,1,0:T(8,128)S(1)}, f32[2,128,128]{2,1,0:T(8,128)}, u32[]{:S(2)}) copy-start(f32[2,128,128]{2,1,0:T(8,128)} %refs_9_.3) | copy-start | bytes 393220
  23.3 19.3 %copy-start.10 = (f32[2,128,128]{2,1,0:T(8,128)S(1)}, f32[2,128,128]{2,1,0:T(8,128)}, u32[]{:S(2)}) copy-start(f32[2,128,128]{2,1,0:T(8,128)} %refs_10_.5) | copy-start | bytes 393220
  23.3 16.4 %collective-permute-start.10 = (f32[512,128]{1,0:T(8,128)S(1)}, f32[512,128]{1,0:T(8,128)S(1)}, u32[]{:S(2)}, u32[]{:S(2)}) collective-permute-start(f32[512,128]{1,0:T(8,128)S(1)} %get-tuple-element.31), channel_id=1, source_target_pairs={{0,24},{8,16},{16,8},{24,0},{1,25},{9,17},{17,9},{25,1},{2,26},{10... | collective-permute-start | bytes 786440 | tf_op jit(solution)/shard_map/ppermute | solution.py:512
  25.8 13.9 %collective-permute-start.8 = (f32[512,128]{1,0:T(8,128)S(1)}, f32[512,128]{1,0:T(8,128)S(1)}, u32[]{:S(2)}, u32[]{:S(2)}) collective-permute-start(f32[512,128]{1,0:T(8,128)S(1)} %get-tuple-element.31), channel_id=1, source_target_pairs={{0,8},{8,0},{16,24},{24,16},{1,9},{9,1},{17,25},{25,17},{2,10},{10... | collective-permute-start | bytes 786440 | tf_op jit(solution)/shard_map/ppermute | solution.py:512
  26.4 13.4 %collective-permute-start.9 = (f32[512,128]{1,0:T(8,128)S(1)}, f32[512,128]{1,0:T(8,128)S(1)}, u32[]{:S(2)}, u32[]{:S(2)}) collective-permute-start(f32[512,128]{1,0:T(8,128)S(1)} %get-tuple-element.31), channel_id=1, source_target_pairs={{0,16},{8,24},{16,0},{24,8},{1,17},{9,25},{17,1},{25,9},{2,18},{10... | collective-permute-start | bytes 786440 | tf_op jit(solution)/shard_map/ppermute | solution.py:512
  39.8 2.7 %collective-permute-start.11 = (f32[512,128]{1,0:T(8,128)S(1)}, f32[512,128]{1,0:T(8,128)S(1)}, u32[]{:S(2)}, u32[]{:S(2)}) collective-permute-start(f32[512,128]{1,0:T(8,128)S(1)} %add_add_fusion.1.refs_4_), channel_id=1, source_target_pairs={{0,1},{1,0},{2,3},{3,2},{4,5},{5,4},{6,7},{7,6},{8,9},{9,8},{10,11... | collective-permute-start | bytes 786440 | tf_op jit(solution)/shard_map/ppermute | solution.py:512
  39.9 1.8 %collective-permute-start.12 = (f32[384,128]{1,0:T(8,128)S(1)}, f32[384,128]{1,0:T(8,128)S(1)}, u32[]{:S(2)}, u32[]{:S(2)}) collective-permute-start(f32[384,128]{1,0:T(8,128)S(1)} %bitcast.6), channel_id=1, source_target_pairs={{0,1},{1,0},{2,3},{3,2},{4,5},{5,4},{6,7},{7,6},{8,9},{9,8},{10,11... | collective-permute-start | bytes 589832 | tf_op jit(solution)/shard_map/ppermute | solution.py:512
  40.4 1.6 %collective-permute-start.13 = (f32[384,128]{1,0:T(8,128)S(1)}, f32[384,128]{1,0:T(8,128)S(1)}, u32[]{:S(2)}, u32[]{:S(2)}) collective-permute-start(f32[384,128]{1,0:T(8,128)S(1)} %collective-permute-done.7.refs_14_), channel_id=1, source_target_pairs={{0,1},{1,0},{2,3},{3,2},{4,5},{5,4},{6,7},{7,6},{8,9},{9,8},{10,11... | collective-permute-start | bytes 589832 | tf_op jit(solution)/shard_map/ppermute | solution.py:512
  40.5 1.8 %collective-permute-start.15 = (f32[384,128]{1,0:T(8,128)S(1)}, f32[384,128]{1,0:T(8,128)S(1)}, u32[]{:S(2)}, u32[]{:S(2)}) collective-permute-start(f32[384,128]{1,0:T(8,128)S(1)} %collective-permute-done.14.refs_16_), channel_id=1, source_target_pairs={{0,1},{1,0},{2,3},{3,2},{4,5},{5,4},{6,7},{7,6},{8,9},{9,8},{10,11... | collective-permute-start | bytes 589832 | tf_op jit(solution)/shard_map/ppermute | solution.py:512
  40.9 1.6 %collective-permute-start.17 = (f32[384,128]{1,0:T(8,128)S(1)}, f32[384,128]{1,0:T(8,128)S(1)}, u32[]{:S(2)}, u32[]{:S(2)}) collective-permute-start(f32[384,128]{1,0:T(8,128)S(1)} %collective-permute-done.16.refs_18_), channel_id=1, source_target_pairs={{0,1},{1,0},{2,3},{3,2},{4,5},{5,4},{6,7},{7,6},{8,9},{9,8},{10,11... | collective-permute-start | bytes 589832 | tf_op jit(solution)/shard_map/ppermute | solution.py:512
  52.3 4.5 %collective-permute-start.19 = (f32[128,128]{1,0:T(8,128)S(1)}, f32[128,128]{1,0:T(8,128)S(1)}, u32[]{:S(2)}, u32[]{:S(2)}) collective-permute-start(f32[128,128]{1,0:T(8,128)S(1)} %get-tuple-element.41.refs_0_), channel_id=1, source_target_pairs={{0,2},{1,3},{2,0},{3,1},{4,6},{5,7},{6,4},{7,5},{8,10},{9,11},{10,... | collective-permute-start | bytes 196616 | tf_op jit(solution)/shard_map/ppermute | solution.py:512
  52.4 5.2 %collective-permute-start.21 = (f32[128,128]{1,0:T(8,128)S(1)}, f32[128,128]{1,0:T(8,128)S(1)}, u32[]{:S(2)}, u32[]{:S(2)}) collective-permute-start(f32[128,128]{1,0:T(8,128)S(1)} %get-tuple-element.41.refs_0_), channel_id=1, source_target_pairs={{0,4},{1,5},{2,6},{3,7},{4,0},{5,1},{6,2},{7,3},{8,12},{9,13},{10,... | collective-permute-start | bytes 196616 | tf_op jit(solution)/shard_map/ppermute | solution.py:512
  52.5 8.6 %collective-permute-start.23 = (f32[128,128]{1,0:T(8,128)S(1)}, f32[128,128]{1,0:T(8,128)S(1)}, u32[]{:S(2)}, u32[]{:S(2)}) collective-permute-start(f32[128,128]{1,0:T(8,128)S(1)} %get-tuple-element.41.refs_0_), channel_id=1, source_target_pairs={{0,6},{1,7},{2,4},{3,5},{4,2},{5,3},{6,0},{7,1},{8,14},{9,15},{10,... | collective-permute-start | bytes 196616 | tf_op jit(solution)/shard_map/ppermute | solution.py:512
  61.1 9.6 %collective-permute-start.25 = (f32[384,128]{1,0:T(8,128)S(1)}, f32[384,128]{1,0:T(8,128)S(1)}, u32[]{:S(2)}, u32[]{:S(2)}) collective-permute-start(f32[384,128]{1,0:T(8,128)S(1)} %get-tuple-element.44.refs_1_), channel_id=1, source_target_pairs={{0,2},{1,3},{2,0},{3,1},{4,6},{5,7},{6,4},{7,5},{8,10},{9,11},{10,... | collective-permute-start | bytes 589832 | tf_op jit(solution)/shard_map/ppermute | solution.py:512
  61.1 1.3 %collective-permute-start.18 = (f32[128,128]{1,0:T(8,128)S(1)}, f32[128,128]{1,0:T(8,128)S(1)}, u32[]{:S(2)}, u32[]{:S(2)}) collective-permute-start(f32[128,128]{1,0:T(8,128)S(1)} %get-tuple-element.41.refs_0_), channel_id=1, source_target_pairs={{0,1},{1,0},{2,3},{3,2},{4,5},{5,4},{6,7},{7,6},{8,9},{9,8},{10,11... | collective-permute-start | bytes 196616 | tf_op jit(solution)/shard_map/ppermute | solution.py:512
  61.1 4.0 %collective-permute-start.20 = (f32[128,128]{1,0:T(8,128)S(1)}, f32[128,128]{1,0:T(8,128)S(1)}, u32[]{:S(2)}, u32[]{:S(2)}) collective-permute-start(f32[128,128]{1,0:T(8,128)S(1)} %collective-permute-done.19.refs_2_), channel_id=1, source_target_pairs={{0,1},{1,0},{2,3},{3,2},{4,5},{5,4},{6,7},{7,6},{8,9},{9,8},{10,11... | collective-permute-start | bytes 196616 | tf_op jit(solution)/shard_map/ppermute | solution.py:512
  61.6 5.1 %collective-permute-start.22 = (f32[128,128]{1,0:T(8,128)S(1)}, f32[128,128]{1,0:T(8,128)S(1)}, u32[]{:S(2)}, u32[]{:S(2)}) collective-permute-start(f32[128,128]{1,0:T(8,128)S(1)} %collective-permute-done.21.refs_4_), channel_id=1, source_target_pairs={{0,1},{1,0},{2,3},{3,2},{4,5},{5,4},{6,7},{7,6},{8,9},{9,8},{10,11... | collective-permute-start | bytes 196616 | tf_op jit(solution)/shard_map/ppermute | solution.py:512
  61.6 5.1 %collective-permute-start.24 = (f32[128,128]{1,0:T(8,128)S(1)}, f32[128,128]{1,0:T(8,128)S(1)}, u32[]{:S(2)}, u32[]{:S(2)}) collective-permute-start(f32[128,128]{1,0:T(8,128)S(1)} %collective-permute-done.23.refs_6_), channel_id=1, source_target_pairs={{0,1},{1,0},{2,3},{3,2},{4,5},{5,4},{6,7},{7,6},{8,9},{9,8},{10,11... | collective-permute-start | bytes 196616 | tf_op jit(solution)/shard_map/ppermute | solution.py:512
  62.4 21.9 %collective-permute-start.32 = (f32[384,128]{1,0:T(8,128)S(1)}, f32[384,128]{1,0:T(8,128)S(1)}, u32[]{:S(2)}, u32[]{:S(2)}) collective-permute-start(f32[384,128]{1,0:T(8,128)S(1)} %get-tuple-element.44.refs_1_), channel_id=1, source_target_pairs={{0,4},{1,5},{2,6},{3,7},{4,0},{5,1},{6,2},{7,3},{8,12},{9,13},{10,... | collective-permute-start | bytes 589832 | tf_op jit(solution)/shard_map/ppermute | solution.py:512
  65.1 19.6 %collective-permute-start.34 = (f32[384,128]{1,0:T(8,128)S(1)}, f32[384,128]{1,0:T(8,128)S(1)}, u32[]{:S(2)}, u32[]{:S(2)}) collective-permute-start(f32[384,128]{1,0:T(8,128)S(1)} %get-tuple-element.44.refs_1_), channel_id=1, source_target_pairs={{0,6},{1,7},{2,4},{3,5},{4,2},{5,3},{6,0},{7,1},{8,14},{9,15},{10,... | collective-permute-start | bytes 589832 | tf_op jit(solution)/shard_map/ppermute | solution.py:512
  68.1 13.7 %collective-permute-start.26 = (f32[512,128]{1,0:T(8,128)S(1)}, f32[512,128]{1,0:T(8,128)S(1)}, u32[]{:S(2)}, u32[]{:S(2)}) collective-permute-start(f32[512,128]{1,0:T(8,128)S(1)} %shard_map.163), channel_id=1, source_target_pairs={{0,8},{8,0},{16,24},{24,16},{1,9},{9,1},{17,25},{25,17},{2,10},{10... | collective-permute-start | bytes 786440 | tf_op jit(solution)/shard_map/ppermute | solution.py:512
  68.1 13.7 %collective-permute-start.27 = (f32[512,128]{1,0:T(8,128)S(1)}, f32[512,128]{1,0:T(8,128)S(1)}, u32[]{:S(2)}, u32[]{:S(2)}) collective-permute-start(f32[512,128]{1,0:T(8,128)S(1)} %shard_map.163), channel_id=1, source_target_pairs={{0,16},{8,24},{16,0},{24,8},{1,17},{9,25},{17,1},{25,9},{2,18},{10... | collective-permute-start | bytes 786440 | tf_op jit(solution)/shard_map/ppermute | solution.py:512
  70.7 12.8 %collective-permute-start.28 = (f32[512,128]{1,0:T(8,128)S(1)}, f32[512,128]{1,0:T(8,128)S(1)}, u32[]{:S(2)}, u32[]{:S(2)}) collective-permute-start(f32[512,128]{1,0:T(8,128)S(1)} %shard_map.163), channel_id=1, source_target_pairs={{0,24},{8,16},{16,8},{24,0},{1,25},{9,17},{17,9},{25,1},{2,26},{10... | collective-permute-start | bytes 786440 | tf_op jit(solution)/shard_map/ppermute | solution.py:512
  83.6 2.7 %collective-permute-start.29 = (f32[512,128]{1,0:T(8,128)S(1)}, f32[512,128]{1,0:T(8,128)S(1)}, u32[]{:S(2)}, u32[]{:S(2)}) collective-permute-start(f32[512,128]{1,0:T(8,128)S(1)} %add_add_fusion.refs_4_), channel_id=1, source_target_pairs={{0,1},{1,0},{2,3},{3,2},{4,5},{5,4},{6,7},{7,6},{8,9},{9,8},{10,11... | collective-permute-start | bytes 786440 | tf_op jit(solution)/shard_map/ppermute | solution.py:512
  83.7 1.8 %collective-permute-start.30 = (f32[384,128]{1,0:T(8,128)S(1)}, f32[384,128]{1,0:T(8,128)S(1)}, u32[]{:S(2)}, u32[]{:S(2)}) collective-permute-start(f32[384,128]{1,0:T(8,128)S(1)} %get-tuple-element.44.refs_1_), channel_id=1, source_target_pairs={{0,1},{1,0},{2,3},{3,2},{4,5},{5,4},{6,7},{7,6},{8,9},{9,8},{10,11... | collective-permute-start | bytes 589832 | tf_op jit(solution)/shard_map/ppermute | solution.py:512
  84.2 1.6 %collective-permute-start.31 = (f32[384,128]{1,0:T(8,128)S(1)}, f32[384,128]{1,0:T(8,128)S(1)}, u32[]{:S(2)}, u32[]{:S(2)}) collective-permute-start(f32[384,128]{1,0:T(8,128)S(1)} %collective-permute-done.25.refs_14_), channel_id=1, source_target_pairs={{0,1},{1,0},{2,3},{3,2},{4,5},{5,4},{6,7},{7,6},{8,9},{9,8},{10,11... | collective-permute-start | bytes 589832 | tf_op jit(solution)/shard_map/ppermute | solution.py:512
  84.3 1.8 %collective-permute-start.33 = (f32[384,128]{1,0:T(8,128)S(1)}, f32[384,128]{1,0:T(8,128)S(1)}, u32[]{:S(2)}, u32[]{:S(2)}) collective-permute-start(f32[384,128]{1,0:T(8,128)S(1)} %collective-permute-done.32.refs_16_), channel_id=1, source_target_pairs={{0,1},{1,0},{2,3},{3,2},{4,5},{5,4},{6,7},{7,6},{8,9},{9,8},{10,11... | collective-permute-start | bytes 589832 | tf_op jit(solution)/shard_map/ppermute | solution.py:512
  84.7 1.6 %collective-permute-start.35 = (f32[384,128]{1,0:T(8,128)S(1)}, f32[384,128]{1,0:T(8,128)S(1)}, u32[]{:S(2)}, u32[]{:S(2)}) collective-permute-start(f32[384,128]{1,0:T(8,128)S(1)} %collective-permute-done.34.refs_18_), channel_id=1, source_target_pairs={{0,1},{1,0},{2,3},{3,2},{4,5},{5,4},{6,7},{7,6},{8,9},{9,8},{10,11... | collective-permute-start | bytes 589832 | tf_op jit(solution)/shard_map/ppermute | solution.py:512
  (3 other events, 8.7 us)

commit v3 on v2

--- a/solution.py
+++ b/solution.py
@@ -14,10 +14,13 @@
 KW = 512
 LAYERS = 2
 BITS = 30
+GROUP = 4
 CUTOFF = 8.0
 SPACING = CUTOFF / (NRBF - 1)
 CENTER = 0.5 * CUTOFF
-VMEM = 44 * 1024 * 1024
+ROOT = math.sqrt(0.5 * math.log2(math.e))
+VMEM = 30 * 1024 * 1024
+TABLE_SLOTS = 16
 WINDOW = 1e10
 F32 = jnp.float32
 BF16 = jnp.bfloat16
@@ -126,9 +129,7 @@
     )(ids, pair_blocks)
 
 
-def near_dots(tables, rows, sources):
-    number = len(sources)
-    values = [tables[i, rows, :] for i in range(number)]
+def value_dots(values, sources):
     highs = [v[:, :BS] for v in values]
     both = [b for b, _ in sources]
     low = [l for _, l in sources]
@@ -137,14 +138,22 @@
     )
 
 
+def near_dots(tables, rows, sources):
+    return value_dots([tables[i, rows, :] for i in range(len(sources))], sources)
+
+
 def add_terms(totals, cols, tables, sources, weight):
-    group = 4
     total = totals[:, cols]
-    for k in range(0, NRBF, group):
-        product = near_dots(tables, slice(k * BS, (k + group) * BS), sources)
-        for g in range(group):
-            total = total + product[g * BS : (g + 1) * BS] * weight[k + g : k + g + 1]
+    for k in range(0, NRBF, GROUP):
+        product = near_dots(tables, slice(k * BS, (k + GROUP) * BS), sources)
+        total = weigh(total, product, weight, k)
     totals[:, cols] = total
+
+
+def weigh(total, product, weight, k):
+    for g in range(GROUP):
+        total = total + product[g * BS : (g + 1) * BS] * weight[k + g : k + g + 1]
+    return total
 
 
 def one_or_two(step, count, act):
@@ -166,11 +175,39 @@
         def _():
             table_copy(table, step + 1, buffer, sems).start()
 
-        table_copy(table, step, buffer, sems).wait()
-        act(step, buffer.at[lax.rem(step, 2)])
+        act(step, buffer.at[lax.rem(step, 2)], table_copy(table, step, buffer, sems).wait)
         return carry
 
     lax.fori_loop(0, steps, one, 0)
+
+
+def resident_copies(count, table, held, sems):
+    steps = (count + 1) // 2
+    return [(steps >= back, table_copy(table, steps - back, held, sems)) for back in (1, 2)]
+
+
+def over_held_tables(count, table, held, buffer, sems, act):
+    steps = (count + 1) // 2
+    for back in (3, 4):
+        pl.when(steps >= back)(table_copy(table, steps - back, buffer, sems).start)
+
+    def resident(at, carry):
+        step = steps - 1 - at
+        act(step, held.at[lax.rem(step, 2)], lambda: None)
+        return carry
+
+    def one(at, carry):
+        step = steps - 1 - at
+        act(step, buffer.at[lax.rem(step, 2)], table_copy(table, step, buffer, sems).wait)
+
+        @pl.when(step >= 2)
+        def _():
+            table_copy(table, step - 2, buffer, sems).start()
+
+        return carry
+
+    lax.fori_loop(0, jnp.minimum(steps, 2), resident, 0)
+    lax.fori_loop(2, jnp.maximum(steps, 2), one, 0)
 
 
 def fill_tables(count, tables, act):
@@ -200,7 +237,13 @@
                 out(steps - back, *t).wait()
 
 
-def radial_tables(meta_ref, listed, at, near, pos_ref, masks_ref, radial_ref, over_ref):
+def block_views(packed, n_sub):
+    chips = n_sub // 2
+    height = packed[0].shape[0] // chips
+    return [packed[e % 2].at[e // 2 * height : (e // 2 + 1) * height, :] for e in range(n_sub)]
+
+
+def pair_geometry(meta_ref, listed, near, masks_ref):
     pair = meta_ref[1, listed]
     slot = meta_ref[2, listed]
     is_first = meta_ref[3, listed]
@@ -226,33 +269,40 @@
     source = jnp.zeros((8, BS), F32)
     for e in range(1, len(near)):
         source = jnp.where(slot == e, near[e][...], source)
-    mine = columns_of(pos_ref[...])
+    mine = columns_of(near[0][...])
     square = jnp.zeros((BS, BS), F32)
     for d in range(3):
         offset = source[d : d + 1, :] - mine[:, d : d + 1]
         square = square + offset * offset
     distance = jnp.sqrt(square + 1.0)
     inverse = 1.0 / distance
-    root = math.sqrt(0.5 * math.log2(math.e))
-    scaled = jnp.where(mask > 0.5, distance * (root / SPACING), 1.0e4)
-    for k in range(NRBF):
-        gap = scaled - k * root
+    return jnp.where(mask > 0.5, distance * (ROOT / SPACING), 1.0e4), inverse
+
+
+def fill_rows(shape, first, at, radial_ref, over_ref):
+    scaled, inverse = shape
+    kept = []
+    for k in range(first, first + GROUP):
+        gap = scaled - k * ROOT
         radial = jnp.exp2(-(gap * gap))
         rows = slice(k * BS, (k + 1) * BS)
         for ref, value in ((radial_ref, radial), (over_ref, radial * inverse)):
             high, low = split(value)
             ref[at, rows, 0:BS] = high
             ref[at, rows, BS : 2 * BS] = low
+        kept.append(jnp.concatenate([high, low], axis=1))
+    return jnp.concatenate(kept, axis=0)
 
 
 def early_kernel(n_sub, build, layer, meta_ref, *refs):
-    blocks, refs = [r.at[:BS, :] for r in refs[:n_sub]], refs[n_sub:]
-    places, refs = [r.at[r.shape[0] - 8 :, :] for r in refs[:n_sub]], refs[n_sub:]
+    blocks = [r.at[:BS, :] for r in block_views(refs[:2], n_sub)]
+    places = [r.at[BS:, :] for r in block_views(refs[2:4], n_sub)]
+    refs = refs[4:]
     if build:
-        in_ref, out_ref, filter_ref, masks_ref, partial_ref, phi_ref, tables_hbm = refs[:7]
-        sources, totals, over_buffer, over_sems, radial_buffer, radial_sems = refs[7:]
+        in_ref, out_ref, filter_ref, masks_ref, partial_ref, phi_ref, held, tables_hbm = refs[:8]
+        sources, totals, over_buffer, over_sems, held_sems = refs[8:]
     else:
-        in_ref, out_ref, filter_ref, tables_hbm, partial_ref, phi_ref, sources, totals, over_buffer, over_sems = refs
+        in_ref, out_ref, filter_ref, tables_hbm, partial_ref, phi_ref, held, sources, totals, over_buffer, over_sems, held_sems = refs
     radial_hbm, over_hbm = tables_hbm.at[0], tables_hbm.at[1]
     count = meta_ref[0, 0]
     if not build:
@@ -260,6 +310,9 @@
         @pl.when(count > 0)
         def _():
             table_copy(over_hbm, 0, over_buffer, over_sems).start()
+
+        for there, copy in resident_copies(count, radial_hbm, held, held_sems):
+            pl.when(there)(copy.start)
 
     totals[...] = jnp.zeros_like(totals)
     scalars = jnp.concatenate([blocks[e][...] for e in range(1, n_sub)], axis=0)
@@ -281,34 +334,45 @@
     weight = filter_ref[layer, :, 2 * BS :]
     weight = jnp.concatenate([weight, weight], axis=1)
 
-    def terms(step, table, number):
-        slot = [meta_ref[2, 2 * step + i] - 1 for i in range(number)]
-        for tile in range(2):
-            cols = slice(tile * 2 * BS, (tile + 1) * 2 * BS)
-            near = [(sources[e, : 2 * BS, cols], sources[e, 2 * BS :, cols]) for e in slot]
-            add_terms(totals, cols, table, near, weight)
+    def near_sources(step, number, tile):
+        cols = slice(tile * 2 * BS, (tile + 1) * 2 * BS)
+        slots = [meta_ref[2, 2 * step + i] - 1 for i in range(number)]
+        return [(sources[e, : 2 * BS, cols], sources[e, 2 * BS :, cols]) for e in slots]
 
     if build:
 
+        def terms(step, tables, number):
+            shapes = [pair_geometry(meta_ref, 2 * step + i, places, masks_ref) for i in range(number)]
+            near = [near_sources(step, number, tile) for tile in range(2)]
+            both = [totals[:, tile * 2 * BS : (tile + 1) * 2 * BS] for tile in range(2)]
+            for k in range(0, NRBF, GROUP):
+                over = [fill_rows(shape, k, i, *tables) for i, shape in enumerate(shapes)]
+                for tile in range(2):
+                    product = value_dots(over, near[tile])
+                    both[tile] = weigh(both[tile], product, weight, k)
+            for tile in range(2):
+                totals[:, tile * 2 * BS : (tile + 1) * 2 * BS] = both[tile]
+
         def act(step, tables):
-            radial, over = tables
-
-            def both(number):
-                for i in range(number):
-                    radial_tables(meta_ref, 2 * step + i, i, places, places[0], masks_ref, radial, over)
-                terms(step, over, number)
-
-            one_or_two(step, count, both)
+            one_or_two(step, count, functools.partial(terms, step, tables))
 
         fill_tables(
-            count, ((radial_hbm, radial_buffer, radial_sems), (over_hbm, over_buffer, over_sems)), act
+            count, ((radial_hbm, held, held_sems), (over_hbm, over_buffer, over_sems)), act
         )
     else:
 
-        def act(step, table):
-            one_or_two(step, count, functools.partial(terms, step, table))
+        def terms(step, table, ready, number):
+            ready()
+            for tile in range(2):
+                cols = slice(tile * 2 * BS, (tile + 1) * 2 * BS)
+                add_terms(totals, cols, table, near_sources(step, number, tile), weight)
+
+        def act(step, table, ready):
+            one_or_two(step, count, functools.partial(terms, step, table, ready))
 
         over_tables(count, over_hbm, over_buffer, over_sems, act)
+        for there, copy in resident_copies(count, radial_hbm, held, held_sems):
+            pl.when(there)(copy.wait)
 
     mine = columns_of(places[0][...])
     for d in range(3):
@@ -321,24 +385,25 @@
     return [pltpu.VMEM((2, 2, NRBF * BS, 2 * BS), BF16), pltpu.SemaphoreType.DMA((2,))] * number
 
 
-def early_terms(meta, layer, blocks, spots, weights, masks=None, tables=None):
-    n_sub = len(blocks)
+def early_terms(meta, layer, n_sub, blocks, spots, weights, masks=None, tables=None):
     slots = meta.shape[1]
     build = tables is None
-    shape = jax.ShapeDtypeStruct((2, slots, NRBF * BS, 2 * BS), BF16)
+    shape = jax.ShapeDtypeStruct((2, max(slots, TABLE_SLOTS), NRBF * BS, 2 * BS), BF16)
     out_shape = [
         jax.ShapeDtypeStruct((3 * BS, BS), F32),
         jax.ShapeDtypeStruct((n_sub - 1, BS, 2 * BS), F32),
+        jax.ShapeDtypeStruct((2, 2, NRBF * BS, 2 * BS), BF16),
     ]
     return pl.pallas_call(
         functools.partial(early_kernel, n_sub, build, layer),
-        in_specs=[SMEM_SPEC] + [VMEM_SPEC] * (2 * n_sub + 3) + [VMEM_SPEC if build else HBM_SPEC],
-        out_specs=[VMEM_SPEC] * 2 + ([HBM_SPEC] if build else []),
+        in_specs=[SMEM_SPEC] + [VMEM_SPEC] * 7 + [VMEM_SPEC if build else HBM_SPEC],
+        out_specs=[VMEM_SPEC] * 3 + ([HBM_SPEC] if build else []),
         scratch_shapes=[
             pltpu.VMEM((n_sub - 1, 3 * BS, 4 * BS), BF16),
             pltpu.VMEM((BS, 4 * BS), F32),
         ]
-        + table_buffers(2 if build else 1),
+        + table_buffers(1)
+        + [pltpu.SemaphoreType.DMA((2,))],
         out_shape=out_shape + ([shape] if build else []),
         compiler_params=pltpu.CompilerParams(vmem_limit_bytes=VMEM),
         cost_estimate=cost(3 * 4 * NRBF * BS * BS * 4 * BS * 2 * 3, 10e6),
@@ -368,8 +433,8 @@
 def structure_kernel(n_sub, build, layer, *refs):
     if build:
         meta_ref, waves_ref, refs = refs[0], refs[1], refs[2:]
-        places = [r.at[r.shape[0] - 8 :, :] for r in refs[:n_sub]]
-    blocks, refs = [r.at[:BS, :] for r in refs[:n_sub]], refs[n_sub:]
+        places = [r.at[BS:, :] for r in block_views(refs[:2], n_sub)]
+    blocks, refs = [r.at[:BS, :] for r in block_views(refs[:2], n_sub)], refs[2:]
     atoms = n_sub * BS
     if build:
         weight_ref, out_ref, trig_ref = refs
@@ -393,16 +458,15 @@
     out_ref[...] = dot3(total, weight_ref[layer])
 
 
-def structure(layer, blocks, weight, meta=None, waves=None, region_trig=None):
-    n_sub = len(blocks)
+def structure(layer, n_sub, blocks, weight, meta=None, waves=None, region_trig=None):
     build = region_trig is None
     out_shape = [jax.ShapeDtypeStruct((KW, BS), F32)]
     if build:
-        in_specs = [SMEM_SPEC] + [VMEM_SPEC] * (n_sub + 2)
+        in_specs = [SMEM_SPEC] + [VMEM_SPEC] * 4
         operands = (meta, waves, *blocks, weight)
         out_shape += [jax.ShapeDtypeStruct((KW, 2 * n_sub * BS), BF16)]
     else:
-        in_specs = [VMEM_SPEC] * (n_sub + 2)
+        in_specs = [VMEM_SPEC] * 4
         operands = (*blocks, weight, region_trig)
     return pl.pallas_call(
         functools.partial(structure_kernel, n_sub, build, layer),
@@ -414,24 +478,19 @@
     )(*operands)
 
 
-def late_kernel(scale, n_sub, layer, last, meta_ref, *refs):
-    scalars_ref, vectors_ref, phi_ref, partial_ref, mine_ref, other_ref, own_ref = refs[:7]
-    factor_ref, filter_ref, left_ref, right_ref, gate_in_ref, gate_out_ref = refs[7:13]
-    near, refs = refs[13 : 12 + n_sub], refs[12 + n_sub :]
-    radial_hbm, refs = refs[0].at[0], refs[1:]
-    outs, (totals, buffer, sems) = refs[:-3], refs[-3:]
+def late_kernel(n_sub, layer, meta_ref, *refs):
+    phi_ref, partial_ref, filter_ref = refs[:3]
+    near, refs = refs[3 : 2 + n_sub], refs[2 + n_sub :]
+    tables_hbm, held, totals, buffer, sems = refs
+    radial_hbm = tables_hbm.at[0]
     count = meta_ref[0, 0]
-
-    @pl.when(count > 0)
-    def _():
-        table_copy(radial_hbm, 0, buffer, sems).start()
 
     totals[:, :BS] = jnp.zeros((BS, BS), F32)
     for d in range(3):
         totals[:, (1 + d) * BS : (2 + d) * BS] = partial_ref[d * BS : (d + 1) * BS, :]
     w_s, w_v = filter_ref[layer, :, :BS], filter_ref[layer, :, BS : 2 * BS]
 
-    def terms(step, table, number):
+    def terms(step, table, ready, number):
         parts = []
         for i in range(number):
             slot = meta_ref[2, 2 * step + i]
@@ -441,16 +500,37 @@
             phi = phi_ref[slot - 1]
             phi_s, phi_v = phi[:, :BS], phi[:, BS:]
             parts.append([phi_s] + [phi_v * vectors[d * BS : (d + 1) * BS, :] for d in range(3)])
+        sources = [
+            [stacked(jnp.concatenate(p[2 * tile : 2 * tile + 2], axis=1)) for p in parts] for tile in range(2)
+        ]
+        ready()
         for tile, names in enumerate(((w_s, w_v), (w_v, w_v))):
             cols = slice(tile * 2 * BS, (tile + 1) * 2 * BS)
-            sources = [stacked(jnp.concatenate(p[2 * tile : 2 * tile + 2], axis=1)) for p in parts]
-            add_terms(totals, cols, table, sources, jnp.concatenate(names, axis=1))
-
-    def act(step, table):
-        one_or_two(step, count, functools.partial(terms, step, table))
-
-    over_tables(count, radial_hbm, buffer, sems, act)
-
+            add_terms(totals, cols, table, sources[tile], jnp.concatenate(names, axis=1))
+
+    def act(step, table, ready):
+        one_or_two(step, count, functools.partial(terms, step, table, ready))
+
+    over_held_tables(count, radial_hbm, held, buffer, sems, act)
+
+
+def late_terms(meta, layer, phi, near, tables, held, partial, weight):
+    n_sub = len(near)
+    return pl.pallas_call(
+        functools.partial(late_kernel, n_sub, layer),
+        in_specs=[SMEM_SPEC] + [VMEM_SPEC] * (2 + n_sub) + [HBM_SPEC, VMEM_SPEC],
+        out_specs=VMEM_SPEC,
+        scratch_shapes=table_buffers(1),
+        out_shape=jax.ShapeDtypeStruct((BS, 4 * BS), F32),
+        compiler_params=pltpu.CompilerParams(vmem_limit_bytes=VMEM),
+        cost_estimate=cost(3 * 4 * NRBF * BS * BS * 4 * BS * 2 * 3, 10e6),
+    )(meta, phi, partial, weight, *near[1:], tables, held)
+
+
+def update_kernel(scale, layer, last, meta_ref, *refs):
+    scalars_ref, vectors_ref, totals, mine_ref, other_ref, own_ref = refs[:6]
+    factor_ref, left_ref, right_ref, gate_in_ref, gate_out_ref = refs[6:11]
+    outs = refs[11:]
     lower = meta_ref[4, 0] == 0
     mine, other = mine_ref[...], other_ref[...]
     half = mine.shape[0] // 2
@@ -493,18 +573,16 @@
             outs[1][p, :] = new_vectors[d]
 
 
-def late_terms(meta, layer, last, scale, scalars, vectors, phi, near, tables, partial, mine, other, own, weights):
-    n_sub = len(near)
+def update(meta, layer, last, scale, scalars, vectors, totals, mine, other, own, weights):
     shapes = [(BS, BS), (3, BS, BS)] if last else [(BS, BS), (3 * BS, BS)]
     return pl.pallas_call(
-        functools.partial(late_kernel, scale, n_sub, layer, last),
-        in_specs=[SMEM_SPEC] + [VMEM_SPEC] * (12 + n_sub) + [HBM_SPEC],
+        functools.partial(update_kernel, scale, layer, last),
+        in_specs=[SMEM_SPEC] + [VMEM_SPEC] * 11,
         out_specs=[VMEM_SPEC] * len(shapes),
-        scratch_shapes=[pltpu.VMEM((BS, 4 * BS), F32)] + table_buffers(1),
         out_shape=[jax.ShapeDtypeStruct(shape, F32) for shape in shapes],
         compiler_params=pltpu.CompilerParams(vmem_limit_bytes=VMEM),
-        cost_estimate=cost(3 * 4 * NRBF * BS * BS * 4 * BS * 2 * 3, 10e6),
-    )(meta, scalars, vectors, phi, partial, mine, other, own, *weights, *near[1:], tables)
+        cost_estimate=cost(3e9, 4e6),
+    )(meta, scalars, vectors, totals, mine, other, own, *weights)
 
 
 def exchange(x, axis, mask):
@@ -512,16 +590,12 @@
     return lax.ppermute(x, axis, [(i, i ^ mask) for i in range(size)])
 
 
-def gather(x, first=()):
-    n_sub = lax.axis_size("sub")
-    parts = [None] * n_sub
-    for e in range(0, n_sub, 2):
-        parts[e] = x if e == 0 else exchange(x, "sub", e)
-    if first:
-        parts[::2] = lax.optimization_barrier((*parts[::2], *first))[: len(parts[::2])]
-    for e in range(0, n_sub, 2):
-        parts[e + 1] = exchange(parts[e], "sub", 1)
-    return parts
+def from_chips(x):
+    return [x] + [exchange(x, "sub", e) for e in range(2, lax.axis_size("sub"), 2)]
+
+
+def both_cores(parts):
+    return [p for pair in zip(parts, [exchange(p, "sub", 1) for p in parts]) for p in pair]
 
 
 def after(x, *others):
@@ -560,33 +634,35 @@
     tables = region_trig = spots = None
     for layer in range(LAYERS):
         last = layer == LAYERS - 1
-        blocks = gather(lean, (meta, own_trig) if layer == 0 else ())
-        near = gather(after(vectors, *blocks[2::2]))
-        near[0] = vectors
+        scalar_parts = from_chips(lean)
+        if layer == 0:
+            scalar_parts = lax.optimization_barrier((*scalar_parts, meta, own_trig))[:-2]
+        packed = jnp.concatenate(scalar_parts, axis=0)
+        blocks = (packed, exchange(packed, "sub", 1))
+        vector_parts = from_chips(after(vectors, scalar_parts[1]))
+        near = both_cores(vector_parts)
         if layer == 0:
             spots = blocks
-            partial, region_trig = structure(layer, blocks, ewald_weight, meta, wavevectors)
+            partial, region_trig = structure(layer, n_sub, blocks, ewald_weight, meta, wavevectors)
         else:
-            (partial,) = structure(layer, blocks, ewald_weight, region_trig=region_trig)
+            (partial,) = structure(layer, n_sub, blocks, ewald_weight, region_trig=region_trig)
         others = [exchange(partial, "region", mask) for mask in range(1, n_region)]
         weights = (message_in, message_out, filter_weight)
         turn = after(meta, partial, *near[2:3])
         if layer == 0:
-            along, phi, tables = early_terms(turn, layer, blocks, spots, weights, masks=pair_mask)
+            along, phi, held, tables = early_terms(turn, layer, n_sub, blocks, spots, weights, masks=pair_mask)
         else:
-            along, phi = early_terms(turn, layer, blocks, spots, weights, tables=tables)
-        *others, along = lax.optimization_barrier((*others, along))
+            along, phi, held = early_terms(turn, layer, n_sub, blocks, spots, weights, tables=tables)
+        others = lax.optimization_barrier((*others, along))[:-1]
         mine = sum(others, partial)
         theirs = exchange(mine, "sub", 1)
-        results = late_terms(
-            meta, layer, last, scale, scalars, vectors, phi, near, tables, along, mine, theirs, own_trig,
-            (ewald_filter, filter_weight, mixing_left, mixing_right, update_in, update_out),
+        totals = late_terms(meta, layer, phi, near, tables, held, along, filter_weight)
+        results = update(
+            meta, layer, last, scale, scalars, vectors, totals, mine, theirs, own_trig,
+            (ewald_filter, mixing_left, mixing_right, update_in, update_out),
         )
-        if last:
-            scalars, vectors = results
-        else:
-            scalars, vectors = results
-            lean = scalars
+        scalars, vectors = results
+        lean = scalars
     return scalars, vectors
 
 

time: 96.5 us -> 87 us (0.902)
  Pallas kernels: 49.2 us -> 36.9 us
  starting transfers between devices: 30.8 us -> 36.4 us
  waiting for transfers between devices: 12.5 us -> 9.31 us
    pallas_call x2 -> x4, Pallas kernels: 20 us -> 13.5 us  [the longest x2 9.49 us: late_terms(): pl.pallas_call(functools.partial(late_kernel, n_sub, layer), in_specs=[SM...]
    pallas_call x2, Pallas kernels: 22.5 us -> 16.8 us  [early_terms(): pl.pallas_call(functools.partial(early_kernel, n_sub, build, layer), in_s...]
    ppermute x36 -> x30, starting transfers between devices: 30.8 us -> 36.4 us  [exchange(): return lax.ppermute(x, axis, [(i, i ^ mask) for i in range(size)])]
    ppermute x36 -> x30, waiting for transfers between devices: 12.5 us -> 9.31 us  [exchange(): return lax.ppermute(x, axis, [(i, i ^ mask) for i in range(size)])]
  transfers between devices with their start and end apart: 36 -> 30, of which waited for: 15 -> 12; matrix products, arithmetic and copies ran while one was open for 1% -> 1% of each run, Pallas kernels for 30% -> 38%
where the time goes in v3:
time: 87 us; the launch traced here: 86.6 us
  Pallas kernels  36.9 us (42%)
  starting transfers between devices  36.4 us (42%)
  waiting for transfers between devices  9.31 us (11%)
  other arithmetic  1.55 us (2%)
  local copies, waits for them, and re-layouts  1.5 us (2%)
  between operations  0.98 us (1%)
    ppermute x30, starting transfers between devices, exchange(): return lax.ppermute(x, axis, [(i, i ^ mask) for i in range(size)])  36.4 us
    pallas_call x2, Pallas kernels, early_terms(): pl.pallas_call(functools.partial(early_kernel, n_sub, build, layer), in_s...  16.8 us
    pallas_call x2, Pallas kernels, late_terms(): pl.pallas_call(functools.partial(late_kernel, n_sub, layer), in_specs=[SM...  9.49 us
    ppermute x30, waiting for transfers between devices, exchange(): return lax.ppermute(x, axis, [(i, i ^ mask) for i in range(size)])  9.31 us
    pallas_call x2, Pallas kernels, structure(): pl.pallas_call(functools.partial(structure_kernel, n_sub, build, layer),...  4.68 us
    pallas_call x2, Pallas kernels, update(): pl.pallas_call(functools.partial(update_kernel, scale, layer, last), in_s...  3.97 us
  transfers between devices with their start and end apart: 30, of which 12 were waited for; matrix products, arithmetic and copies ran while one was open for 1% of the time, Pallas kernels for 38%

profile of v3, /device:TPU:0, one launch (start us, length us, event | category | flops | bytes accessed | tf_op | source)
XLA Modules:
  0.0 86.6 jit_solution(17101564368808927003)
XLA Ops:
  0.6 0.9 select_maximum_fusion.place_ref
  1.5 3.0 %collective-permute-start = (f32[136,128]{1,0:T(8,128)S(1)}, f32[136,128]{1,0:T(8,128)S(1)}, u32[]{:S(2)}, u32[]{:S(2)}) collective-permute-start(f32[136,128]{1,0:T(8,128)S(1)} %select_maximum_fusion.place_ref), channel_id=1, source_target_pairs={{0,2},{1,3},{2,0},{3,1},{4,6},{5,7},{6,4},{7,5},{8,10},{9,11},{10,... | collective-permute-start | bytes 208904 | tf_op jit(solution)/shard_map/ppermute | solution.py:590
  4.5 2.6 %collective-permute-start.1 = (f32[136,128]{1,0:T(8,128)S(1)}, f32[136,128]{1,0:T(8,128)S(1)}, u32[]{:S(2)}, u32[]{:S(2)}) collective-permute-start(f32[136,128]{1,0:T(8,128)S(1)} %select_maximum_fusion.place_ref), channel_id=1, source_target_pairs={{0,4},{1,5},{2,6},{3,7},{4,0},{5,1},{6,2},{7,3},{8,12},{9,13},{10,... | collective-permute-start | bytes 208904 | tf_op jit(solution)/shard_map/ppermute | solution.py:590
  7.1 0.7 copy-done.12
  7.9 0.5 shard_map.159.refs_5_
  8.4 0.6 pad_add_fusion.ids_ref
  8.9 1.5 %shard_map.158.refs_0_.meta_ref = s32[5,8]{1,0:T(8,128)} custom-call(s32[2]{0:T(128)} %pad_add_fusion.ids_ref, s32[2,48]{1,0:T(2,128)} %pairs_ref.1), custom_call_target="tpu_custom_call" | custom-call | tf_op jit(solution)/shard_map/pallas_call | solution.py:124
  10.4 1.6 %collective-permute-done.1 = f32[136,128]{1,0:T(8,128)S(1)} collective-permute-done((f32[136,128]{1,0:T(8,128)S(1)}, f32[136,128]{1,0:T(8,128)S(1)}, u32[]{:S(2)}, u32[]{:S(2)}) %collective-permute-start.1) | collective-permute-done | bytes 69664 | tf_op jit(solution)/shard_map/ppermute | solution.py:590
  12.0 1.3 %collective-permute-done.2 = f32[136,128]{1,0:T(8,128)S(1)} collective-permute-done((f32[136,128]{1,0:T(8,128)S(1)}, f32[136,128]{1,0:T(8,128)S(1)}, u32[]{:S(2)}, u32[]{:S(2)}) %collective-permute-start.2) | collective-permute-done | bytes 69664 | tf_op jit(solution)/shard_map/ppermute | solution.py:590
  13.5 0.8 collective-permute-start.4
  14.3 1.8 %collective-permute-start.7 = (f32[384,128]{1,0:T(8,128)S(1)}, f32[384,128]{1,0:T(8,128)S(1)}, u32[]{:S(2)}, u32[]{:S(2)}) collective-permute-start(f32[384,128]{1,0:T(8,128)S(1)} %bitcast.4), channel_id=1, source_target_pairs={{0,4},{1,5},{2,6},{3,7},{4,0},{5,1},{6,2},{7,3},{8,12},{9,13},{10,... | collective-permute-start | bytes 589832 | tf_op jit(solution)/shard_map/ppermute | solution.py:590
  16.1 1.9 %collective-permute-start.9 = (f32[384,128]{1,0:T(8,128)S(1)}, f32[384,128]{1,0:T(8,128)S(1)}, u32[]{:S(2)}, u32[]{:S(2)}) collective-permute-start(f32[384,128]{1,0:T(8,128)S(1)} %bitcast.5), channel_id=1, source_target_pairs={{0,6},{1,7},{2,4},{3,5},{4,2},{5,3},{6,0},{7,1},{8,14},{9,15},{10,... | collective-permute-start | bytes 589832 | tf_op jit(solution)/shard_map/ppermute | solution.py:590
  18.0 0.7 copy-done.2
  18.7 3.4 %shard_map.160 = (f32[512,128]{1,0:T(8,128)S(1)}, bf16[512,2048]{1,0:T(8,128)(2,1)S(1)}) custom-call(s32[5,8]{1,0:T(8,128)S(1)} %copy-done.2, f32[3,512]{1,0:T(4,128)S(1)} %copy-done.13, f32[544,128]{1,0:T(8,128)S(1)} %constant_dynamic-update-slice_fusion.refs_2_.refs_0_, f32[544,128]{1,0:T(8,128)S(1)} %collective-permute-done.3.refs_3_.refs_1_, ...), custom_call_target="tpu_custom_call" | custom-call | flops 402653184 | bytes 4000000 | tf_op jit(solution)/shard_map/pallas_call | solution.py:471
  22.1 1.6 %collective-permute-start.11 = (f32[512,128]{1,0:T(8,128)S(1)}, f32[512,128]{1,0:T(8,128)S(1)}, u32[]{:S(2)}, u32[]{:S(2)}) collective-permute-start(f32[512,128]{1,0:T(8,128)S(1)} %get-tuple-element.31), channel_id=1, source_target_pairs={{0,8},{8,0},{16,24},{24,16},{1,9},{9,1},{17,25},{25,17},{2,10},{10... | collective-permute-start | bytes 786440 | tf_op jit(solution)/shard_map/ppermute | solution.py:590
  23.7 1.5 %collective-permute-start.12 = (f32[512,128]{1,0:T(8,128)S(1)}, f32[512,128]{1,0:T(8,128)S(1)}, u32[]{:S(2)}, u32[]{:S(2)}) collective-permute-start(f32[512,128]{1,0:T(8,128)S(1)} %get-tuple-element.31), channel_id=1, source_target_pairs={{0,16},{8,24},{16,0},{24,8},{1,17},{9,25},{17,1},{25,9},{2,18},{10... | collective-permute-start | bytes 786440 | tf_op jit(solution)/shard_map/ppermute | solution.py:590
  25.2 1.8 %collective-permute-start.13 = (f32[512,128]{1,0:T(8,128)S(1)}, f32[512,128]{1,0:T(8,128)S(1)}, u32[]{:S(2)}, u32[]{:S(2)}) collective-permute-start(f32[512,128]{1,0:T(8,128)S(1)} %get-tuple-element.31), channel_id=1, source_target_pairs={{0,24},{8,16},{16,8},{24,0},{1,25},{9,17},{17,9},{25,1},{2,26},{10... | collective-permute-start | bytes 786440 | tf_op jit(solution)/shard_map/ppermute | solution.py:590
  26.9 9.2 %shard_map.161 = (f32[384,128]{1,0:T(8,128)S(1)}, f32[7,128,256]{2,1,0:T(8,128)S(1)}, bf16[2,2,2560,256]{3,2,1,0:T(8,128)(2,1)S(1)}, bf16[2,16,2560,256]{3,2,1,0:T(8,128)(2,1)}) custom-call(s32[5,8]{1,0:T(8,128)S(1)} %copy-done.2, f32[544,128]{1,0:T(8,128)S(1)} %constant_dynamic-update-slice_fusion.refs_2_.refs_0_, ...), custom_call_target="tpu_custom_call" | custom-call | flops 12079595520 | bytes 10000000 | tf_op jit(solution)/shard_map/pallas_call | solution.py:397
  36.2 0.5 collective-permute-start.6
  36.8 0.4 collective-permute-start.10
  37.3 0.2 collective-permute-start.14
  37.5 0.2 collective-permute-done.5.refs_3_
  37.7 0.3 collective-permute-done.6.refs_5_
  37.9 0.3 collective-permute-done.8.refs_7_
  38.2 0.3 collective-permute-done.10.refs_9_
  38.5 4.8 %shard_map.162.refs_2_ = f32[128,512]{1,0:T(8,128)S(1)} custom-call(s32[5,8]{1,0:T(8,128)S(1)} %copy-done.2, f32[7,128,256]{2,1,0:T(8,128)S(1)} %get-tuple-element.34.refs_0_, f32[384,128]{1,0:T(8,128)S(1)} %get-tuple-element.35.refs_1_, f32[2,20,384]{2,1,0:T(8,128)S(1)} %copy.17.refs_6_.refs_2_, f32[384,128]{1,0:T(8,128)S(1)} %collective-permute-done.5.refs_3_, ...), custom_call_target="tpu_custom_call" | custom-call | flops 12079595520 | bytes 10000000 | tf_op jit(solution)/shard_map/pallas_call | solution.py:519
  43.5 1.7 %shard_map.163 = (f32[128,128]{1,0:T(8,128)S(1)}, f32[384,128]{1,0:T(8,128)S(1)}) custom-call(s32[5,8]{1,0:T(8,128)S(1)} %copy-done.2, f32[128,128]{1,0:T(8,128)S(1)} %copy-done.1, f32[384,128]{1,0:T(8,128)S(1)} %bitcast.7, f32[128,512]{1,0:T(8,128)S(1)} %shard_map.162.refs_2_, f32[512,128]{1,0:T(8,128)S(1)} %add_add_fusion.1.refs_3_, ...), custom_call_target="tpu_custom_call" | custom-call | flops 3000000000 | bytes 4000000 | tf_op jit(solution)/shard_map/pallas_call | solution.py:578
  45.2 2.3 %collective-permute-start.16 = (f32[128,128]{1,0:T(8,128)S(1)}, f32[128,128]{1,0:T(8,128)S(1)}, u32[]{:S(2)}, u32[]{:S(2)}) collective-permute-start(f32[128,128]{1,0:T(8,128)S(1)} %get-tuple-element.41.refs_0_), channel_id=1, source_target_pairs={{0,4},{1,5},{2,6},{3,7},{4,0},{5,1},{6,2},{7,3},{8,12},{9,13},{10,... | collective-permute-start | bytes 196616 | tf_op jit(solution)/shard_map/ppermute | solution.py:590
  47.5 2.1 %collective-permute-start.17 = (f32[128,128]{1,0:T(8,128)S(1)}, f32[128,128]{1,0:T(8,128)S(1)}, u32[]{:S(2)}, u32[]{:S(2)}) collective-permute-start(f32[128,128]{1,0:T(8,128)S(1)} %get-tuple-element.41.refs_0_), channel_id=1, source_target_pairs={{0,6},{1,7},{2,4},{3,5},{4,2},{5,3},{6,0},{7,1},{8,14},{9,15},{10,... | collective-permute-start | bytes 196616 | tf_op jit(solution)/shard_map/ppermute | solution.py:590
  49.6 0.8 collective-permute-done.15
  50.4 3.5 %collective-permute-done.16 = f32[128,128]{1,0:T(8,128)S(1)} collective-permute-done((f32[128,128]{1,0:T(8,128)S(1)}, f32[128,128]{1,0:T(8,128)S(1)}, u32[]{:S(2)}, u32[]{:S(2)}) %collective-permute-start.16) | collective-permute-done | bytes 65568 | tf_op jit(solution)/shard_map/ppermute | solution.py:590
  54.0 1.2 %collective-permute-start.19 = (f32[384,128]{1,0:T(8,128)S(1)}, f32[384,128]{1,0:T(8,128)S(1)}, u32[]{:S(2)}, u32[]{:S(2)}) collective-permute-start(f32[384,128]{1,0:T(8,128)S(1)} %get-tuple-element.44.refs_1_), channel_id=1, source_target_pairs={{0,2},{1,3},{2,0},{3,1},{4,6},{5,7},{6,4},{7,5},{8,10},{9,11},{10,... | collective-permute-start | bytes 589832 | tf_op jit(solution)/shard_map/ppermute | solution.py:590
  55.3 1.3 %collective-permute-start.22 = (f32[384,128]{1,0:T(8,128)S(1)}, f32[384,128]{1,0:T(8,128)S(1)}, u32[]{:S(2)}, u32[]{:S(2)}) collective-permute-start(f32[384,128]{1,0:T(8,128)S(1)} %get-tuple-element.44.refs_1_), channel_id=1, source_target_pairs={{0,4},{1,5},{2,6},{3,7},{4,0},{5,1},{6,2},{7,3},{8,12},{9,13},{10,... | collective-permute-start | bytes 589832 | tf_op jit(solution)/shard_map/ppermute | solution.py:590
  56.6 1.9 %collective-permute-start.24 = (f32[384,128]{1,0:T(8,128)S(1)}, f32[384,128]{1,0:T(8,128)S(1)}, u32[]{:S(2)}, u32[]{:S(2)}) collective-permute-start(f32[384,128]{1,0:T(8,128)S(1)} %get-tuple-element.44.refs_1_), channel_id=1, source_target_pairs={{0,6},{1,7},{2,4},{3,5},{4,2},{5,3},{6,0},{7,1},{8,14},{9,15},{10,... | collective-permute-start | bytes 589832 | tf_op jit(solution)/shard_map/ppermute | solution.py:590
  58.5 1.3 %shard_map.164 = f32[512,128]{1,0:T(8,128)S(1)} custom-call(f32[512,128]{1,0:T(8,128)S(1)} %constant_dynamic-update-slice_fusion.4.refs_0_, f32[512,128]{1,0:T(8,128)S(1)} %collective-permute-done.18.refs_1_, f32[2,128,128]{2,1,0:T(8,128)S(1)} %copy-done, bf16[512,2048]{1,0:T(8,128)(2,1)S(1)} %get-tuple-element.43.refs_3_), custom_call_target="tpu_custom_call" | custom-call | flops 402653184 | bytes 4000000 | tf_op jit(solution)/shard_map/pallas_call | solution.py:471
  59.8 2.9 %collective-permute-start.26 = (f32[512,128]{1,0:T(8,128)S(1)}, f32[512,128]{1,0:T(8,128)S(1)}, u32[]{:S(2)}, u32[]{:S(2)}) collective-permute-start(f32[512,128]{1,0:T(8,128)S(1)} %shard_map.164), channel_id=1, source_target_pairs={{0,8},{8,0},{16,24},{24,16},{1,9},{9,1},{17,25},{25,17},{2,10},{10... | collective-permute-start | bytes 786440 | tf_op jit(solution)/shard_map/ppermute | solution.py:590
  62.7 2.6 %collective-permute-start.27 = (f32[512,128]{1,0:T(8,128)S(1)}, f32[512,128]{1,0:T(8,128)S(1)}, u32[]{:S(2)}, u32[]{:S(2)}) collective-permute-start(f32[512,128]{1,0:T(8,128)S(1)} %shard_map.164), channel_id=1, source_target_pairs={{0,16},{8,24},{16,0},{24,8},{1,17},{9,25},{17,1},{25,9},{2,18},{10... | collective-permute-start | bytes 786440 | tf_op jit(solution)/shard_map/ppermute | solution.py:590
  65.3 4.4 %collective-permute-start.28 = (f32[512,128]{1,0:T(8,128)S(1)}, f32[512,128]{1,0:T(8,128)S(1)}, u32[]{:S(2)}, u32[]{:S(2)}) collective-permute-start(f32[512,128]{1,0:T(8,128)S(1)} %shard_map.164), channel_id=1, source_target_pairs={{0,24},{8,16},{16,8},{24,0},{1,25},{9,17},{17,9},{25,1},{2,26},{10... | collective-permute-start | bytes 786440 | tf_op jit(solution)/shard_map/ppermute | solution.py:590
  69.7 7.6 %shard_map.165 = (f32[384,128]{1,0:T(8,128)S(1)}, f32[7,128,256]{2,1,0:T(8,128)S(1)}, bf16[2,2,2560,256]{3,2,1,0:T(8,128)(2,1)S(1)}) custom-call(s32[5,8]{1,0:T(8,128)S(1)} %copy-done.2, f32[512,128]{1,0:T(8,128)S(1)} %constant_dynamic-update-slice_fusion.4.refs_0_, f32[512,128]{1,0:T(8,128)S(1)} %collective-permute-done.18.refs_1_, ...), custom_call_target="tpu_custom_call" | custom-call | flops 12079595520 | bytes 10000000 | tf_op jit(solution)/shard_map/pallas_call | solution.py:397
  77.4 0.5 collective-permute-start.21
  78.0 0.4 collective-permute-start.25
  78.5 0.1 collective-permute-start.29
  78.6 0.2 collective-permute-done.20.refs_3_
  78.8 0.3 collective-permute-done.21.refs_5_
  79.1 0.3 collective-permute-done.23.refs_7_
  79.4 0.3 collective-permute-done.25.refs_9_
  79.6 4.6 %shard_map.166.refs_2_ = f32[128,512]{1,0:T(8,128)S(1)} custom-call(s32[5,8]{1,0:T(8,128)S(1)} %copy-done.2, f32[7,128,256]{2,1,0:T(8,128)S(1)} %get-tuple-element.46.refs_0_, f32[384,128]{1,0:T(8,128)S(1)} %get-tuple-element.47.refs_1_, f32[2,20,384]{2,1,0:T(8,128)S(1)} %copy.17.refs_6_.refs_2_, f32[384,128]{1,0:T(8,128)S(1)} %collective-permute-done.20.refs_3_, ...), custom_call_target="tpu_custom_call" | custom-call | flops 12079595520 | bytes 10000000 | tf_op jit(solution)/shard_map/pallas_call | solution.py:519
  84.3 2.3 %shard_map.167 = (f32[128,128]{1,0:T(8,128)}, f32[3,128,128]{2,1,0:T(8,128)}) custom-call(s32[5,8]{1,0:T(8,128)S(1)} %copy-done.2, f32[128,128]{1,0:T(8,128)S(1)} %get-tuple-element.41.refs_0_, f32[384,128]{1,0:T(8,128)S(1)} %get-tuple-element.44.refs_1_, f32[128,512]{1,0:T(8,128)S(1)} %shard_map.166.refs_2_, f32[512,128]{1,0:T(8,128)S(1)} %add_add_fusion.refs_3_, ...), custom_call_target="tpu_custom_call" | custom-call | flops 3000000000 | bytes 4000000 | tf_op jit(solution)/shard_map/pallas_call | solution.py:578
  (65 shorter events, 0.8 us)
Async XLA Ops:
  1.5 8.9 %collective-permute-start = (f32[136,128]{1,0:T(8,128)S(1)}, f32[136,128]{1,0:T(8,128)S(1)}, u32[]{:S(2)}, u32[]{:S(2)}) collective-permute-start(f32[136,128]{1,0:T(8,128)S(1)} %select_maximum_fusion.place_ref), channel_id=1, source_target_pairs={{0,2},{1,3},{2,0},{3,1},{4,6},{5,7},{6,4},{7,5},{8,10},{9,11},{10,... | collective-permute-start | bytes 208904 | tf_op jit(solution)/shard_map/ppermute | solution.py:590
  4.5 7.5 %collective-permute-start.1 = (f32[136,128]{1,0:T(8,128)S(1)}, f32[136,128]{1,0:T(8,128)S(1)}, u32[]{:S(2)}, u32[]{:S(2)}) collective-permute-start(f32[136,128]{1,0:T(8,128)S(1)} %select_maximum_fusion.place_ref), channel_id=1, source_target_pairs={{0,4},{1,5},{2,6},{3,7},{4,0},{5,1},{6,2},{7,3},{8,12},{9,13},{10,... | collective-permute-start | bytes 208904 | tf_op jit(solution)/shard_map/ppermute | solution.py:590
  7.1 6.2 %collective-permute-start.2 = (f32[136,128]{1,0:T(8,128)S(1)}, f32[136,128]{1,0:T(8,128)S(1)}, u32[]{:S(2)}, u32[]{:S(2)}) collective-permute-start(f32[136,128]{1,0:T(8,128)S(1)} %select_maximum_fusion.place_ref), channel_id=1, source_target_pairs={{0,6},{1,7},{2,4},{3,5},{4,2},{5,3},{6,0},{7,1},{8,14},{9,15},{10,... | collective-permute-start | bytes 208904 | tf_op jit(solution)/shard_map/ppermute | solution.py:590
  7.1 0.7 copy-start.12
  7.8 5.6 %copy-start.7 = (f32[3,128,128]{2,1,0:T(8,128)S(1)}, f32[3,128,128]{2,1,0:T(8,128)}, u32[]{:S(2)}) copy-start(f32[3,128,128]{2,1,0:T(8,128)} %param.16) | copy-start | bytes 589828
  7.8 6.5 %copy-start.14 = (f32[2,20,384]{2,0,1:T(2,128)S(1)}, f32[2,20,384]{2,0,1:T(2,128)}, u32[]{:S(2)}) copy-start(f32[2,20,384]{2,0,1:T(2,128)} %param.23) | copy-start | bytes 184324
  7.8 10.2 %copy-start = (f32[2,128,128]{2,1,0:T(8,128)S(1)}, f32[2,128,128]{2,1,0:T(8,128)}, u32[]{:S(2)}) copy-start(f32[2,128,128]{2,1,0:T(8,128)} %refs_2_.3) | copy-start | bytes 393220
  7.8 10.2 %copy-start.13 = (f32[3,512]{1,0:T(4,128)S(1)}, f32[3,512]{1,0:T(4,128)}, u32[]{:S(2)}) copy-start(f32[3,512]{1,0:T(4,128)} %refs_1_.1) | copy-start | bytes 18436
  7.8 19.1 %copy-start.4 = (f32[2,128,384]{2,1,0:T(8,128)S(1)}, f32[2,128,384]{2,1,0:T(8,128)}, u32[]{:S(2)}) copy-start(f32[2,128,384]{2,1,0:T(8,128)} %refs_5_.3) | copy-start | bytes 1179652
  7.8 19.1 %copy-start.8 = (f32[2,128,128]{2,1,0:T(8,128)S(1)}, f32[2,128,128]{2,1,0:T(8,128)}, u32[]{:S(2)}) copy-start(f32[2,128,128]{2,1,0:T(8,128)} %refs_4_.5) | copy-start | bytes 393220
  7.8 19.1 %copy-start.11 = (s32[48,547]{1,0:T(8,128)S(1)}, s32[48,547]{1,0:T(8,128)}, u32[]{:S(2)}) copy-start(s32[48,547]{1,0:T(8,128)} %refs_7_.3) | copy-start | bytes 315076
  13.4 4.6 %collective-permute-start.3 = (f32[544,128]{1,0:T(8,128)S(1)}, f32[544,128]{1,0:T(8,128)S(1)}, u32[]{:S(2)}, u32[]{:S(2)}) collective-permute-start(f32[544,128]{1,0:T(8,128)S(1)} %constant_dynamic-update-slice_fusion.refs_2_.refs_0_), channel_id=1, source_target_pairs={{0,1},{1,0},{2,3},{3,2},{4,5},{5,4},{6,7},{7,6},{8,9},{9,8},{10,11... | collective-permute-start | bytes 835592 | tf_op jit(solution)/shard_map/ppermute | solution.py:590
  13.5 11.7 %collective-permute-start.4 = (f32[384,128]{1,0:T(8,128)S(1)}, f32[384,128]{1,0:T(8,128)S(1)}, u32[]{:S(2)}, u32[]{:S(2)}) collective-permute-start(f32[384,128]{1,0:T(8,128)S(1)} %bitcast.3), channel_id=1, source_target_pairs={{0,2},{1,3},{2,0},{3,1},{4,6},{5,7},{6,4},{7,5},{8,10},{9,11},{10,... | collective-permute-start | bytes 589832 | tf_op jit(solution)/shard_map/ppermute | solution.py:590
  14.3 21.8 %collective-permute-start.7 = (f32[384,128]{1,0:T(8,128)S(1)}, f32[384,128]{1,0:T(8,128)S(1)}, u32[]{:S(2)}, u32[]{:S(2)}) collective-permute-start(f32[384,128]{1,0:T(8,128)S(1)} %bitcast.4), channel_id=1, source_target_pairs={{0,4},{1,5},{2,6},{3,7},{4,0},{5,1},{6,2},{7,3},{8,12},{9,13},{10,... | collective-permute-start | bytes 589832 | tf_op jit(solution)/shard_map/ppermute | solution.py:590
  16.1 20.1 %collective-permute-start.9 = (f32[384,128]{1,0:T(8,128)S(1)}, f32[384,128]{1,0:T(8,128)S(1)}, u32[]{:S(2)}, u32[]{:S(2)}) collective-permute-start(f32[384,128]{1,0:T(8,128)S(1)} %bitcast.5), channel_id=1, source_target_pairs={{0,6},{1,7},{2,4},{3,5},{4,2},{5,3},{6,0},{7,1},{8,14},{9,15},{10,... | collective-permute-start | bytes 589832 | tf_op jit(solution)/shard_map/ppermute | solution.py:590
  18.0 0.7 copy-start.2
  22.1 14.6 %collective-permute-start.11 = (f32[512,128]{1,0:T(8,128)S(1)}, f32[512,128]{1,0:T(8,128)S(1)}, u32[]{:S(2)}, u32[]{:S(2)}) collective-permute-start(f32[512,128]{1,0:T(8,128)S(1)} %get-tuple-element.31), channel_id=1, source_target_pairs={{0,8},{8,0},{16,24},{24,16},{1,9},{9,1},{17,25},{25,17},{2,10},{10... | collective-permute-start | bytes 786440 | tf_op jit(solution)/shard_map/ppermute | solution.py:590
  23.7 13.2 %collective-permute-start.12 = (f32[512,128]{1,0:T(8,128)S(1)}, f32[512,128]{1,0:T(8,128)S(1)}, u32[]{:S(2)}, u32[]{:S(2)}) collective-permute-start(f32[512,128]{1,0:T(8,128)S(1)} %get-tuple-element.31), channel_id=1, source_target_pairs={{0,16},{8,24},{16,0},{24,8},{1,17},{9,25},{17,1},{25,9},{2,18},{10... | collective-permute-start | bytes 786440 | tf_op jit(solution)/shard_map/ppermute | solution.py:590
  25.2 12.1 %collective-permute-start.13 = (f32[512,128]{1,0:T(8,128)S(1)}, f32[512,128]{1,0:T(8,128)S(1)}, u32[]{:S(2)}, u32[]{:S(2)}) collective-permute-start(f32[512,128]{1,0:T(8,128)S(1)} %get-tuple-element.31), channel_id=1, source_target_pairs={{0,24},{8,16},{16,8},{24,0},{1,25},{9,17},{17,9},{25,1},{2,26},{10... | collective-permute-start | bytes 786440 | tf_op jit(solution)/shard_map/ppermute | solution.py:590
  36.1 1.5 %collective-permute-start.5 = (f32[384,128]{1,0:T(8,128)S(1)}, f32[384,128]{1,0:T(8,128)S(1)}, u32[]{:S(2)}, u32[]{:S(2)}) collective-permute-start(f32[384,128]{1,0:T(8,128)S(1)} %bitcast.6), channel_id=1, source_target_pairs={{0,1},{1,0},{2,3},{3,2},{4,5},{5,4},{6,7},{7,6},{8,9},{9,8},{10,11... | collective-permute-start | bytes 589832 | tf_op jit(solution)/shard_map/ppermute | solution.py:590
  36.2 1.7 %collective-permute-start.6 = (f32[384,128]{1,0:T(8,128)S(1)}, f32[384,128]{1,0:T(8,128)S(1)}, u32[]{:S(2)}, u32[]{:S(2)}) collective-permute-start(f32[384,128]{1,0:T(8,128)S(1)} %collective-permute-done.4.refs_4_), channel_id=1, source_target_pairs={{0,1},{1,0},{2,3},{3,2},{4,5},{5,4},{6,7},{7,6},{8,9},{9,8},{10,11... | collective-permute-start | bytes 589832 | tf_op jit(solution)/shard_map/ppermute | solution.py:590
  36.7 1.5 %collective-permute-start.8 = (f32[384,128]{1,0:T(8,128)S(1)}, f32[384,128]{1,0:T(8,128)S(1)}, u32[]{:S(2)}, u32[]{:S(2)}) collective-permute-start(f32[384,128]{1,0:T(8,128)S(1)} %collective-permute-done.7.refs_6_), channel_id=1, source_target_pairs={{0,1},{1,0},{2,3},{3,2},{4,5},{5,4},{6,7},{7,6},{8,9},{9,8},{10,11... | collective-permute-start | bytes 589832 | tf_op jit(solution)/shard_map/ppermute | solution.py:590
  36.8 1.7 %collective-permute-start.10 = (f32[384,128]{1,0:T(8,128)S(1)}, f32[384,128]{1,0:T(8,128)S(1)}, u32[]{:S(2)}, u32[]{:S(2)}) collective-permute-start(f32[384,128]{1,0:T(8,128)S(1)} %collective-permute-done.9.refs_8_), channel_id=1, source_target_pairs={{0,1},{1,0},{2,3},{3,2},{4,5},{5,4},{6,7},{7,6},{8,9},{9,8},{10,11... | collective-permute-start | bytes 589832 | tf_op jit(solution)/shard_map/ppermute | solution.py:590
  37.3 6.1 %collective-permute-start.14 = (f32[512,128]{1,0:T(8,128)S(1)}, f32[512,128]{1,0:T(8,128)S(1)}, u32[]{:S(2)}, u32[]{:S(2)}) collective-permute-start(f32[512,128]{1,0:T(8,128)S(1)} %add_add_fusion.1.refs_3_), channel_id=1, source_target_pairs={{0,1},{1,0},{2,3},{3,2},{4,5},{5,4},{6,7},{7,6},{8,9},{9,8},{10,11... | collective-permute-start | bytes 786440 | tf_op jit(solution)/shard_map/ppermute | solution.py:590
  38.5 4.9 %copy-start.1 = (f32[128,128]{1,0:T(8,128)S(1)}, f32[128,128]{1,0:T(8,128)}, u32[]{:S(2)}) copy-start(f32[128,128]{1,0:T(8,128)} %refs_0_.1) | copy-start | bytes 196612
  38.5 4.9 %copy-start.3 = (f32[2,512,128]{2,1,0:T(8,128)S(1)}, f32[2,512,128]{2,1,0:T(8,128)}, u32[]{:S(2)}) copy-start(f32[2,512,128]{2,1,0:T(8,128)} %refs_6_.5) | copy-start | bytes 1572868
  38.5 4.9 %copy-start.5 = (f32[2,128,384]{2,1,0:T(8,128)S(1)}, f32[2,128,384]{2,1,0:T(8,128)}, u32[]{:S(2)}) copy-start(f32[2,128,384]{2,1,0:T(8,128)} %refs_10_.3) | copy-start | bytes 1179652
  38.5 4.9 %copy-start.6 = (f32[2,256,128]{2,1,0:T(8,128)S(1)}, f32[2,256,128]{2,1,0:T(8,128)}, u32[]{:S(2)}) copy-start(f32[2,256,128]{2,1,0:T(8,128)} %refs_9_.3) | copy-start | bytes 786436
  38.5 4.9 %copy-start.9 = (f32[2,128,128]{2,1,0:T(8,128)S(1)}, f32[2,128,128]{2,1,0:T(8,128)}, u32[]{:S(2)}) copy-start(f32[2,128,128]{2,1,0:T(8,128)} %refs_7_.5) | copy-start | bytes 393220
  38.5 4.9 %copy-start.10 = (f32[2,128,128]{2,1,0:T(8,128)S(1)}, f32[2,128,128]{2,1,0:T(8,128)}, u32[]{:S(2)}) copy-start(f32[2,128,128]{2,1,0:T(8,128)} %refs_8_.3) | copy-start | bytes 393220
  45.1 5.3 %collective-permute-start.15 = (f32[128,128]{1,0:T(8,128)S(1)}, f32[128,128]{1,0:T(8,128)S(1)}, u32[]{:S(2)}, u32[]{:S(2)}) collective-permute-start(f32[128,128]{1,0:T(8,128)S(1)} %get-tuple-element.41.refs_0_), channel_id=1, source_target_pairs={{0,2},{1,3},{2,0},{3,1},{4,6},{5,7},{6,4},{7,5},{8,10},{9,11},{10,... | collective-permute-start | bytes 196616 | tf_op jit(solution)/shard_map/ppermute | solution.py:590
  45.2 8.7 %collective-permute-start.16 = (f32[128,128]{1,0:T(8,128)S(1)}, f32[128,128]{1,0:T(8,128)S(1)}, u32[]{:S(2)}, u32[]{:S(2)}) collective-permute-start(f32[128,128]{1,0:T(8,128)S(1)} %get-tuple-element.41.refs_0_), channel_id=1, source_target_pairs={{0,4},{1,5},{2,6},{3,7},{4,0},{5,1},{6,2},{7,3},{8,12},{9,13},{10,... | collective-permute-start | bytes 196616 | tf_op jit(solution)/shard_map/ppermute | solution.py:590
  47.5 6.4 %collective-permute-start.17 = (f32[128,128]{1,0:T(8,128)S(1)}, f32[128,128]{1,0:T(8,128)S(1)}, u32[]{:S(2)}, u32[]{:S(2)}) collective-permute-start(f32[128,128]{1,0:T(8,128)S(1)} %get-tuple-element.41.refs_0_), channel_id=1, source_target_pairs={{0,6},{1,7},{2,4},{3,5},{4,2},{5,3},{6,0},{7,1},{8,14},{9,15},{10,... | collective-permute-start | bytes 196616 | tf_op jit(solution)/shard_map/ppermute | solution.py:590
  53.9 4.5 %collective-permute-start.18 = (f32[512,128]{1,0:T(8,128)S(1)}, f32[512,128]{1,0:T(8,128)S(1)}, u32[]{:S(2)}, u32[]{:S(2)}) collective-permute-start(f32[512,128]{1,0:T(8,128)S(1)} %constant_dynamic-update-slice_fusion.4.refs_0_), channel_id=1, source_target_pairs={{0,1},{1,0},{2,3},{3,2},{4,5},{5,4},{6,7},{7,6},{8,9},{9,8},{10,11... | collective-permute-start | bytes 786440 | tf_op jit(solution)/shard_map/ppermute | solution.py:590
  54.0 11.3 %collective-permute-start.19 = (f32[384,128]{1,0:T(8,128)S(1)}, f32[384,128]{1,0:T(8,128)S(1)}, u32[]{:S(2)}, u32[]{:S(2)}) collective-permute-start(f32[384,128]{1,0:T(8,128)S(1)} %get-tuple-element.44.refs_1_), channel_id=1, source_target_pairs={{0,2},{1,3},{2,0},{3,1},{4,6},{5,7},{6,4},{7,5},{8,10},{9,11},{10,... | collective-permute-start | bytes 589832 | tf_op jit(solution)/shard_map/ppermute | solution.py:590
  55.3 22.0 %collective-permute-start.22 = (f32[384,128]{1,0:T(8,128)S(1)}, f32[384,128]{1,0:T(8,128)S(1)}, u32[]{:S(2)}, u32[]{:S(2)}) collective-permute-start(f32[384,128]{1,0:T(8,128)S(1)} %get-tuple-element.44.refs_1_), channel_id=1, source_target_pairs={{0,4},{1,5},{2,6},{3,7},{4,0},{5,1},{6,2},{7,3},{8,12},{9,13},{10,... | collective-permute-start | bytes 589832 | tf_op jit(solution)/shard_map/ppermute | solution.py:590
  56.6 20.8 %collective-permute-start.24 = (f32[384,128]{1,0:T(8,128)S(1)}, f32[384,128]{1,0:T(8,128)S(1)}, u32[]{:S(2)}, u32[]{:S(2)}) collective-permute-start(f32[384,128]{1,0:T(8,128)S(1)} %get-tuple-element.44.refs_1_), channel_id=1, source_target_pairs={{0,6},{1,7},{2,4},{3,5},{4,2},{5,3},{6,0},{7,1},{8,14},{9,15},{10,... | collective-permute-start | bytes 589832 | tf_op jit(solution)/shard_map/ppermute | solution.py:590
  59.8 18.1 %collective-permute-start.26 = (f32[512,128]{1,0:T(8,128)S(1)}, f32[512,128]{1,0:T(8,128)S(1)}, u32[]{:S(2)}, u32[]{:S(2)}) collective-permute-start(f32[512,128]{1,0:T(8,128)S(1)} %shard_map.164), channel_id=1, source_target_pairs={{0,8},{8,0},{16,24},{24,16},{1,9},{9,1},{17,25},{25,17},{2,10},{10... | collective-permute-start | bytes 786440 | tf_op jit(solution)/shard_map/ppermute | solution.py:590
  62.7 15.3 %collective-permute-start.27 = (f32[512,128]{1,0:T(8,128)S(1)}, f32[512,128]{1,0:T(8,128)S(1)}, u32[]{:S(2)}, u32[]{:S(2)}) collective-permute-start(f32[512,128]{1,0:T(8,128)S(1)} %shard_map.164), channel_id=1, source_target_pairs={{0,16},{8,24},{16,0},{24,8},{1,17},{9,25},{17,1},{25,9},{2,18},{10... | collective-permute-start | bytes 786440 | tf_op jit(solution)/shard_map/ppermute | solution.py:590
  65.3 13.1 %collective-permute-start.28 = (f32[512,128]{1,0:T(8,128)S(1)}, f32[512,128]{1,0:T(8,128)S(1)}, u32[]{:S(2)}, u32[]{:S(2)}) collective-permute-start(f32[512,128]{1,0:T(8,128)S(1)} %shard_map.164), channel_id=1, source_target_pairs={{0,24},{8,16},{16,8},{24,0},{1,25},{9,17},{17,9},{25,1},{2,26},{10... | collective-permute-start | bytes 786440 | tf_op jit(solution)/shard_map/ppermute | solution.py:590
  77.3 1.5 %collective-permute-start.20 = (f32[384,128]{1,0:T(8,128)S(1)}, f32[384,128]{1,0:T(8,128)S(1)}, u32[]{:S(2)}, u32[]{:S(2)}) collective-permute-start(f32[384,128]{1,0:T(8,128)S(1)} %get-tuple-element.44.refs_1_), channel_id=1, source_target_pairs={{0,1},{1,0},{2,3},{3,2},{4,5},{5,4},{6,7},{7,6},{8,9},{9,8},{10,11... | collective-permute-start | bytes 589832 | tf_op jit(solution)/shard_map/ppermute | solution.py:590
  77.4 1.7 %collective-permute-start.21 = (f32[384,128]{1,0:T(8,128)S(1)}, f32[384,128]{1,0:T(8,128)S(1)}, u32[]{:S(2)}, u32[]{:S(2)}) collective-permute-start(f32[384,128]{1,0:T(8,128)S(1)} %collective-permute-done.19.refs_4_), channel_id=1, source_target_pairs={{0,1},{1,0},{2,3},{3,2},{4,5},{5,4},{6,7},{7,6},{8,9},{9,8},{10,11... | collective-permute-start | bytes 589832 | tf_op jit(solution)/shard_map/ppermute | solution.py:590
  77.9 1.5 %collective-permute-start.23 = (f32[384,128]{1,0:T(8,128)S(1)}, f32[384,128]{1,0:T(8,128)S(1)}, u32[]{:S(2)}, u32[]{:S(2)}) collective-permute-start(f32[384,128]{1,0:T(8,128)S(1)} %collective-permute-done.22.refs_6_), channel_id=1, source_target_pairs={{0,1},{1,0},{2,3},{3,2},{4,5},{5,4},{6,7},{7,6},{8,9},{9,8},{10,11... | collective-permute-start | bytes 589832 | tf_op jit(solution)/shard_map/ppermute | solution.py:590
  78.0 1.7 %collective-permute-start.25 = (f32[384,128]{1,0:T(8,128)S(1)}, f32[384,128]{1,0:T(8,128)S(1)}, u32[]{:S(2)}, u32[]{:S(2)}) collective-permute-start(f32[384,128]{1,0:T(8,128)S(1)} %collective-permute-done.24.refs_8_), channel_id=1, source_target_pairs={{0,1},{1,0},{2,3},{3,2},{4,5},{5,4},{6,7},{7,6},{8,9},{9,8},{10,11... | collective-permute-start | bytes 589832 | tf_op jit(solution)/shard_map/ppermute | solution.py:590
  78.5 5.8 %collective-permute-start.29 = (f32[512,128]{1,0:T(8,128)S(1)}, f32[512,128]{1,0:T(8,128)S(1)}, u32[]{:S(2)}, u32[]{:S(2)}) collective-permute-start(f32[512,128]{1,0:T(8,128)S(1)} %add_add_fusion.refs_3_), channel_id=1, source_target_pairs={{0,1},{1,0},{2,3},{3,2},{4,5},{5,4},{6,7},{7,6},{8,9},{9,8},{10,11... | collective-permute-start | bytes 786440 | tf_op jit(solution)/shard_map/ppermute | solution.py:590

commit v4 on v3

--- a/solution.py
+++ b/solution.py
@@ -99,7 +99,7 @@
 def meta_kernel(n_sub, per_region, slots, ids_ref, pairs_ref, meta_ref):
     region, sub = ids_ref[0], ids_ref[1]
     base = region * per_region
-    for row in range(5):
+    for row in range(6):
         for slot in range(slots):
             meta_ref[row, slot] = lax.rem(sub, 2) if row == 4 else 0
 
@@ -114,6 +114,7 @@
             meta_ref[1, found] = base + p
             meta_ref[2, found] = other ^ sub
             meta_ref[3, found] = (first == sub).astype(jnp.int32)
+            meta_ref[5, found] = near_place(other ^ sub, lax.rem(sub, 2))
 
         return found + hit.astype(jnp.int32)
 
@@ -125,7 +126,7 @@
         functools.partial(meta_kernel, n_sub, per_region, slots),
         in_specs=[SMEM_SPEC, SMEM_SPEC],
         out_specs=SMEM_SPEC,
-        out_shape=jax.ShapeDtypeStruct((5, slots), jnp.int32),
+        out_shape=jax.ShapeDtypeStruct((6, slots), jnp.int32),
     )(ids, pair_blocks)
 
 
@@ -167,26 +168,7 @@
     return pltpu.make_async_copy(table.at[pl.ds(2 * step, 2)], buffer.at[slot], sems.at[slot])
 
 
-def over_tables(count, table, buffer, sems, act):
-    steps = (count + 1) // 2
-
-    def one(step, carry):
-        @pl.when(step + 1 < steps)
-        def _():
-            table_copy(table, step + 1, buffer, sems).start()
-
-        act(step, buffer.at[lax.rem(step, 2)], table_copy(table, step, buffer, sems).wait)
-        return carry
-
-    lax.fori_loop(0, steps, one, 0)
-
-
-def resident_copies(count, table, held, sems):
-    steps = (count + 1) // 2
-    return [(steps >= back, table_copy(table, steps - back, held, sems)) for back in (1, 2)]
-
-
-def over_held_tables(count, table, held, buffer, sems, act):
+def over_tables(count, table, held, buffer, sems, act):
     steps = (count + 1) // 2
     for back in (3, 4):
         pl.when(steps >= back)(table_copy(table, steps - back, buffer, sems).start)
@@ -299,21 +281,12 @@
     places = [r.at[BS:, :] for r in block_views(refs[2:4], n_sub)]
     refs = refs[4:]
     if build:
-        in_ref, out_ref, filter_ref, masks_ref, partial_ref, phi_ref, held, tables_hbm = refs[:8]
-        sources, totals, over_buffer, over_sems, held_sems = refs[8:]
+        in_ref, out_ref, filter_ref, masks_ref, partial_ref, phi_ref, held, held_over, tables_hbm = refs[:9]
+        sources, totals, held_sems, over_sems = refs[9:]
     else:
-        in_ref, out_ref, filter_ref, tables_hbm, partial_ref, phi_ref, held, sources, totals, over_buffer, over_sems, held_sems = refs
+        in_ref, out_ref, filter_ref, tables_hbm, held_over, partial_ref, phi_ref, sources, totals, buffer, sems = refs
     radial_hbm, over_hbm = tables_hbm.at[0], tables_hbm.at[1]
     count = meta_ref[0, 0]
-    if not build:
-
-        @pl.when(count > 0)
-        def _():
-            table_copy(over_hbm, 0, over_buffer, over_sems).start()
-
-        for there, copy in resident_copies(count, radial_hbm, held, held_sems):
-            pl.when(there)(copy.start)
-
     totals[...] = jnp.zeros_like(totals)
     scalars = jnp.concatenate([blocks[e][...] for e in range(1, n_sub)], axis=0)
     hidden = silu(dot3(scalars, in_ref[layer]))
@@ -357,7 +330,7 @@
             one_or_two(step, count, functools.partial(terms, step, tables))
 
         fill_tables(
-            count, ((radial_hbm, held, held_sems), (over_hbm, over_buffer, over_sems)), act
+            count, ((radial_hbm, held, held_sems), (over_hbm, held_over, over_sems)), act
         )
     else:
 
@@ -370,9 +343,7 @@
         def act(step, table, ready):
             one_or_two(step, count, functools.partial(terms, step, table, ready))
 
-        over_tables(count, over_hbm, over_buffer, over_sems, act)
-        for there, copy in resident_copies(count, radial_hbm, held, held_sems):
-            pl.when(there)(copy.wait)
+        over_tables(count, over_hbm, held_over, buffer, sems, act)
 
     mine = columns_of(places[0][...])
     for d in range(3):
@@ -385,29 +356,28 @@
     return [pltpu.VMEM((2, 2, NRBF * BS, 2 * BS), BF16), pltpu.SemaphoreType.DMA((2,))] * number
 
 
-def early_terms(meta, layer, n_sub, blocks, spots, weights, masks=None, tables=None):
+def early_terms(meta, layer, n_sub, blocks, spots, weights, masks=None, tables=None, held=None):
     slots = meta.shape[1]
     build = tables is None
-    shape = jax.ShapeDtypeStruct((2, max(slots, TABLE_SLOTS), NRBF * BS, 2 * BS), BF16)
     out_shape = [
         jax.ShapeDtypeStruct((3 * BS, BS), F32),
         jax.ShapeDtypeStruct((n_sub - 1, BS, 2 * BS), F32),
-        jax.ShapeDtypeStruct((2, 2, NRBF * BS, 2 * BS), BF16),
     ]
+    two = jax.ShapeDtypeStruct((2, 2, NRBF * BS, 2 * BS), BF16)
+    every = jax.ShapeDtypeStruct((2, max(slots, TABLE_SLOTS), NRBF * BS, 2 * BS), BF16)
     return pl.pallas_call(
         functools.partial(early_kernel, n_sub, build, layer),
-        in_specs=[SMEM_SPEC] + [VMEM_SPEC] * 7 + [VMEM_SPEC if build else HBM_SPEC],
-        out_specs=[VMEM_SPEC] * 3 + ([HBM_SPEC] if build else []),
+        in_specs=[SMEM_SPEC] + [VMEM_SPEC] * 7 + ([VMEM_SPEC] if build else [HBM_SPEC, VMEM_SPEC]),
+        out_specs=[VMEM_SPEC] * 2 + ([VMEM_SPEC] * 2 + [HBM_SPEC] if build else []),
         scratch_shapes=[
             pltpu.VMEM((n_sub - 1, 3 * BS, 4 * BS), BF16),
             pltpu.VMEM((BS, 4 * BS), F32),
         ]
-        + table_buffers(1)
-        + [pltpu.SemaphoreType.DMA((2,))],
-        out_shape=out_shape + ([shape] if build else []),
+        + ([pltpu.SemaphoreType.DMA((2,))] * 2 if build else table_buffers(1)),
+        out_shape=out_shape + ([two, two, every] if build else []),
         compiler_params=pltpu.CompilerParams(vmem_limit_bytes=VMEM),
         cost_estimate=cost(3 * 4 * NRBF * BS * BS * 4 * BS * 2 * 3, 10e6),
-    )(meta, *blocks, *spots, *weights, masks if build else tables)
+    )(meta, *blocks, *spots, *weights, *((masks,) if build else (tables, held)))
 
 
 def own_trig_kernel(waves_ref, place_ref, own_ref):
@@ -478,9 +448,10 @@
     )(*operands)
 
 
-def late_kernel(n_sub, layer, meta_ref, *refs):
+def late_kernel(arrays, layer, paired, meta_ref, *refs):
     phi_ref, partial_ref, filter_ref = refs[:3]
-    near, refs = refs[3 : 2 + n_sub], refs[2 + n_sub :]
+    near, refs = refs[3 : 3 + arrays], refs[3 + arrays :]
+    near = [r.at[at : at + 3 * BS, :] for r in near for at in range(0, r.shape[0], 3 * BS)]
     tables_hbm, held, totals, buffer, sems = refs
     radial_hbm = tables_hbm.at[0]
     count = meta_ref[0, 0]
@@ -494,9 +465,10 @@
         parts = []
         for i in range(number):
             slot = meta_ref[2, 2 * step + i]
+            place = meta_ref[5, 2 * step + i] if paired else slot - 1
             vectors = near[0][...]
-            for e in range(2, n_sub):
-                vectors = jnp.where(slot == e, near[e - 1][...], vectors)
+            for at in range(1, len(near)):
+                vectors = jnp.where(place == at, near[at][...], vectors)
             phi = phi_ref[slot - 1]
             phi_s, phi_v = phi[:, :BS], phi[:, BS:]
             parts.append([phi_s] + [phi_v * vectors[d * BS : (d + 1) * BS, :] for d in range(3)])
@@ -511,20 +483,20 @@
     def act(step, table, ready):
         one_or_two(step, count, functools.partial(terms, step, table, ready))
 
-    over_held_tables(count, radial_hbm, held, buffer, sems, act)
-
-
-def late_terms(meta, layer, phi, near, tables, held, partial, weight):
-    n_sub = len(near)
+    over_tables(count, radial_hbm, held, buffer, sems, act)
+
+
+def late_terms(meta, layer, paired, phi, near, tables, held, partial, weight):
+    arrays = len(near)
     return pl.pallas_call(
-        functools.partial(late_kernel, n_sub, layer),
-        in_specs=[SMEM_SPEC] + [VMEM_SPEC] * (2 + n_sub) + [HBM_SPEC, VMEM_SPEC],
+        functools.partial(late_kernel, arrays, layer, paired),
+        in_specs=[SMEM_SPEC] + [VMEM_SPEC] * (3 + arrays) + [HBM_SPEC, VMEM_SPEC],
         out_specs=VMEM_SPEC,
         scratch_shapes=table_buffers(1),
         out_shape=jax.ShapeDtypeStruct((BS, 4 * BS), F32),
         compiler_params=pltpu.CompilerParams(vmem_limit_bytes=VMEM),
         cost_estimate=cost(3 * 4 * NRBF * BS * BS * 4 * BS * 2 * 3, 10e6),
-    )(meta, phi, partial, weight, *near[1:], tables, held)
+    )(meta, phi, partial, weight, *near, tables, held)
 
 
 def update_kernel(scale, layer, last, meta_ref, *refs):
@@ -598,6 +570,21 @@
     return [p for pair in zip(parts, [exchange(p, "sub", 1) for p in parts]) for p in pair]
 
 
+def vector_blocks(pair):
+    size = lax.axis_size("sub")
+    nearest = exchange(pair[: 3 * BS], "sub", 2) if size > 2 else None
+    far = []
+    for chips in range(2, size // 2, 2):
+        far.append(lax.ppermute(pair, "sub", [(i, i ^ (2 * (chips + i % 2))) for i in range(size)]))
+    return nearest, far
+
+
+def near_place(e, core):
+    low = e & 1
+    same = ((e >> 1) & 1) == core
+    return jnp.where(e < 4, e - 1, (e >> 2) * 4 - 1 + jnp.where(same, low, 3 - low))
+
+
 def after(x, *others):
     return lax.optimization_barrier((x, *others))[0]
 
@@ -635,12 +622,19 @@
     for layer in range(LAYERS):
         last = layer == LAYERS - 1
         scalar_parts = from_chips(lean)
-        if layer == 0:
-            scalar_parts = lax.optimization_barrier((*scalar_parts, meta, own_trig))[:-2]
+        paired = layer == 0
+        ahead = (meta, own_trig) if layer == 0 else ()
+        if paired:
+            beside = exchange(vectors, "sub", 1)
+            ahead += (beside,)
+        scalar_parts = lax.optimization_barrier((*scalar_parts, *ahead))[: len(scalar_parts)]
         packed = jnp.concatenate(scalar_parts, axis=0)
         blocks = (packed, exchange(packed, "sub", 1))
-        vector_parts = from_chips(after(vectors, scalar_parts[1]))
-        near = both_cores(vector_parts)
+        own = after(vectors, scalar_parts[1])
+        if paired:
+            nearest, far = vector_blocks(jnp.concatenate([own, beside], axis=0))
+        else:
+            near = both_cores(from_chips(own))[1:]
         if layer == 0:
             spots = blocks
             partial, region_trig = structure(layer, n_sub, blocks, ewald_weight, meta, wavevectors)
@@ -648,15 +642,20 @@
             (partial,) = structure(layer, n_sub, blocks, ewald_weight, region_trig=region_trig)
         others = [exchange(partial, "region", mask) for mask in range(1, n_region)]
         weights = (message_in, message_out, filter_weight)
-        turn = after(meta, partial, *near[2:3])
+        turn = after(meta, partial, *([] if paired else near[1:2]))
         if layer == 0:
-            along, phi, held, tables = early_terms(turn, layer, n_sub, blocks, spots, weights, masks=pair_mask)
+            along, phi, held, held_over, tables = early_terms(turn, layer, n_sub, blocks, spots, weights, masks=pair_mask)
         else:
-            along, phi, held = early_terms(turn, layer, n_sub, blocks, spots, weights, tables=tables)
+            along, phi = early_terms(turn, layer, n_sub, blocks, spots, weights, tables=tables, held=held_over)
         others = lax.optimization_barrier((*others, along))[:-1]
         mine = sum(others, partial)
         theirs = exchange(mine, "sub", 1)
-        totals = late_terms(meta, layer, phi, near, tables, held, along, filter_weight)
+        if paired:
+            near = [beside]
+            for part in ([nearest] if nearest is not None else []) + far:
+                part = after(part, along)
+                near += [part, exchange(part, "sub", 1)]
+        totals = late_terms(meta, layer, paired, phi, near, tables, held, along, filter_weight)
         results = update(
             meta, layer, last, scale, scalars, vectors, totals, mine, theirs, own_trig,
             (ewald_filter, mixing_left, mixing_right, update_in, update_out),

time: 87 us -> 88.5 us (1.017)
  the two profiles are of different devices: /device:TPU:0 before, /device:TPU:6 now
where the time goes in v4:
time: 88.5 us; the launch traced here: 88.2 us
  Pallas kernels  49.2 us (56%)
  starting transfers between devices  21.8 us (25%)
  waiting for transfers between devices  13 us (15%)
  local copies, waits for them, and re-layouts  1.6 us (2%)
  other arithmetic  1.59 us (2%)
  between operations  1.05 us (1%)
    pallas_call x2, Pallas kernels, early_terms(): pl.pallas_call(functools.partial(early_kernel, n_sub, build, layer), in_s...  22.1 us
    ppermute x27, starting transfers between devices, exchange(): return lax.ppermute(x, axis, [(i, i ^ mask) for i in range(size)])  20 us
    pallas_call x2, Pallas kernels, late_terms(): pl.pallas_call(functools.partial(late_kernel, arrays, layer, paired), in_...  16.4 us
    ppermute x27, waiting for transfers between devices, exchange(): return lax.ppermute(x, axis, [(i, i ^ mask) for i in range(size)])  13 us
    pallas_call x2, Pallas kernels, structure(): pl.pallas_call(functools.partial(structure_kernel, n_sub, build, layer),...  4.69 us
    pallas_call x2, Pallas kernels, update(): pl.pallas_call(functools.partial(update_kernel, scale, layer, last), in_s...  3.98 us
    ppermute x1, starting transfers between devices, vector_blocks(): lax.ppermute(pair, 'sub', [(i, i ^ 2 * (chips + i % 2)) for i in range(si...  1.8 us
  transfers between devices with their start and end apart: 28, of which 10 were waited for; matrix products, arithmetic and copies ran while one was open for 1% of the time, Pallas kernels for 51%

profile of v4, /device:TPU:6, one launch (start us, length us, event | category | flops | bytes accessed | tf_op | source)
XLA Modules:
  0.0 88.2 jit_solution(16746721422047519928)
XLA Ops:
  0.6 0.9 select_maximum_fusion.place_ref
  1.5 1.6 %collective-permute-start = (f32[136,128]{1,0:T(8,128)S(1)}, f32[136,128]{1,0:T(8,128)S(1)}, u32[]{:S(2)}, u32[]{:S(2)}) collective-permute-start(f32[136,128]{1,0:T(8,128)S(1)} %select_maximum_fusion.place_ref), channel_id=1, source_target_pairs={{0,2},{1,3},{2,0},{3,1},{4,6},{5,7},{6,4},{7,5},{8,10},{9,11},{10,... | collective-permute-start | bytes 208904 | tf_op jit(solution)/shard_map/ppermute | solution.py:562
  3.1 2.6 %collective-permute-start.1 = (f32[136,128]{1,0:T(8,128)S(1)}, f32[136,128]{1,0:T(8,128)S(1)}, u32[]{:S(2)}, u32[]{:S(2)}) collective-permute-start(f32[136,128]{1,0:T(8,128)S(1)} %select_maximum_fusion.place_ref), channel_id=1, source_target_pairs={{0,4},{1,5},{2,6},{3,7},{4,0},{5,1},{6,2},{7,3},{8,12},{9,13},{10,... | collective-permute-start | bytes 208904 | tf_op jit(solution)/shard_map/ppermute | solution.py:562
  5.7 0.2 collective-permute-start.2
  6.0 0.8 copy-done.12
  6.8 0.5 shard_map.159.refs_5_
  7.3 0.6 pad_add_fusion.ids_ref
  7.9 1.5 %shard_map.158.refs_0_.meta_ref = s32[6,8]{1,0:T(8,128)} custom-call(s32[2]{0:T(128)} %pad_add_fusion.ids_ref, s32[2,48]{1,0:T(2,128)} %pairs_ref.1), custom_call_target="tpu_custom_call" | custom-call | tf_op jit(solution)/shard_map/pallas_call | solution.py:125
  9.4 1.2 %collective-permute-done.1 = f32[136,128]{1,0:T(8,128)S(1)} collective-permute-done((f32[136,128]{1,0:T(8,128)S(1)}, f32[136,128]{1,0:T(8,128)S(1)}, u32[]{:S(2)}, u32[]{:S(2)}) %collective-permute-start.1) | collective-permute-done | bytes 69664 | tf_op jit(solution)/shard_map/ppermute | solution.py:562
  10.6 1.3 %collective-permute-done.2 = f32[136,128]{1,0:T(8,128)S(1)} collective-permute-done((f32[136,128]{1,0:T(8,128)S(1)}, f32[136,128]{1,0:T(8,128)S(1)}, u32[]{:S(2)}, u32[]{:S(2)}) %collective-permute-start.2) | collective-permute-done | bytes 69664 | tf_op jit(solution)/shard_map/ppermute | solution.py:562
  11.9 0.1 collective-permute-start.4
  12.0 0.8 collective-permute-start.5
  12.9 1.8 %collective-permute-start.7 = (f32[768,128]{1,0:T(8,128)S(1)}, f32[768,128]{1,0:T(8,128)S(1)}, u32[]{:S(2)}, u32[]{:S(2)}) collective-permute-start(f32[768,128]{1,0:T(8,128)S(1)} %pad_maximum_fusion), channel_id=1, source_target_pairs={{0,4},{1,7},{2,6},{3,5},{4,0},{5,3},{6,2},{7,1},{8,12},{9,15},{10,... | collective-permute-start | bytes 1179656 | tf_op jit(solution)/shard_map/ppermute | solution.py:578
  14.7 0.7 copy-done.4
  15.4 3.4 %shard_map.160 = (f32[512,128]{1,0:T(8,128)S(1)}, bf16[512,2048]{1,0:T(8,128)(2,1)S(1)}) custom-call(s32[6,8]{1,0:T(8,128)S(1)} %copy-done.4, f32[3,512]{1,0:T(4,128)S(1)} %copy-done.13, f32[544,128]{1,0:T(8,128)S(1)} %constant_dynamic-update-slice_fusion.refs_2_.refs_0_, f32[544,128]{1,0:T(8,128)S(1)} %collective-permute-done.4.refs_3_.refs_1_, ...), custom_call_target="tpu_custom_call" | custom-call | flops 402653184 | bytes 4000000 | tf_op jit(solution)/shard_map/pallas_call | solution.py:441
  18.8 0.6 collective-permute-start.9
  19.4 0.5 collective-permute-start.10
  20.0 2.4 %collective-permute-start.11 = (f32[512,128]{1,0:T(8,128)S(1)}, f32[512,128]{1,0:T(8,128)S(1)}, u32[]{:S(2)}, u32[]{:S(2)}) collective-permute-start(f32[512,128]{1,0:T(8,128)S(1)} %get-tuple-element.37), channel_id=1, source_target_pairs={{0,24},{8,16},{16,8},{24,0},{1,25},{9,17},{17,9},{25,1},{2,26},{10... | collective-permute-start | bytes 786440 | tf_op jit(solution)/shard_map/ppermute | solution.py:562
  22.4 13.1 %shard_map.161 = (f32[384,128]{1,0:T(8,128)S(1)}, f32[7,128,256]{2,1,0:T(8,128)S(1)}, bf16[2,2,2560,256]{3,2,1,0:T(8,128)(2,1)S(1)}, bf16[2,2,2560,256]{3,2,1,0:T(8,128)(2,1)S(1)}, bf16[2,16,2560,256]{3,2,1,0:T(8,128)(2,1)}) custom-call(s32[6,8]{1,0:T(8,128)S(1)} %copy-done.4, f32[544,128]{1,0:T(8,128)S(1)} %constant_dynamic-update-slice_fusion.refs_2_.refs_0_, ...), custom_call_target="tpu_custom_call" | custom-call | flops 12079595520 | bytes 10000000 | tf_op jit(solution)/shard_map/pallas_call | solution.py:368
  35.5 0.1 collective-permute-start.8
  35.6 0.5 collective-permute-start.6
  36.1 0.1 add_add_fusion.1.refs_3_
  36.2 0.1 collective-permute-start.12
  36.4 1.2 %collective-permute-done.6.refs_5_ = f32[384,128]{1,0:T(8,128)S(1)} collective-permute-done((f32[384,128]{1,0:T(8,128)S(1)}, f32[384,128]{1,0:T(8,128)S(1)}, u32[]{:S(2)}, u32[]{:S(2)}) %collective-permute-start.6) | collective-permute-done | bytes 196640 | tf_op jit(solution)/shard_map/ppermute | solution.py:562
  37.7 8.2 %shard_map.162.refs_2_ = f32[128,512]{1,0:T(8,128)S(1)} custom-call(s32[6,8]{1,0:T(8,128)S(1)} %copy-done.4, f32[7,128,256]{2,1,0:T(8,128)S(1)} %get-tuple-element.39.refs_0_, f32[384,128]{1,0:T(8,128)S(1)} %get-tuple-element.40.refs_1_, f32[2,20,384]{2,1,0:T(8,128)S(1)} %copy.17.refs_6_.refs_2_, f32[384,128]{1,0:T(8,128)S(1)} %collective-permute-done.3.refs_3_, ...), custom_call_target="tpu_custom_call" | custom-call | flops 12079595520 | bytes 10000000 | tf_op jit(solution)/shard_map/pallas_call | solution.py:491
  45.9 1.7 %shard_map.163 = (f32[128,128]{1,0:T(8,128)S(1)}, f32[384,128]{1,0:T(8,128)S(1)}) custom-call(s32[6,8]{1,0:T(8,128)S(1)} %copy-done.4, f32[128,128]{1,0:T(8,128)S(1)} %copy-done.5, f32[384,128]{1,0:T(8,128)S(1)} %bitcast.6, f32[128,512]{1,0:T(8,128)S(1)} %shard_map.162.refs_2_, f32[512,128]{1,0:T(8,128)S(1)} %add_add_fusion.1.refs_3_, ...), custom_call_target="tpu_custom_call" | custom-call | flops 3000000000 | bytes 4000000 | tf_op jit(solution)/shard_map/pallas_call | solution.py:550
  47.7 0.6 collective-permute-start.14
  48.2 3.8 %collective-permute-start.15 = (f32[128,128]{1,0:T(8,128)S(1)}, f32[128,128]{1,0:T(8,128)S(1)}, u32[]{:S(2)}, u32[]{:S(2)}) collective-permute-start(f32[128,128]{1,0:T(8,128)S(1)} %get-tuple-element.51.refs_0_), channel_id=1, source_target_pairs={{0,6},{1,7},{2,4},{3,5},{4,2},{5,3},{6,0},{7,1},{8,14},{9,15},{10,... | collective-permute-start | bytes 196616 | tf_op jit(solution)/shard_map/ppermute | solution.py:562
  52.0 0.9 collective-permute-done.14
  52.9 2.1 %collective-permute-done.15 = f32[128,128]{1,0:T(8,128)S(1)} collective-permute-done((f32[128,128]{1,0:T(8,128)S(1)}, f32[128,128]{1,0:T(8,128)S(1)}, u32[]{:S(2)}, u32[]{:S(2)}) %collective-permute-start.15) | collective-permute-done | bytes 65568 | tf_op jit(solution)/shard_map/ppermute | solution.py:562
  55.0 0.1 collective-permute-start.16
  55.2 3.7 %collective-permute-start.20 = (f32[384,128]{1,0:T(8,128)S(1)}, f32[384,128]{1,0:T(8,128)S(1)}, u32[]{:S(2)}, u32[]{:S(2)}) collective-permute-start(f32[384,128]{1,0:T(8,128)S(1)} %get-tuple-element.56.refs_1_), channel_id=1, source_target_pairs={{0,4},{1,5},{2,6},{3,7},{4,0},{5,1},{6,2},{7,3},{8,12},{9,13},{10,... | collective-permute-start | bytes 589832 | tf_op jit(solution)/shard_map/ppermute | solution.py:562
  58.9 0.7 collective-permute-start.22
  59.6 1.3 %shard_map.164 = f32[512,128]{1,0:T(8,128)S(1)} custom-call(f32[512,128]{1,0:T(8,128)S(1)} %constant_dynamic-update-slice_fusion.4.refs_0_, f32[512,128]{1,0:T(8,128)S(1)} %collective-permute-done.16.refs_1_, f32[2,128,128]{2,1,0:T(8,128)S(1)} %copy-done.3, bf16[512,2048]{1,0:T(8,128)(2,1)S(1)} %get-tuple-element.55.refs_3_), custom_call_target="tpu_custom_call" | custom-call | flops 402653184 | bytes 4000000 | tf_op jit(solution)/shard_map/pallas_call | solution.py:441
  60.9 0.1 collective-permute-start.25
  61.0 5.3 %collective-permute-done.17.refs_4_ = f32[384,128]{1,0:T(8,128)S(1)} collective-permute-done((f32[384,128]{1,0:T(8,128)S(1)}, f32[384,128]{1,0:T(8,128)S(1)}, u32[]{:S(2)}, u32[]{:S(2)}) %collective-permute-start.17) | collective-permute-done | bytes 196640 | tf_op jit(solution)/shard_map/ppermute | solution.py:562
  66.3 9.0 %shard_map.165 = (f32[384,128]{1,0:T(8,128)S(1)}, f32[7,128,256]{2,1,0:T(8,128)S(1)}) custom-call(s32[6,8]{1,0:T(8,128)S(1)} %copy-done.4, f32[512,128]{1,0:T(8,128)S(1)} %constant_dynamic-update-slice_fusion.4.refs_0_, f32[512,128]{1,0:T(8,128)S(1)} %collective-permute-done.16.refs_1_, f32[544,128]{1,0:T(8,128)S(1)} %constant_dynamic-update-slice_fusion.refs_2_.refs_0_, ...), custom_call_target="tpu_custom_call" | custom-call | flops 12079595520 | bytes 10000000 | tf_op jit(solution)/shard_map/pallas_call | solution.py:368
  75.3 0.1 collective-permute-start.18
  75.4 0.5 collective-permute-start.19
  75.9 0.1 collective-permute-start.21
  76.0 0.4 collective-permute-start.23
  76.5 0.2 collective-permute-start.27
  76.6 0.2 collective-permute-done.18.refs_3_
  76.8 0.3 collective-permute-done.19.refs_5_
  77.1 0.3 collective-permute-done.21.refs_7_
  77.4 0.3 collective-permute-done.23.refs_9_
  77.7 8.2 %shard_map.166.refs_2_ = f32[128,512]{1,0:T(8,128)S(1)} custom-call(s32[6,8]{1,0:T(8,128)S(1)} %copy-done.4, f32[7,128,256]{2,1,0:T(8,128)S(1)} %get-tuple-element.59.refs_0_, f32[384,128]{1,0:T(8,128)S(1)} %get-tuple-element.60.refs_1_, f32[2,20,384]{2,1,0:T(8,128)S(1)} %copy.17.refs_6_.refs_2_, f32[384,128]{1,0:T(8,128)S(1)} %collective-permute-done.18.refs_3_, ...), custom_call_target="tpu_custom_call" | custom-call | flops 12079595520 | bytes 10000000 | tf_op jit(solution)/shard_map/pallas_call | solution.py:491
  85.9 2.3 %shard_map.167 = (f32[128,128]{1,0:T(8,128)}, f32[3,128,128]{2,1,0:T(8,128)}) custom-call(s32[6,8]{1,0:T(8,128)S(1)} %copy-done.4, f32[128,128]{1,0:T(8,128)S(1)} %get-tuple-element.51.refs_0_, f32[384,128]{1,0:T(8,128)S(1)} %get-tuple-element.56.refs_1_, f32[128,512]{1,0:T(8,128)S(1)} %shard_map.166.refs_2_, f32[512,128]{1,0:T(8,128)S(1)} %add_add_fusion.refs_3_, ...), custom_call_target="tpu_custom_call" | custom-call | flops 3000000000 | bytes 4000000 | tf_op jit(solution)/shard_map/pallas_call | solution.py:550
  (62 shorter events, 0.5 us)
Async XLA Ops:
  1.5 7.9 %collective-permute-start = (f32[136,128]{1,0:T(8,128)S(1)}, f32[136,128]{1,0:T(8,128)S(1)}, u32[]{:S(2)}, u32[]{:S(2)}) collective-permute-start(f32[136,128]{1,0:T(8,128)S(1)} %select_maximum_fusion.place_ref), channel_id=1, source_target_pairs={{0,2},{1,3},{2,0},{3,1},{4,6},{5,7},{6,4},{7,5},{8,10},{9,11},{10,... | collective-permute-start | bytes 208904 | tf_op jit(solution)/shard_map/ppermute | solution.py:562
  3.1 7.5 %collective-permute-start.1 = (f32[136,128]{1,0:T(8,128)S(1)}, f32[136,128]{1,0:T(8,128)S(1)}, u32[]{:S(2)}, u32[]{:S(2)}) collective-permute-start(f32[136,128]{1,0:T(8,128)S(1)} %select_maximum_fusion.place_ref), channel_id=1, source_target_pairs={{0,4},{1,5},{2,6},{3,7},{4,0},{5,1},{6,2},{7,3},{8,12},{9,13},{10,... | collective-permute-start | bytes 208904 | tf_op jit(solution)/shard_map/ppermute | solution.py:562
  5.7 6.2 %collective-permute-start.2 = (f32[136,128]{1,0:T(8,128)S(1)}, f32[136,128]{1,0:T(8,128)S(1)}, u32[]{:S(2)}, u32[]{:S(2)}) collective-permute-start(f32[136,128]{1,0:T(8,128)S(1)} %select_maximum_fusion.place_ref), channel_id=1, source_target_pairs={{0,6},{1,7},{2,4},{3,5},{4,2},{5,3},{6,0},{7,1},{8,14},{9,15},{10,... | collective-permute-start | bytes 208904 | tf_op jit(solution)/shard_map/ppermute | solution.py:562
  5.9 6.2 %copy-start.1 = (f32[3,128,128]{2,1,0:T(8,128)S(1)}, f32[3,128,128]{2,1,0:T(8,128)}, u32[]{:S(2)}) copy-start(f32[3,128,128]{2,1,0:T(8,128)} %param.16) | copy-start | bytes 589828
  5.9 8.8 %copy-start.3 = (f32[2,128,128]{2,1,0:T(8,128)S(1)}, f32[2,128,128]{2,1,0:T(8,128)}, u32[]{:S(2)}) copy-start(f32[2,128,128]{2,1,0:T(8,128)} %refs_2_.3) | copy-start | bytes 393220
  5.9 16.5 %copy-start = (f32[2,128,384]{2,1,0:T(8,128)S(1)}, f32[2,128,384]{2,1,0:T(8,128)}, u32[]{:S(2)}) copy-start(f32[2,128,384]{2,1,0:T(8,128)} %refs_5_.3) | copy-start | bytes 1179652
  5.9 16.5 %copy-start.2 = (f32[2,128,128]{2,1,0:T(8,128)S(1)}, f32[2,128,128]{2,1,0:T(8,128)}, u32[]{:S(2)}) copy-start(f32[2,128,128]{2,1,0:T(8,128)} %refs_4_.5) | copy-start | bytes 393220
  5.9 16.5 %copy-start.11 = (s32[48,547]{1,0:T(8,128)S(1)}, s32[48,547]{1,0:T(8,128)}, u32[]{:S(2)}) copy-start(s32[48,547]{1,0:T(8,128)} %refs_7_.3) | copy-start | bytes 315076
  5.9 6.0 %collective-permute-start.3 = (f32[384,128]{1,0:T(8,128)}, f32[384,128]{1,0:T(8,128)S(1)}, u32[]{:S(2)}, u32[]{:S(2)}) collective-permute-start(f32[384,128]{1,0:T(8,128)} %bitcast.3), channel_id=1, source_target_pairs={{0,1},{1,0},{2,3},{3,2},{4,5},{5,4},{6,7},{7,6},{8,9},{9,8},{10,11... | collective-permute-start | bytes 589832 | tf_op jit(solution)/shard_map/ppermute | solution.py:562
  6.0 0.8 copy-start.12
  6.8 5.2 %copy-start.14 = (f32[2,20,384]{2,0,1:T(2,128)S(1)}, f32[2,20,384]{2,0,1:T(2,128)}, u32[]{:S(2)}) copy-start(f32[2,20,384]{2,0,1:T(2,128)} %param.23) | copy-start | bytes 184324
  6.8 7.9 %copy-start.13 = (f32[3,512]{1,0:T(4,128)S(1)}, f32[3,512]{1,0:T(4,128)}, u32[]{:S(2)}) copy-start(f32[3,512]{1,0:T(4,128)} %refs_1_.1) | copy-start | bytes 18436
  11.9 2.8 %collective-permute-start.4 = (f32[544,128]{1,0:T(8,128)S(1)}, f32[544,128]{1,0:T(8,128)S(1)}, u32[]{:S(2)}, u32[]{:S(2)}) collective-permute-start(f32[544,128]{1,0:T(8,128)S(1)} %constant_dynamic-update-slice_fusion.refs_2_.refs_0_), channel_id=1, source_target_pairs={{0,1},{1,0},{2,3},{3,2},{4,5},{5,4},{6,7},{7,6},{8,9},{9,8},{10,11... | collective-permute-start | bytes 835592 | tf_op jit(solution)/shard_map/ppermute | solution.py:562
  12.0 23.6 %collective-permute-start.5 = (f32[384,128]{1,0:T(8,128)S(1)}, f32[384,128]{1,0:T(8,128)S(1)}, u32[]{:S(2)}, u32[]{:S(2)}) collective-permute-start(f32[384,128]{1,0:T(8,128)S(1)} %bitcast.4), channel_id=1, source_target_pairs={{0,2},{1,3},{2,0},{3,1},{4,6},{5,7},{6,4},{7,5},{8,10},{9,11},{10,... | collective-permute-start | bytes 589832 | tf_op jit(solution)/shard_map/ppermute | solution.py:562
  12.9 22.6 %collective-permute-start.7 = (f32[768,128]{1,0:T(8,128)S(1)}, f32[768,128]{1,0:T(8,128)S(1)}, u32[]{:S(2)}, u32[]{:S(2)}) collective-permute-start(f32[768,128]{1,0:T(8,128)S(1)} %pad_maximum_fusion), channel_id=1, source_target_pairs={{0,4},{1,7},{2,6},{3,5},{4,0},{5,3},{6,2},{7,1},{8,12},{9,15},{10,... | collective-permute-start | bytes 1179656 | tf_op jit(solution)/shard_map/ppermute | solution.py:578
  14.7 0.7 copy-start.4
  18.8 17.3 %collective-permute-start.9 = (f32[512,128]{1,0:T(8,128)S(1)}, f32[512,128]{1,0:T(8,128)S(1)}, u32[]{:S(2)}, u32[]{:S(2)}) collective-permute-start(f32[512,128]{1,0:T(8,128)S(1)} %get-tuple-element.37), channel_id=1, source_target_pairs={{0,8},{8,0},{16,24},{24,16},{1,9},{9,1},{17,25},{25,17},{2,10},{10... | collective-permute-start | bytes 786440 | tf_op jit(solution)/shard_map/ppermute | solution.py:562
  19.4 16.7 %collective-permute-start.10 = (f32[512,128]{1,0:T(8,128)S(1)}, f32[512,128]{1,0:T(8,128)S(1)}, u32[]{:S(2)}, u32[]{:S(2)}) collective-permute-start(f32[512,128]{1,0:T(8,128)S(1)} %get-tuple-element.37), channel_id=1, source_target_pairs={{0,16},{8,24},{16,0},{24,8},{1,17},{9,25},{17,1},{25,9},{2,18},{10... | collective-permute-start | bytes 786440 | tf_op jit(solution)/shard_map/ppermute | solution.py:562
  20.0 16.2 %collective-permute-start.11 = (f32[512,128]{1,0:T(8,128)S(1)}, f32[512,128]{1,0:T(8,128)S(1)}, u32[]{:S(2)}, u32[]{:S(2)}) collective-permute-start(f32[512,128]{1,0:T(8,128)S(1)} %get-tuple-element.37), channel_id=1, source_target_pairs={{0,24},{8,16},{16,8},{24,0},{1,25},{9,17},{17,9},{25,1},{2,26},{10... | collective-permute-start | bytes 786440 | tf_op jit(solution)/shard_map/ppermute | solution.py:562
  35.5 2.1 %collective-permute-start.8 = (f32[768,128]{1,0:T(8,128)S(1)}, f32[768,128]{1,0:T(8,128)S(1)}, u32[]{:S(2)}, u32[]{:S(2)}) collective-permute-start(f32[768,128]{1,0:T(8,128)S(1)} %collective-permute-done.7.refs_6_), channel_id=1, source_target_pairs={{0,1},{1,0},{2,3},{3,2},{4,5},{5,4},{6,7},{7,6},{8,9},{9,8},{10,11... | collective-permute-start | bytes 1179656 | tf_op jit(solution)/shard_map/ppermute | solution.py:562
  35.6 2.0 %collective-permute-start.6 = (f32[384,128]{1,0:T(8,128)S(1)}, f32[384,128]{1,0:T(8,128)S(1)}, u32[]{:S(2)}, u32[]{:S(2)}) collective-permute-start(f32[384,128]{1,0:T(8,128)S(1)} %collective-permute-done.5.refs_4_), channel_id=1, source_target_pairs={{0,1},{1,0},{2,3},{3,2},{4,5},{5,4},{6,7},{7,6},{8,9},{9,8},{10,11... | collective-permute-start | bytes 589832 | tf_op jit(solution)/shard_map/ppermute | solution.py:562
  36.2 9.6 %collective-permute-start.12 = (f32[512,128]{1,0:T(8,128)S(1)}, f32[512,128]{1,0:T(8,128)S(1)}, u32[]{:S(2)}, u32[]{:S(2)}) collective-permute-start(f32[512,128]{1,0:T(8,128)S(1)} %add_add_fusion.1.refs_3_), channel_id=1, source_target_pairs={{0,1},{1,0},{2,3},{3,2},{4,5},{5,4},{6,7},{7,6},{8,9},{9,8},{10,11... | collective-permute-start | bytes 786440 | tf_op jit(solution)/shard_map/ppermute | solution.py:562
  37.6 8.2 %copy-start.5 = (f32[128,128]{1,0:T(8,128)S(1)}, f32[128,128]{1,0:T(8,128)}, u32[]{:S(2)}) copy-start(f32[128,128]{1,0:T(8,128)} %refs_0_.1) | copy-start | bytes 196612
  37.6 8.3 %copy-start.6 = (f32[2,512,128]{2,1,0:T(8,128)S(1)}, f32[2,512,128]{2,1,0:T(8,128)}, u32[]{:S(2)}) copy-start(f32[2,512,128]{2,1,0:T(8,128)} %refs_6_.5) | copy-start | bytes 1572868
  37.6 8.3 %copy-start.7 = (f32[2,128,384]{2,1,0:T(8,128)S(1)}, f32[2,128,384]{2,1,0:T(8,128)}, u32[]{:S(2)}) copy-start(f32[2,128,384]{2,1,0:T(8,128)} %refs_10_.3) | copy-start | bytes 1179652
  37.6 8.3 %copy-start.8 = (f32[2,256,128]{2,1,0:T(8,128)S(1)}, f32[2,256,128]{2,1,0:T(8,128)}, u32[]{:S(2)}) copy-start(f32[2,256,128]{2,1,0:T(8,128)} %refs_9_.3) | copy-start | bytes 786436
  37.6 8.3 %copy-start.9 = (f32[2,128,128]{2,1,0:T(8,128)S(1)}, f32[2,128,128]{2,1,0:T(8,128)}, u32[]{:S(2)}) copy-start(f32[2,128,128]{2,1,0:T(8,128)} %refs_7_.5) | copy-start | bytes 393220
  37.6 8.3 %copy-start.10 = (f32[2,128,128]{2,1,0:T(8,128)S(1)}, f32[2,128,128]{2,1,0:T(8,128)}, u32[]{:S(2)}) copy-start(f32[2,128,128]{2,1,0:T(8,128)} %refs_8_.3) | copy-start | bytes 393220
  47.6 4.5 %collective-permute-start.13 = (f32[128,128]{1,0:T(8,128)S(1)}, f32[128,128]{1,0:T(8,128)S(1)}, u32[]{:S(2)}, u32[]{:S(2)}) collective-permute-start(f32[128,128]{1,0:T(8,128)S(1)} %get-tuple-element.51.refs_0_), channel_id=1, source_target_pairs={{0,2},{1,3},{2,0},{3,1},{4,6},{5,7},{6,4},{7,5},{8,10},{9,11},{10,... | collective-permute-start | bytes 196616 | tf_op jit(solution)/shard_map/ppermute | solution.py:562
  47.7 5.2 %collective-permute-start.14 = (f32[128,128]{1,0:T(8,128)S(1)}, f32[128,128]{1,0:T(8,128)S(1)}, u32[]{:S(2)}, u32[]{:S(2)}) collective-permute-start(f32[128,128]{1,0:T(8,128)S(1)} %get-tuple-element.51.refs_0_), channel_id=1, source_target_pairs={{0,4},{1,5},{2,6},{3,7},{4,0},{5,1},{6,2},{7,3},{8,12},{9,13},{10,... | collective-permute-start | bytes 196616 | tf_op jit(solution)/shard_map/ppermute | solution.py:562
  48.2 6.8 %collective-permute-start.15 = (f32[128,128]{1,0:T(8,128)S(1)}, f32[128,128]{1,0:T(8,128)S(1)}, u32[]{:S(2)}, u32[]{:S(2)}) collective-permute-start(f32[128,128]{1,0:T(8,128)S(1)} %get-tuple-element.51.refs_0_), channel_id=1, source_target_pairs={{0,6},{1,7},{2,4},{3,5},{4,2},{5,3},{6,0},{7,1},{8,14},{9,15},{10,... | collective-permute-start | bytes 196616 | tf_op jit(solution)/shard_map/ppermute | solution.py:562
  55.0 4.5 %collective-permute-start.16 = (f32[512,128]{1,0:T(8,128)S(1)}, f32[512,128]{1,0:T(8,128)S(1)}, u32[]{:S(2)}, u32[]{:S(2)}) collective-permute-start(f32[512,128]{1,0:T(8,128)S(1)} %constant_dynamic-update-slice_fusion.4.refs_0_), channel_id=1, source_target_pairs={{0,1},{1,0},{2,3},{3,2},{4,5},{5,4},{6,7},{7,6},{8,9},{9,8},{10,11... | collective-permute-start | bytes 786440 | tf_op jit(solution)/shard_map/ppermute | solution.py:562
  55.1 11.2 %collective-permute-start.17 = (f32[384,128]{1,0:T(8,128)S(1)}, f32[384,128]{1,0:T(8,128)S(1)}, u32[]{:S(2)}, u32[]{:S(2)}) collective-permute-start(f32[384,128]{1,0:T(8,128)S(1)} %get-tuple-element.56.refs_1_), channel_id=1, source_target_pairs={{0,2},{1,3},{2,0},{3,1},{4,6},{5,7},{6,4},{7,5},{8,10},{9,11},{10,... | collective-permute-start | bytes 589832 | tf_op jit(solution)/shard_map/ppermute | solution.py:562
  55.2 20.1 %collective-permute-start.20 = (f32[384,128]{1,0:T(8,128)S(1)}, f32[384,128]{1,0:T(8,128)S(1)}, u32[]{:S(2)}, u32[]{:S(2)}) collective-permute-start(f32[384,128]{1,0:T(8,128)S(1)} %get-tuple-element.56.refs_1_), channel_id=1, source_target_pairs={{0,4},{1,5},{2,6},{3,7},{4,0},{5,1},{6,2},{7,3},{8,12},{9,13},{10,... | collective-permute-start | bytes 589832 | tf_op jit(solution)/shard_map/ppermute | solution.py:562
  58.9 16.5 %collective-permute-start.22 = (f32[384,128]{1,0:T(8,128)S(1)}, f32[384,128]{1,0:T(8,128)S(1)}, u32[]{:S(2)}, u32[]{:S(2)}) collective-permute-start(f32[384,128]{1,0:T(8,128)S(1)} %get-tuple-element.56.refs_1_), channel_id=1, source_target_pairs={{0,6},{1,7},{2,4},{3,5},{4,2},{5,3},{6,0},{7,1},{8,14},{9,15},{10,... | collective-permute-start | bytes 589832 | tf_op jit(solution)/shard_map/ppermute | solution.py:562
  60.9 15.0 %collective-permute-start.24 = (f32[512,128]{1,0:T(8,128)S(1)}, f32[512,128]{1,0:T(8,128)S(1)}, u32[]{:S(2)}, u32[]{:S(2)}) collective-permute-start(f32[512,128]{1,0:T(8,128)S(1)} %shard_map.164), channel_id=1, source_target_pairs={{0,8},{8,0},{16,24},{24,16},{1,9},{9,1},{17,25},{25,17},{2,10},{10... | collective-permute-start | bytes 786440 | tf_op jit(solution)/shard_map/ppermute | solution.py:562
  60.9 15.0 %collective-permute-start.25 = (f32[512,128]{1,0:T(8,128)S(1)}, f32[512,128]{1,0:T(8,128)S(1)}, u32[]{:S(2)}, u32[]{:S(2)}) collective-permute-start(f32[512,128]{1,0:T(8,128)S(1)} %shard_map.164), channel_id=1, source_target_pairs={{0,16},{8,24},{16,0},{24,8},{1,17},{9,25},{17,1},{25,9},{2,18},{10... | collective-permute-start | bytes 786440 | tf_op jit(solution)/shard_map/ppermute | solution.py:562
  66.3 10.1 %collective-permute-start.26 = (f32[512,128]{1,0:T(8,128)S(1)}, f32[512,128]{1,0:T(8,128)S(1)}, u32[]{:S(2)}, u32[]{:S(2)}) collective-permute-start(f32[512,128]{1,0:T(8,128)S(1)} %shard_map.164), channel_id=1, source_target_pairs={{0,24},{8,16},{16,8},{24,0},{1,25},{9,17},{17,9},{25,1},{2,26},{10... | collective-permute-start | bytes 786440 | tf_op jit(solution)/shard_map/ppermute | solution.py:562
  75.3 1.5 %collective-permute-start.18 = (f32[384,128]{1,0:T(8,128)S(1)}, f32[384,128]{1,0:T(8,128)S(1)}, u32[]{:S(2)}, u32[]{:S(2)}) collective-permute-start(f32[384,128]{1,0:T(8,128)S(1)} %get-tuple-element.56.refs_1_), channel_id=1, source_target_pairs={{0,1},{1,0},{2,3},{3,2},{4,5},{5,4},{6,7},{7,6},{8,9},{9,8},{10,11... | collective-permute-start | bytes 589832 | tf_op jit(solution)/shard_map/ppermute | solution.py:562
  75.4 1.7 %collective-permute-start.19 = (f32[384,128]{1,0:T(8,128)S(1)}, f32[384,128]{1,0:T(8,128)S(1)}, u32[]{:S(2)}, u32[]{:S(2)}) collective-permute-start(f32[384,128]{1,0:T(8,128)S(1)} %collective-permute-done.17.refs_4_), channel_id=1, source_target_pairs={{0,1},{1,0},{2,3},{3,2},{4,5},{5,4},{6,7},{7,6},{8,9},{9,8},{10,11... | collective-permute-start | bytes 589832 | tf_op jit(solution)/shard_map/ppermute | solution.py:562
  75.9 1.5 %collective-permute-start.21 = (f32[384,128]{1,0:T(8,128)S(1)}, f32[384,128]{1,0:T(8,128)S(1)}, u32[]{:S(2)}, u32[]{:S(2)}) collective-permute-start(f32[384,128]{1,0:T(8,128)S(1)} %collective-permute-done.20.refs_6_), channel_id=1, source_target_pairs={{0,1},{1,0},{2,3},{3,2},{4,5},{5,4},{6,7},{7,6},{8,9},{9,8},{10,11... | collective-permute-start | bytes 589832 | tf_op jit(solution)/shard_map/ppermute | solution.py:562
  76.0 1.7 %collective-permute-start.23 = (f32[384,128]{1,0:T(8,128)S(1)}, f32[384,128]{1,0:T(8,128)S(1)}, u32[]{:S(2)}, u32[]{:S(2)}) collective-permute-start(f32[384,128]{1,0:T(8,128)S(1)} %collective-permute-done.22.refs_8_), channel_id=1, source_target_pairs={{0,1},{1,0},{2,3},{3,2},{4,5},{5,4},{6,7},{7,6},{8,9},{9,8},{10,11... | collective-permute-start | bytes 589832 | tf_op jit(solution)/shard_map/ppermute | solution.py:562
  76.5 9.5 %collective-permute-start.27 = (f32[512,128]{1,0:T(8,128)S(1)}, f32[512,128]{1,0:T(8,128)S(1)}, u32[]{:S(2)}, u32[]{:S(2)}) collective-permute-start(f32[512,128]{1,0:T(8,128)S(1)} %add_add_fusion.refs_3_), channel_id=1, source_target_pairs={{0,1},{1,0},{2,3},{3,2},{4,5},{5,4},{6,7},{7,6},{8,9},{9,8},{10,11... | collective-permute-start | bytes 786440 | tf_op jit(solution)/shard_map/ppermute | solution.py:562

commit v5 on v4

--- a/solution.py
+++ b/solution.py
@@ -206,17 +206,15 @@
                 out(step - 2, *t).wait()
 
         act(step, [buffer.at[lax.rem(step, 2)] for _, buffer, _ in tables])
-        for t in tables:
-            out(step, *t).start()
-        return carry
-
-    lax.fori_loop(0, steps, one, 0)
-    for back in (2, 1):
-
-        @pl.when(steps >= back)
+
+        @pl.when(step + 2 < steps)
         def _():
             for t in tables:
-                out(steps - back, *t).wait()
+                out(step, *t).start()
+
+        return carry
+
+    lax.fori_loop(0, steps, one, 0)
 
 
 def block_views(packed, n_sub):
@@ -617,7 +615,7 @@
     lean = jnp.concatenate([scalars, place], axis=0)
     vectors = vectors.reshape(3 * BS, -1)
     meta = find_pairs(ids, pair_blocks, n_sub, per_region, slots)
-    own_trig = own_trig_of(wavevectors, lean)
+    own_trig = own_trig_of(wavevectors, after(lean, meta))
     tables = region_trig = spots = None
     for layer in range(LAYERS):
         last = layer == LAYERS - 1

time: 88.5 us -> 85.2 us (0.963)
  the two profiles are of different devices: /device:TPU:6 before, /device:TPU:4 now
where the time goes in v5:
time: 85.2 us
  Pallas kernels  43.6 us (51%)
  starting transfers between devices  25.4 us (30%)
  waiting for transfers between devices  12.8 us (15%)
  other arithmetic  1.66 us (2%)
  between operations  1.02 us (1%)
    ppermute x27, starting transfers between devices, exchange(): return lax.ppermute(x, axis, [(i, i ^ mask) for i in range(size)])  23.6 us
    pallas_call x2, Pallas kernels, early_terms(): pl.pallas_call(functools.partial(early_kernel, n_sub, build, layer), in_s...  18 us
    pallas_call x2, Pallas kernels, late_terms(): pl.pallas_call(functools.partial(late_kernel, arrays, layer, paired), in_...  14.9 us
    ppermute x27, waiting for transfers between devices, exchange(): return lax.ppermute(x, axis, [(i, i ^ mask) for i in range(size)])  10.9 us
    pallas_call x2, Pallas kernels, structure(): pl.pallas_call(functools.partial(structure_kernel, n_sub, build, layer),...  4.69 us
    pallas_call x2, Pallas kernels, update(): pl.pallas_call(functools.partial(update_kernel, scale, layer, last), in_s...  3.99 us
    ppermute x1, waiting for transfers between devices, vector_blocks(): lax.ppermute(pair, 'sub', [(i, i ^ 2 * (chips + i % 2)) for i in range(si...  1.87 us
    ppermute x1, starting transfers between devices, vector_blocks(): lax.ppermute(pair, 'sub', [(i, i ^ 2 * (chips + i % 2)) for i in range(si...  1.8 us
  transfers between devices with their start and end apart: 28, of which 11 were waited for; matrix products, arithmetic and copies ran while one was open for 1% of the time, Pallas kernels for 46%

profile of v5, /device:TPU:4, one launch (start us, length us, event | category | flops | bytes accessed | tf_op | source)
XLA Modules:
  0.0 85.2 jit_solution(5202329191899120122)
XLA Ops:
  0.6 0.9 %select_maximum_fusion.place_ref = f32[136,128]{1,0:T(8,128)S(1)} fusion(f32[3,128]{1,0:T(4,128)} %param.17, f32[128,128]{1,0:T(8,128)} %refs_0_.1), kind=kLoop, calls=%fused_computation.3 | loop fusion | flops 52224 | bytes 136704 | tf_op jit(solution)/shard_map/concatenate | solution.py:615
  1.5 1.6 %collective-permute-start = (f32[136,128]{1,0:T(8,128)S(1)}, f32[136,128]{1,0:T(8,128)S(1)}, u32[]{:S(2)}, u32[]{:S(2)}) collective-permute-start(f32[136,128]{1,0:T(8,128)S(1)} %select_maximum_fusion.place_ref), channel_id=1, source_target_pairs={{0,2},{1,3},{2,0},{3,1},{4,6},{5,7},{6,4},{7,5},{8,10},{9,11},{10,... | collective-permute-start | bytes 208904 | tf_op jit(solution)/shard_map/ppermute | solution.py:560
  3.1 2.6 %collective-permute-start.1 = (f32[136,128]{1,0:T(8,128)S(1)}, f32[136,128]{1,0:T(8,128)S(1)}, u32[]{:S(2)}, u32[]{:S(2)}) collective-permute-start(f32[136,128]{1,0:T(8,128)S(1)} %select_maximum_fusion.place_ref), channel_id=1, source_target_pairs={{0,4},{1,5},{2,6},{3,7},{4,0},{5,1},{6,2},{7,3},{8,12},{9,13},{10,... | collective-permute-start | bytes 208904 | tf_op jit(solution)/shard_map/ppermute | solution.py:560
  5.7 0.2 collective-permute-start.2
  5.9 0.6 pad_add_fusion.ids_ref
  6.5 1.5 %shard_map.158.refs_0_.meta_ref = s32[6,8]{1,0:T(8,128)} custom-call(s32[2]{0:T(128)} %pad_add_fusion.ids_ref, s32[2,48]{1,0:T(2,128)} %pairs_ref.1), custom_call_target="tpu_custom_call" | custom-call | tf_op jit(solution)/shard_map/pallas_call | solution.py:125
  8.1 0.7 copy-done.12
  8.8 0.5 shard_map.159.refs_5_
  9.4 1.2 %collective-permute-done.1 = f32[136,128]{1,0:T(8,128)S(1)} collective-permute-done((f32[136,128]{1,0:T(8,128)S(1)}, f32[136,128]{1,0:T(8,128)S(1)}, u32[]{:S(2)}, u32[]{:S(2)}) %collective-permute-start.1) | collective-permute-done | bytes 69664 | tf_op jit(solution)/shard_map/ppermute | solution.py:560
  10.6 1.3 %collective-permute-done.2 = f32[136,128]{1,0:T(8,128)S(1)} collective-permute-done((f32[136,128]{1,0:T(8,128)S(1)}, f32[136,128]{1,0:T(8,128)S(1)}, u32[]{:S(2)}, u32[]{:S(2)}) %collective-permute-start.2) | collective-permute-done | bytes 69664 | tf_op jit(solution)/shard_map/ppermute | solution.py:560
  11.9 0.1 collective-permute-start.4
  12.0 0.8 collective-permute-start.5
  12.9 1.8 %collective-permute-start.7 = (f32[768,128]{1,0:T(8,128)S(1)}, f32[768,128]{1,0:T(8,128)S(1)}, u32[]{:S(2)}, u32[]{:S(2)}) collective-permute-start(f32[768,128]{1,0:T(8,128)S(1)} %pad_maximum_fusion), channel_id=1, source_target_pairs={{0,4},{1,7},{2,6},{3,5},{4,0},{5,3},{6,2},{7,1},{8,12},{9,15},{10,... | collective-permute-start | bytes 1179656 | tf_op jit(solution)/shard_map/ppermute | solution.py:576
  14.7 3.4 %shard_map.160 = (f32[512,128]{1,0:T(8,128)S(1)}, bf16[512,2048]{1,0:T(8,128)(2,1)S(1)}) custom-call(s32[6,8]{1,0:T(8,128)S(1)} %copy-done.4, f32[3,512]{1,0:T(4,128)S(1)} %copy-done.12, f32[544,128]{1,0:T(8,128)S(1)} %constant_dynamic-update-slice_fusion.refs_2_.refs_0_, f32[544,128]{1,0:T(8,128)S(1)} %collective-permute-done.4.refs_3_.refs_1_, ...), custom_call_target="tpu_custom_call" | custom-call | flops 402653184 | bytes 4000000 | tf_op jit(solution)/shard_map/pallas_call | solution.py:439
  18.2 1.6 %collective-permute-start.9 = (f32[512,128]{1,0:T(8,128)S(1)}, f32[512,128]{1,0:T(8,128)S(1)}, u32[]{:S(2)}, u32[]{:S(2)}) collective-permute-start(f32[512,128]{1,0:T(8,128)S(1)} %get-tuple-element.39), channel_id=1, source_target_pairs={{0,8},{8,0},{16,24},{24,16},{1,9},{9,1},{17,25},{25,17},{2,10},{10... | collective-permute-start | bytes 786440 | tf_op jit(solution)/shard_map/ppermute | solution.py:560
  19.7 0.5 collective-permute-start.10
  20.2 1.5 %collective-permute-start.11 = (f32[512,128]{1,0:T(8,128)S(1)}, f32[512,128]{1,0:T(8,128)S(1)}, u32[]{:S(2)}, u32[]{:S(2)}) collective-permute-start(f32[512,128]{1,0:T(8,128)S(1)} %get-tuple-element.39), channel_id=1, source_target_pairs={{0,24},{8,16},{16,8},{24,0},{1,25},{9,17},{17,9},{25,1},{2,26},{10... | collective-permute-start | bytes 786440 | tf_op jit(solution)/shard_map/ppermute | solution.py:560
  21.7 9.7 %shard_map.161 = (f32[384,128]{1,0:T(8,128)S(1)}, f32[7,128,256]{2,1,0:T(8,128)S(1)}, bf16[2,2,2560,256]{3,2,1,0:T(8,128)(2,1)S(1)}, bf16[2,2,2560,256]{3,2,1,0:T(8,128)(2,1)S(1)}, bf16[2,16,2560,256]{3,2,1,0:T(8,128)(2,1)}) custom-call(s32[6,8]{1,0:T(8,128)S(1)} %copy-done.4, f32[544,128]{1,0:T(8,128)S(1)} %constant_dynamic-update-slice_fusion.refs_2_.refs_0_, ...), custom_call_target="tpu_custom_call" | custom-call | flops 12079595520 | bytes 10000000 | tf_op jit(solution)/shard_map/pallas_call | solution.py:366
  31.4 1.9 %collective-permute-done.7.refs_6_ = f32[768,128]{1,0:T(8,128)S(1)} collective-permute-done((f32[768,128]{1,0:T(8,128)S(1)}, f32[768,128]{1,0:T(8,128)S(1)}, u32[]{:S(2)}, u32[]{:S(2)}) %collective-permute-start.7) | collective-permute-done | bytes 393248 | tf_op jit(solution)/shard_map/ppermute | solution.py:576
  33.3 0.5 collective-permute-start.6
  33.8 0.1 collective-permute-done.10
  33.9 0.1 add_add_fusion.1.refs_3_
  34.1 1.2 %collective-permute-done.6.refs_5_ = f32[384,128]{1,0:T(8,128)S(1)} collective-permute-done((f32[384,128]{1,0:T(8,128)S(1)}, f32[384,128]{1,0:T(8,128)S(1)}, u32[]{:S(2)}, u32[]{:S(2)}) %collective-permute-start.6) | collective-permute-done | bytes 196640 | tf_op jit(solution)/shard_map/ppermute | solution.py:560
  35.4 7.4 %shard_map.162.refs_2_ = f32[128,512]{1,0:T(8,128)S(1)} custom-call(s32[6,8]{1,0:T(8,128)S(1)} %copy-done.4, f32[7,128,256]{2,1,0:T(8,128)S(1)} %get-tuple-element.41.refs_0_, f32[384,128]{1,0:T(8,128)S(1)} %get-tuple-element.42.refs_1_, f32[2,20,384]{2,1,0:T(8,128)S(1)} %copy.17.refs_6_.refs_2_, f32[384,128]{1,0:T(8,128)S(1)} %collective-permute-done.3.refs_3_, ...), custom_call_target="tpu_custom_call" | custom-call | flops 12079595520 | bytes 10000000 | tf_op jit(solution)/shard_map/pallas_call | solution.py:489
  42.8 1.7 %shard_map.163 = (f32[128,128]{1,0:T(8,128)S(1)}, f32[384,128]{1,0:T(8,128)S(1)}) custom-call(s32[6,8]{1,0:T(8,128)S(1)} %copy-done.4, f32[128,128]{1,0:T(8,128)S(1)} %copy-done.5, f32[384,128]{1,0:T(8,128)S(1)} %bitcast.6, f32[128,512]{1,0:T(8,128)S(1)} %shard_map.162.refs_2_, f32[512,128]{1,0:T(8,128)S(1)} %add_add_fusion.1.refs_3_, ...), custom_call_target="tpu_custom_call" | custom-call | flops 3000000000 | bytes 4000000 | tf_op jit(solution)/shard_map/pallas_call | solution.py:548
  44.6 0.1 collective-permute-start.14
  44.7 4.3 %collective-permute-start.15 = (f32[128,128]{1,0:T(8,128)S(1)}, f32[128,128]{1,0:T(8,128)S(1)}, u32[]{:S(2)}, u32[]{:S(2)}) collective-permute-start(f32[128,128]{1,0:T(8,128)S(1)} %get-tuple-element.53.refs_0_), channel_id=1, source_target_pairs={{0,6},{1,7},{2,4},{3,5},{4,2},{5,3},{6,0},{7,1},{8,14},{9,15},{10,... | collective-permute-start | bytes 196616 | tf_op jit(solution)/shard_map/ppermute | solution.py:560
  49.0 3.0 %collective-permute-done.14 = f32[128,128]{1,0:T(8,128)S(1)} collective-permute-done((f32[128,128]{1,0:T(8,128)S(1)}, f32[128,128]{1,0:T(8,128)S(1)}, u32[]{:S(2)}, u32[]{:S(2)}) %collective-permute-start.14) | collective-permute-done | bytes 65568 | tf_op jit(solution)/shard_map/ppermute | solution.py:560
  52.1 1.3 %collective-permute-start.17 = (f32[384,128]{1,0:T(8,128)S(1)}, f32[384,128]{1,0:T(8,128)S(1)}, u32[]{:S(2)}, u32[]{:S(2)}) collective-permute-start(f32[384,128]{1,0:T(8,128)S(1)} %get-tuple-element.58.refs_1_), channel_id=1, source_target_pairs={{0,2},{1,3},{2,0},{3,1},{4,6},{5,7},{6,4},{7,5},{8,10},{9,11},{10,... | collective-permute-start | bytes 589832 | tf_op jit(solution)/shard_map/ppermute | solution.py:560
  53.4 2.4 %collective-permute-start.20 = (f32[384,128]{1,0:T(8,128)S(1)}, f32[384,128]{1,0:T(8,128)S(1)}, u32[]{:S(2)}, u32[]{:S(2)}) collective-permute-start(f32[384,128]{1,0:T(8,128)S(1)} %get-tuple-element.58.refs_1_), channel_id=1, source_target_pairs={{0,4},{1,5},{2,6},{3,7},{4,0},{5,1},{6,2},{7,3},{8,12},{9,13},{10,... | collective-permute-start | bytes 589832 | tf_op jit(solution)/shard_map/ppermute | solution.py:560
  55.8 0.7 collective-permute-start.22
  56.5 1.3 %shard_map.164 = f32[512,128]{1,0:T(8,128)S(1)} custom-call(f32[512,128]{1,0:T(8,128)S(1)} %constant_dynamic-update-slice_fusion.4.refs_0_, f32[512,128]{1,0:T(8,128)S(1)} %collective-permute-done.16.refs_1_, f32[2,128,128]{2,1,0:T(8,128)S(1)} %copy-done.3, bf16[512,2048]{1,0:T(8,128)(2,1)S(1)} %get-tuple-element.57.refs_3_), custom_call_target="tpu_custom_call" | custom-call | flops 402653184 | bytes 4000000 | tf_op jit(solution)/shard_map/pallas_call | solution.py:439
  57.8 1.6 %collective-permute-start.24 = (f32[512,128]{1,0:T(8,128)S(1)}, f32[512,128]{1,0:T(8,128)S(1)}, u32[]{:S(2)}, u32[]{:S(2)}) collective-permute-start(f32[512,128]{1,0:T(8,128)S(1)} %shard_map.164), channel_id=1, source_target_pairs={{0,8},{8,0},{16,24},{24,16},{1,9},{9,1},{17,25},{25,17},{2,10},{10... | collective-permute-start | bytes 786440 | tf_op jit(solution)/shard_map/ppermute | solution.py:560
  59.5 0.5 collective-permute-start.25
  60.0 3.0 %collective-permute-done.17.refs_4_ = f32[384,128]{1,0:T(8,128)S(1)} collective-permute-done((f32[384,128]{1,0:T(8,128)S(1)}, f32[384,128]{1,0:T(8,128)S(1)}, u32[]{:S(2)}, u32[]{:S(2)}) %collective-permute-start.17) | collective-permute-done | bytes 196640 | tf_op jit(solution)/shard_map/ppermute | solution.py:560
  63.0 1.8 %collective-permute-start.26 = (f32[512,128]{1,0:T(8,128)S(1)}, f32[512,128]{1,0:T(8,128)S(1)}, u32[]{:S(2)}, u32[]{:S(2)}) collective-permute-start(f32[512,128]{1,0:T(8,128)S(1)} %shard_map.164), channel_id=1, source_target_pairs={{0,24},{8,16},{16,8},{24,0},{1,25},{9,17},{17,9},{25,1},{2,26},{10... | collective-permute-start | bytes 786440 | tf_op jit(solution)/shard_map/ppermute | solution.py:560
  64.8 8.3 %shard_map.165 = (f32[384,128]{1,0:T(8,128)S(1)}, f32[7,128,256]{2,1,0:T(8,128)S(1)}) custom-call(s32[6,8]{1,0:T(8,128)S(1)} %copy-done.4, f32[512,128]{1,0:T(8,128)S(1)} %constant_dynamic-update-slice_fusion.4.refs_0_, f32[512,128]{1,0:T(8,128)S(1)} %collective-permute-done.16.refs_1_, f32[544,128]{1,0:T(8,128)S(1)} %constant_dynamic-update-slice_fusion.refs_2_.refs_0_, ...), custom_call_target="tpu_custom_call" | custom-call | flops 12079595520 | bytes 10000000 | tf_op jit(solution)/shard_map/pallas_call | solution.py:366
  73.1 0.1 collective-permute-start.18
  73.2 0.5 collective-permute-start.19
  73.6 0.1 collective-permute-start.21
  73.7 0.4 collective-permute-start.23
  74.2 0.2 collective-permute-start.27
  74.4 0.2 collective-permute-done.18.refs_3_
  74.6 0.3 collective-permute-done.19.refs_5_
  74.9 0.3 collective-permute-done.21.refs_7_
  75.1 0.3 collective-permute-done.23.refs_9_
  75.4 7.5 %shard_map.166.refs_2_ = f32[128,512]{1,0:T(8,128)S(1)} custom-call(s32[6,8]{1,0:T(8,128)S(1)} %copy-done.4, f32[7,128,256]{2,1,0:T(8,128)S(1)} %get-tuple-element.61.refs_0_, f32[384,128]{1,0:T(8,128)S(1)} %get-tuple-element.62.refs_1_, f32[2,20,384]{2,1,0:T(8,128)S(1)} %copy.17.refs_6_.refs_2_, f32[384,128]{1,0:T(8,128)S(1)} %collective-permute-done.18.refs_3_, ...), custom_call_target="tpu_custom_call" | custom-call | flops 12079595520 | bytes 10000000 | tf_op jit(solution)/shard_map/pallas_call | solution.py:489
  82.9 2.3 %shard_map.167 = (f32[128,128]{1,0:T(8,128)}, f32[3,128,128]{2,1,0:T(8,128)}) custom-call(s32[6,8]{1,0:T(8,128)S(1)} %copy-done.4, f32[128,128]{1,0:T(8,128)S(1)} %get-tuple-element.53.refs_0_, f32[384,128]{1,0:T(8,128)S(1)} %get-tuple-element.58.refs_1_, f32[128,512]{1,0:T(8,128)S(1)} %shard_map.166.refs_2_, f32[512,128]{1,0:T(8,128)S(1)} %add_add_fusion.refs_3_, ...), custom_call_target="tpu_custom_call" | custom-call | flops 3000000000 | bytes 4000000 | tf_op jit(solution)/shard_map/pallas_call | solution.py:548
  (60 shorter events, 0.5 us)
Async XLA Ops:
  1.5 7.9 %collective-permute-start = (f32[136,128]{1,0:T(8,128)S(1)}, f32[136,128]{1,0:T(8,128)S(1)}, u32[]{:S(2)}, u32[]{:S(2)}) collective-permute-start(f32[136,128]{1,0:T(8,128)S(1)} %select_maximum_fusion.place_ref), channel_id=1, source_target_pairs={{0,2},{1,3},{2,0},{3,1},{4,6},{5,7},{6,4},{7,5},{8,10},{9,11},{10,... | collective-permute-start | bytes 208904 | tf_op jit(solution)/shard_map/ppermute | solution.py:560
  3.1 7.5 %collective-permute-start.1 = (f32[136,128]{1,0:T(8,128)S(1)}, f32[136,128]{1,0:T(8,128)S(1)}, u32[]{:S(2)}, u32[]{:S(2)}) collective-permute-start(f32[136,128]{1,0:T(8,128)S(1)} %select_maximum_fusion.place_ref), channel_id=1, source_target_pairs={{0,4},{1,5},{2,6},{3,7},{4,0},{5,1},{6,2},{7,3},{8,12},{9,13},{10,... | collective-permute-start | bytes 208904 | tf_op jit(solution)/shard_map/ppermute | solution.py:560
  5.7 6.2 %collective-permute-start.2 = (f32[136,128]{1,0:T(8,128)S(1)}, f32[136,128]{1,0:T(8,128)S(1)}, u32[]{:S(2)}, u32[]{:S(2)}) collective-permute-start(f32[136,128]{1,0:T(8,128)S(1)} %select_maximum_fusion.place_ref), channel_id=1, source_target_pairs={{0,6},{1,7},{2,4},{3,5},{4,2},{5,3},{6,0},{7,1},{8,14},{9,15},{10,... | collective-permute-start | bytes 208904 | tf_op jit(solution)/shard_map/ppermute | solution.py:560
  5.9 6.0 %collective-permute-start.3 = (f32[384,128]{1,0:T(8,128)}, f32[384,128]{1,0:T(8,128)S(1)}, u32[]{:S(2)}, u32[]{:S(2)}) collective-permute-start(f32[384,128]{1,0:T(8,128)} %bitcast.3), channel_id=1, source_target_pairs={{0,1},{1,0},{2,3},{3,2},{4,5},{5,4},{6,7},{7,6},{8,9},{9,8},{10,11... | collective-permute-start | bytes 589832 | tf_op jit(solution)/shard_map/ppermute | solution.py:560
  8.1 0.7 copy-start.12
  8.8 3.2 %copy-start.13 = (f32[2,20,384]{2,0,1:T(2,128)S(1)}, f32[2,20,384]{2,0,1:T(2,128)}, u32[]{:S(2)}) copy-start(f32[2,20,384]{2,0,1:T(2,128)} %param.23) | copy-start | bytes 184324
  8.8 3.3 %copy-start.1 = (f32[3,128,128]{2,1,0:T(8,128)S(1)}, f32[3,128,128]{2,1,0:T(8,128)}, u32[]{:S(2)}) copy-start(f32[3,128,128]{2,1,0:T(8,128)} %param.16) | copy-start | bytes 589828
  8.8 6.0 %copy-start.3 = (f32[2,128,128]{2,1,0:T(8,128)S(1)}, f32[2,128,128]{2,1,0:T(8,128)}, u32[]{:S(2)}) copy-start(f32[2,128,128]{2,1,0:T(8,128)} %refs_2_.3) | copy-start | bytes 393220
  8.8 6.0 %copy-start.4 = (s32[6,8]{1,0:T(8,128)S(1)}, s32[6,8]{1,0:T(8,128)}, u32[]{:S(2)}) copy-start(s32[6,8]{1,0:T(8,128)} %shard_map.158.refs_0_.meta_ref) | copy-start | bytes 580
  8.8 13.0 %copy-start = (f32[2,128,384]{2,1,0:T(8,128)S(1)}, f32[2,128,384]{2,1,0:T(8,128)}, u32[]{:S(2)}) copy-start(f32[2,128,384]{2,1,0:T(8,128)} %refs_5_.3) | copy-start | bytes 1179652
  8.8 12.9 %copy-start.2 = (f32[2,128,128]{2,1,0:T(8,128)S(1)}, f32[2,128,128]{2,1,0:T(8,128)}, u32[]{:S(2)}) copy-start(f32[2,128,128]{2,1,0:T(8,128)} %refs_4_.5) | copy-start | bytes 393220
  8.8 12.9 %copy-start.11 = (s32[48,547]{1,0:T(8,128)S(1)}, s32[48,547]{1,0:T(8,128)}, u32[]{:S(2)}) copy-start(s32[48,547]{1,0:T(8,128)} %refs_7_.3) | copy-start | bytes 315076
  11.9 2.8 %collective-permute-start.4 = (f32[544,128]{1,0:T(8,128)S(1)}, f32[544,128]{1,0:T(8,128)S(1)}, u32[]{:S(2)}, u32[]{:S(2)}) collective-permute-start(f32[544,128]{1,0:T(8,128)S(1)} %constant_dynamic-update-slice_fusion.refs_2_.refs_0_), channel_id=1, source_target_pairs={{0,1},{1,0},{2,3},{3,2},{4,5},{5,4},{6,7},{7,6},{8,9},{9,8},{10,11... | collective-permute-start | bytes 835592 | tf_op jit(solution)/shard_map/ppermute | solution.py:560
  12.0 21.3 %collective-permute-start.5 = (f32[384,128]{1,0:T(8,128)S(1)}, f32[384,128]{1,0:T(8,128)S(1)}, u32[]{:S(2)}, u32[]{:S(2)}) collective-permute-start(f32[384,128]{1,0:T(8,128)S(1)} %bitcast.4), channel_id=1, source_target_pairs={{0,2},{1,3},{2,0},{3,1},{4,6},{5,7},{6,4},{7,5},{8,10},{9,11},{10,... | collective-permute-start | bytes 589832 | tf_op jit(solution)/shard_map/ppermute | solution.py:560
  12.9 20.4 %collective-permute-start.7 = (f32[768,128]{1,0:T(8,128)S(1)}, f32[768,128]{1,0:T(8,128)S(1)}, u32[]{:S(2)}, u32[]{:S(2)}) collective-permute-start(f32[768,128]{1,0:T(8,128)S(1)} %pad_maximum_fusion), channel_id=1, source_target_pairs={{0,4},{1,7},{2,6},{3,5},{4,0},{5,3},{6,2},{7,1},{8,12},{9,15},{10,... | collective-permute-start | bytes 1179656 | tf_op jit(solution)/shard_map/ppermute | solution.py:576
  18.2 15.7 %collective-permute-start.9 = (f32[512,128]{1,0:T(8,128)S(1)}, f32[512,128]{1,0:T(8,128)S(1)}, u32[]{:S(2)}, u32[]{:S(2)}) collective-permute-start(f32[512,128]{1,0:T(8,128)S(1)} %get-tuple-element.39), channel_id=1, source_target_pairs={{0,8},{8,0},{16,24},{24,16},{1,9},{9,1},{17,25},{25,17},{2,10},{10... | collective-permute-start | bytes 786440 | tf_op jit(solution)/shard_map/ppermute | solution.py:560
  19.7 14.2 %collective-permute-start.10 = (f32[512,128]{1,0:T(8,128)S(1)}, f32[512,128]{1,0:T(8,128)S(1)}, u32[]{:S(2)}, u32[]{:S(2)}) collective-permute-start(f32[512,128]{1,0:T(8,128)S(1)} %get-tuple-element.39), channel_id=1, source_target_pairs={{0,16},{8,24},{16,0},{24,8},{1,17},{9,25},{17,1},{25,9},{2,18},{10... | collective-permute-start | bytes 786440 | tf_op jit(solution)/shard_map/ppermute | solution.py:560
  20.2 13.7 %collective-permute-start.11 = (f32[512,128]{1,0:T(8,128)S(1)}, f32[512,128]{1,0:T(8,128)S(1)}, u32[]{:S(2)}, u32[]{:S(2)}) collective-permute-start(f32[512,128]{1,0:T(8,128)S(1)} %get-tuple-element.39), channel_id=1, source_target_pairs={{0,24},{8,16},{16,8},{24,0},{1,25},{9,17},{17,9},{25,1},{2,26},{10... | collective-permute-start | bytes 786440 | tf_op jit(solution)/shard_map/ppermute | solution.py:560
  33.3 2.0 %collective-permute-start.8 = (f32[768,128]{1,0:T(8,128)S(1)}, f32[768,128]{1,0:T(8,128)S(1)}, u32[]{:S(2)}, u32[]{:S(2)}) collective-permute-start(f32[768,128]{1,0:T(8,128)S(1)} %collective-permute-done.7.refs_6_), channel_id=1, source_target_pairs={{0,1},{1,0},{2,3},{3,2},{4,5},{5,4},{6,7},{7,6},{8,9},{9,8},{10,11... | collective-permute-start | bytes 1179656 | tf_op jit(solution)/shard_map/ppermute | solution.py:560
  33.3 2.0 %collective-permute-start.6 = (f32[384,128]{1,0:T(8,128)S(1)}, f32[384,128]{1,0:T(8,128)S(1)}, u32[]{:S(2)}, u32[]{:S(2)}) collective-permute-start(f32[384,128]{1,0:T(8,128)S(1)} %collective-permute-done.5.refs_4_), channel_id=1, source_target_pairs={{0,1},{1,0},{2,3},{3,2},{4,5},{5,4},{6,7},{7,6},{8,9},{9,8},{10,11... | collective-permute-start | bytes 589832 | tf_op jit(solution)/shard_map/ppermute | solution.py:560
  34.0 8.8 %collective-permute-start.12 = (f32[512,128]{1,0:T(8,128)S(1)}, f32[512,128]{1,0:T(8,128)S(1)}, u32[]{:S(2)}, u32[]{:S(2)}) collective-permute-start(f32[512,128]{1,0:T(8,128)S(1)} %add_add_fusion.1.refs_3_), channel_id=1, source_target_pairs={{0,1},{1,0},{2,3},{3,2},{4,5},{5,4},{6,7},{7,6},{8,9},{9,8},{10,11... | collective-permute-start | bytes 786440 | tf_op jit(solution)/shard_map/ppermute | solution.py:560
  35.3 7.5 %copy-start.5 = (f32[128,128]{1,0:T(8,128)S(1)}, f32[128,128]{1,0:T(8,128)}, u32[]{:S(2)}) copy-start(f32[128,128]{1,0:T(8,128)} %refs_0_.1) | copy-start | bytes 196612
  35.3 7.5 %copy-start.6 = (f32[2,512,128]{2,1,0:T(8,128)S(1)}, f32[2,512,128]{2,1,0:T(8,128)}, u32[]{:S(2)}) copy-start(f32[2,512,128]{2,1,0:T(8,128)} %refs_6_.5) | copy-start | bytes 1572868
  35.3 7.5 %copy-start.7 = (f32[2,128,384]{2,1,0:T(8,128)S(1)}, f32[2,128,384]{2,1,0:T(8,128)}, u32[]{:S(2)}) copy-start(f32[2,128,384]{2,1,0:T(8,128)} %refs_10_.3) | copy-start | bytes 1179652
  35.3 7.5 %copy-start.8 = (f32[2,256,128]{2,1,0:T(8,128)S(1)}, f32[2,256,128]{2,1,0:T(8,128)}, u32[]{:S(2)}) copy-start(f32[2,256,128]{2,1,0:T(8,128)} %refs_9_.3) | copy-start | bytes 786436
  35.4 7.5 %copy-start.9 = (f32[2,128,128]{2,1,0:T(8,128)S(1)}, f32[2,128,128]{2,1,0:T(8,128)}, u32[]{:S(2)}) copy-start(f32[2,128,128]{2,1,0:T(8,128)} %refs_7_.5) | copy-start | bytes 393220
  35.4 7.5 %copy-start.10 = (f32[2,128,128]{2,1,0:T(8,128)S(1)}, f32[2,128,128]{2,1,0:T(8,128)}, u32[]{:S(2)}) copy-start(f32[2,128,128]{2,1,0:T(8,128)} %refs_8_.3) | copy-start | bytes 393220
  44.5 4.5 %collective-permute-start.13 = (f32[128,128]{1,0:T(8,128)S(1)}, f32[128,128]{1,0:T(8,128)S(1)}, u32[]{:S(2)}, u32[]{:S(2)}) collective-permute-start(f32[128,128]{1,0:T(8,128)S(1)} %get-tuple-element.53.refs_0_), channel_id=1, source_target_pairs={{0,2},{1,3},{2,0},{3,1},{4,6},{5,7},{6,4},{7,5},{8,10},{9,11},{10,... | collective-permute-start | bytes 196616 | tf_op jit(solution)/shard_map/ppermute | solution.py:560
  44.6 7.3 %collective-permute-start.14 = (f32[128,128]{1,0:T(8,128)S(1)}, f32[128,128]{1,0:T(8,128)S(1)}, u32[]{:S(2)}, u32[]{:S(2)}) collective-permute-start(f32[128,128]{1,0:T(8,128)S(1)} %get-tuple-element.53.refs_0_), channel_id=1, source_target_pairs={{0,4},{1,5},{2,6},{3,7},{4,0},{5,1},{6,2},{7,3},{8,12},{9,13},{10,... | collective-permute-start | bytes 196616 | tf_op jit(solution)/shard_map/ppermute | solution.py:560
  44.7 7.3 %collective-permute-start.15 = (f32[128,128]{1,0:T(8,128)S(1)}, f32[128,128]{1,0:T(8,128)S(1)}, u32[]{:S(2)}, u32[]{:S(2)}) collective-permute-start(f32[128,128]{1,0:T(8,128)S(1)} %get-tuple-element.53.refs_0_), channel_id=1, source_target_pairs={{0,6},{1,7},{2,4},{3,5},{4,2},{5,3},{6,0},{7,1},{8,14},{9,15},{10,... | collective-permute-start | bytes 196616 | tf_op jit(solution)/shard_map/ppermute | solution.py:560
  52.0 4.5 %collective-permute-start.16 = (f32[512,128]{1,0:T(8,128)S(1)}, f32[512,128]{1,0:T(8,128)S(1)}, u32[]{:S(2)}, u32[]{:S(2)}) collective-permute-start(f32[512,128]{1,0:T(8,128)S(1)} %constant_dynamic-update-slice_fusion.4.refs_0_), channel_id=1, source_target_pairs={{0,1},{1,0},{2,3},{3,2},{4,5},{5,4},{6,7},{7,6},{8,9},{9,8},{10,11... | collective-permute-start | bytes 786440 | tf_op jit(solution)/shard_map/ppermute | solution.py:560
  52.1 10.9 %collective-permute-start.17 = (f32[384,128]{1,0:T(8,128)S(1)}, f32[384,128]{1,0:T(8,128)S(1)}, u32[]{:S(2)}, u32[]{:S(2)}) collective-permute-start(f32[384,128]{1,0:T(8,128)S(1)} %get-tuple-element.58.refs_1_), channel_id=1, source_target_pairs={{0,2},{1,3},{2,0},{3,1},{4,6},{5,7},{6,4},{7,5},{8,10},{9,11},{10,... | collective-permute-start | bytes 589832 | tf_op jit(solution)/shard_map/ppermute | solution.py:560
  53.4 19.7 %collective-permute-start.20 = (f32[384,128]{1,0:T(8,128)S(1)}, f32[384,128]{1,0:T(8,128)S(1)}, u32[]{:S(2)}, u32[]{:S(2)}) collective-permute-start(f32[384,128]{1,0:T(8,128)S(1)} %get-tuple-element.58.refs_1_), channel_id=1, source_target_pairs={{0,4},{1,5},{2,6},{3,7},{4,0},{5,1},{6,2},{7,3},{8,12},{9,13},{10,... | collective-permute-start | bytes 589832 | tf_op jit(solution)/shard_map/ppermute | solution.py:560
  55.8 17.4 %collective-permute-start.22 = (f32[384,128]{1,0:T(8,128)S(1)}, f32[384,128]{1,0:T(8,128)S(1)}, u32[]{:S(2)}, u32[]{:S(2)}) collective-permute-start(f32[384,128]{1,0:T(8,128)S(1)} %get-tuple-element.58.refs_1_), channel_id=1, source_target_pairs={{0,6},{1,7},{2,4},{3,5},{4,2},{5,3},{6,0},{7,1},{8,14},{9,15},{10,... | collective-permute-start | bytes 589832 | tf_op jit(solution)/shard_map/ppermute | solution.py:560
  57.8 15.8 %collective-permute-start.24 = (f32[512,128]{1,0:T(8,128)S(1)}, f32[512,128]{1,0:T(8,128)S(1)}, u32[]{:S(2)}, u32[]{:S(2)}) collective-permute-start(f32[512,128]{1,0:T(8,128)S(1)} %shard_map.164), channel_id=1, source_target_pairs={{0,8},{8,0},{16,24},{24,16},{1,9},{9,1},{17,25},{25,17},{2,10},{10... | collective-permute-start | bytes 786440 | tf_op jit(solution)/shard_map/ppermute | solution.py:560
  59.5 14.3 %collective-permute-start.25 = (f32[512,128]{1,0:T(8,128)S(1)}, f32[512,128]{1,0:T(8,128)S(1)}, u32[]{:S(2)}, u32[]{:S(2)}) collective-permute-start(f32[512,128]{1,0:T(8,128)S(1)} %shard_map.164), channel_id=1, source_target_pairs={{0,16},{8,24},{16,0},{24,8},{1,17},{9,25},{17,1},{25,9},{2,18},{10... | collective-permute-start | bytes 786440 | tf_op jit(solution)/shard_map/ppermute | solution.py:560
  63.0 11.2 %collective-permute-start.26 = (f32[512,128]{1,0:T(8,128)S(1)}, f32[512,128]{1,0:T(8,128)S(1)}, u32[]{:S(2)}, u32[]{:S(2)}) collective-permute-start(f32[512,128]{1,0:T(8,128)S(1)} %shard_map.164), channel_id=1, source_target_pairs={{0,24},{8,16},{16,8},{24,0},{1,25},{9,17},{17,9},{25,1},{2,26},{10... | collective-permute-start | bytes 786440 | tf_op jit(solution)/shard_map/ppermute | solution.py:560
  73.1 1.5 %collective-permute-start.18 = (f32[384,128]{1,0:T(8,128)S(1)}, f32[384,128]{1,0:T(8,128)S(1)}, u32[]{:S(2)}, u32[]{:S(2)}) collective-permute-start(f32[384,128]{1,0:T(8,128)S(1)} %get-tuple-element.58.refs_1_), channel_id=1, source_target_pairs={{0,1},{1,0},{2,3},{3,2},{4,5},{5,4},{6,7},{7,6},{8,9},{9,8},{10,11... | collective-permute-start | bytes 589832 | tf_op jit(solution)/shard_map/ppermute | solution.py:560
  73.2 1.7 %collective-permute-start.19 = (f32[384,128]{1,0:T(8,128)S(1)}, f32[384,128]{1,0:T(8,128)S(1)}, u32[]{:S(2)}, u32[]{:S(2)}) collective-permute-start(f32[384,128]{1,0:T(8,128)S(1)} %collective-permute-done.17.refs_4_), channel_id=1, source_target_pairs={{0,1},{1,0},{2,3},{3,2},{4,5},{5,4},{6,7},{7,6},{8,9},{9,8},{10,11... | collective-permute-start | bytes 589832 | tf_op jit(solution)/shard_map/ppermute | solution.py:560
  73.6 1.5 %collective-permute-start.21 = (f32[384,128]{1,0:T(8,128)S(1)}, f32[384,128]{1,0:T(8,128)S(1)}, u32[]{:S(2)}, u32[]{:S(2)}) collective-permute-start(f32[384,128]{1,0:T(8,128)S(1)} %collective-permute-done.20.refs_6_), channel_id=1, source_target_pairs={{0,1},{1,0},{2,3},{3,2},{4,5},{5,4},{6,7},{7,6},{8,9},{9,8},{10,11... | collective-permute-start | bytes 589832 | tf_op jit(solution)/shard_map/ppermute | solution.py:560
  73.7 1.7 %collective-permute-start.23 = (f32[384,128]{1,0:T(8,128)S(1)}, f32[384,128]{1,0:T(8,128)S(1)}, u32[]{:S(2)}, u32[]{:S(2)}) collective-permute-start(f32[384,128]{1,0:T(8,128)S(1)} %collective-permute-done.22.refs_8_), channel_id=1, source_target_pairs={{0,1},{1,0},{2,3},{3,2},{4,5},{5,4},{6,7},{7,6},{8,9},{9,8},{10,11... | collective-permute-start | bytes 589832 | tf_op jit(solution)/shard_map/ppermute | solution.py:560
  74.2 8.7 %collective-permute-start.27 = (f32[512,128]{1,0:T(8,128)S(1)}, f32[512,128]{1,0:T(8,128)S(1)}, u32[]{:S(2)}, u32[]{:S(2)}) collective-permute-start(f32[512,128]{1,0:T(8,128)S(1)} %add_add_fusion.refs_3_), channel_id=1, source_target_pairs={{0,1},{1,0},{2,3},{3,2},{4,5},{5,4},{6,7},{7,6},{8,9},{9,8},{10,11... | collective-permute-start | bytes 786440 | tf_op jit(solution)/shard_map/ppermute | solution.py:560
